TPU v7x, 512 devices: a whole 4x8x8 slice. The times are simulated.
512 devices in a mesh: gx: 8 (over x, core), gy: 4 (over z_hi), gz: 16 (over y, z_lo).
Axes of the slice: x: 4, y: 8, z: 8 (z_hi: 4, z_lo: 2; z = z_hi * 2 + z_lo), core: 2. Of those that a mesh axis runs over, the one named last changes fastest.
Arguments:
- state: float32 [19, 64, 32, 1024], P(None, 'gz', 'gy', 'gx'), may hold values from 0 to 0.5, as said below
- adjoint_seed: float32 [19, 64, 32, 1024], P(None, 'gz', 'gy', 'gx'), may hold values from -6 to 6
- eddy_rate: float32 [64, 32, 1024], P('gz', 'gy', 'gx'), may hold values from 0.005 to 3
- smag_coeff: float32 [], replicated, may hold values from 0.1 to 0.3
- heights: int32 [32, 1024], replicated, may hold values from 0 to 32, as said below
Outputs:
- adjoint_state: float32 [19, 64, 32, 1024], P(None, 'gz', 'gy', 'gx')
- viscosity_gradient: float32 [64, 32, 1024], P('gz', 'gy', 'gx')
- totals: float32 [2], replicated
Inputs may be any that keep to these rules, and one draw needn't show every extreme that they name: `state`: all populations are positive; each cell's density is near one and its mean velocity is mostly streamwise. `heights`: heights are constant over aligned 4 x 4 footprints of columns.
All inputs are finite; a program needn't handle non-finite values.
Results may differ from a plain program's by a relative error of at most 0.000068.
Values sent between devices are 32-bit elements; how exact they have to be, the bound alone decides.
No kernel may reach another device: no remote copies, remote signals or barrier semaphores. Data moves between devices by JAX's collectives and lax.ppermute only.
A program may use at most 64 MiB of HBM per device.

v0:
```python
import math

import jax
import jax.numpy as jnp
import numpy as np
from jax import lax
from jax.sharding import PartitionSpec as P

VEL = np.array(
    [
        [0, 0, 0],
        [1, 0, 0],
        [-1, 0, 0],
        [0, 1, 0],
        [0, -1, 0],
        [0, 0, 1],
        [0, 0, -1],
        [1, 1, 0],
        [-1, -1, 0],
        [1, -1, 0],
        [-1, 1, 0],
        [1, 0, 1],
        [-1, 0, -1],
        [1, 0, -1],
        [-1, 0, 1],
        [0, 1, 1],
        [0, -1, -1],
        [0, 1, -1],
        [0, -1, 1],
    ]
)
OPPOSITE = [0, 2, 1, 4, 3, 6, 5, 8, 7, 10, 9, 12, 11, 14, 13, 16, 15, 18, 17]
LATTICE_WEIGHTS = [1.0 / 3.0] + [1.0 / 18.0] * 6 + [1.0 / 36.0] * 12
UREF = 0.08
NU_BASE = 0.004


def extended_2(block, sides, width):
    for axis, dim in sides:
        count = lax.axis_size(axis)
        forward = [(i, i + 1) for i in range(count - 1)]
        backward = [(target, source) for source, target in forward]
        low = lax.ppermute(
            lax.slice_in_dim(block, block.shape[dim] - width, None, axis=dim), axis, forward
        )
        high = lax.ppermute(lax.slice_in_dim(block, 0, width, axis=dim), axis, backward)
        block = jnp.concatenate([low, block, high], axis=dim)
    return block


def column(values):
    return jnp.array(values, jnp.float32).reshape(19, 1, 1, 1)


def collide(populations, omega):
    comp_x = column([float(v) for v in VEL[:, 0]])
    comp_y = column([float(v) for v in VEL[:, 1]])
    comp_z = column([float(v) for v in VEL[:, 2]])
    weights = column(LATTICE_WEIGHTS)
    density = jnp.sum(populations, 0)
    vel_x = jnp.sum(comp_x * populations, 0) / density
    vel_y = jnp.sum(comp_y * populations, 0) / density
    vel_z = jnp.sum(comp_z * populations, 0) / density
    usq = vel_x * vel_x + vel_y * vel_y + vel_z * vel_z
    along = comp_x * vel_x + comp_y * vel_y + comp_z * vel_z
    equil = weights * density * (1.0 + 3.0 * along + 4.5 * along * along - 1.5 * usq)
    return populations - omega * (populations - equil)


def window(grid, index, offset):
    depth, rows, cols = (grid.shape[-3] - 2, grid.shape[-2] - 2, grid.shape[-1] - 2)
    off_x, off_y, off_z = offset
    if index is None:
        return grid[
            1 + off_z : 1 + off_z + depth,
            1 + off_y : 1 + off_y + rows,
            1 + off_x : 1 + off_x + cols,
        ]
    return grid[
        index,
        1 + off_z : 1 + off_z + depth,
        1 + off_y : 1 + off_y + rows,
        1 + off_x : 1 + off_x + cols,
    ]


def pull(field, extended, solid_ext):
    pieces = []
    for idx in range(19):
        offset = (-int(VEL[idx, 0]), -int(VEL[idx, 1]), -int(VEL[idx, 2]))
        source = window(extended, idx, offset)
        blocked = window(solid_ext, None, offset)
        pieces.append((1.0 - blocked) * source + blocked * field[OPPOSITE[idx]])
    return jnp.stack(pieces, 0)


def push(field, extended, solid_ext):
    own = window(solid_ext, None, (0, 0, 0))
    pieces = []
    for idx in range(19):
        offset = (int(VEL[idx, 0]), int(VEL[idx, 1]), int(VEL[idx, 2]))
        target = window(extended, idx, offset)
        blocked = window(solid_ext, None, offset)
        pieces.append((1.0 - own) * target + blocked * field[OPPOSITE[idx]])
    return jnp.stack(pieces, 0)


def drag_links(solid_ext):
    own = window(solid_ext, None, (0, 0, 0))
    pieces = []
    for idx in range(19):
        offset = (int(VEL[idx, 0]), int(VEL[idx, 1]), int(VEL[idx, 2]))
        pieces.append(2.0 * float(VEL[idx, 0]) * (1.0 - own) * window(solid_ext, None, offset))
    return jnp.stack(pieces, 0)


def solid_box(heights, margin, depth, rows, cols, total_z):
    padded = jnp.pad(heights, 3, constant_values=total_z + 2)
    flags = jnp.pad(jnp.ones_like(heights), 3)
    start_y = lax.axis_index("gy") * rows + 3 - margin
    start_x = lax.axis_index("gx") * cols + 3 - margin
    columns = lax.dynamic_slice(padded, (start_y, start_x), (rows + 2 * margin, cols + 2 * margin))
    inner = lax.dynamic_slice(flags, (start_y, start_x), (rows + 2 * margin, cols + 2 * margin))
    levels = (
        lax.axis_index("gz") * depth - margin + lax.iota(jnp.int32, depth + 2 * margin)
    ).reshape(depth + 2 * margin, 1, 1)
    solid = ((levels < columns[None]) | (levels >= total_z)).astype(jnp.float32)
    inside = ((inner[None] > 0) & (levels >= 0) & (levels < total_z)).astype(jnp.float32)
    return (solid, inside)


def rims(field):
    return extended_2(field, (("gx", 3), ("gy", 2), ("gz", 1)), 1)


def on_device(state, adjoint_seed, eddy_rate, smag_coeff, heights):
    depth, rows, cols = eddy_rate.shape
    total_x = cols * lax.axis_size("gx")
    total_y = rows * lax.axis_size("gy")
    total_z = depth * lax.axis_size("gz")
    scale = 1.0 / (2.0 * UREF * total_x * total_y)
    omega = 1.0 / (0.5 + 3.0 * (NU_BASE + smag_coeff * eddy_rate))
    solid_ext = solid_box(heights, 1, depth, rows, cols, total_z)[0]
    links = drag_links(solid_ext)
    post_zero, back_zero = jax.vjp(collide, state, omega)
    f_one = pull(post_zero, rims(post_zero), solid_ext)
    post_one, back_one = jax.vjp(collide, f_one, omega)
    drag_local = scale * jnp.sum(links * (post_zero + post_one))
    seed_links = push(adjoint_seed, rims(adjoint_seed), solid_ext) + scale * links
    adjoint_one, omega_one = back_one(seed_links)
    carried = push(adjoint_one, rims(adjoint_one), solid_ext) + scale * links
    adjoint_state, omega_zero = back_zero(carried)
    omega_sum = omega_zero + omega_one
    viscosity_gradient = -3.0 * omega * omega * omega_sum
    sens_local = jnp.sum(viscosity_gradient * eddy_rate) / math.sqrt(total_x * total_y * total_z)
    drag = lax.psum(drag_local, ("gx", "gy", "gz"))
    sensitivity = lax.psum(sens_local, ("gx", "gy", "gz"))
    totals = jnp.stack([drag, sensitivity])
    return (adjoint_state, viscosity_gradient, totals)


def solution(mesh):
    return jax.shard_map(
        on_device,
        mesh=mesh,
        in_specs=(
            P(None, "gz", "gy", "gx"),
            P(None, "gz", "gy", "gx"),
            P("gz", "gy", "gx"),
            P(),
            P(),
        ),
        out_specs=(P(None, "gz", "gy", "gx"), P("gz", "gy", "gx"), P()),
        check_vma=False,
    )
```

profile of v0, /device:TPU:1, one launch (start us, length us, event | category | flops | bytes accessed | tf_op | source)
XLA Modules:
  0.0 217.5 jit_solution(17481721383254483485)
XLA Ops:
  0.6 1.3 fusion.243
  1.9 8.8 %collective-permute-start = (f32[19,4,8,1]{3,2,1,0:T(8,128)S(1)}, f32[19,4,8,1]{3,2,1,0:T(8,128)S(1)}, u32[]{:S(2)}, u32[]{:S(2)}) collective-permute-start(f32[19,4,8,1]{3,2,1,0:T(8,128)S(1)} %get-tuple-element.95), channel_id=1, source_target_pairs={{64,0},{128,64},{192,128},{256,192},{320,256},{384,320},{448,384},... | collective-permute-start | bytes 7304 | tf_op jit(solution)/shard_map/ppermute | solution.py:46
  10.7 1.9 collective-permute-start.1
  13.4 0.6 copy-done.4
  14.0 0.1 multiply_reduce_fusion.16
  14.1 0.6 copy-done.7
  14.8 0.3 multiply_subtract_fusion
  15.1 0.9 fusion.244
  15.9 1.9 collective-permute-start.6
  17.9 2.4 %collective-permute-start.7 = (f32[19,4,8,1]{3,2,1,0:T(8,128)S(1)}, f32[19,4,8,1]{3,2,1,0:T(8,128)S(1)}, u32[]{:S(2)}, u32[]{:S(2)}) collective-permute-start(f32[19,4,8,1]{3,2,1,0:T(8,128)S(1)} %get-tuple-element.96), channel_id=1, source_target_pairs={{64,0},{128,64},{192,128},{256,192},{320,256},{384,320},{448,384},... | collective-permute-start | bytes 7304 | tf_op jit(solution)/shard_map/ppermute | solution.py:46
  20.3 0.1 pad_dynamic-slice_fusion
  22.1 0.5 pad_maximum_fusion.21
  22.6 1.3 collective-permute-start.2
  23.9 4.9 %collective-permute-start.3 = (f32[19,4,1,130]{3,2,1,0:T(1,128)S(1)}, f32[19,4,1,130]{3,2,1,0:T(1,128)S(1)}, u32[]{:S(2)}, u32[]{:S(2)}) collective-permute-start(f32[19,4,1,130]{3,2,1,0:T(1,128)S(1)} %get-tuple-element.88), channel_id=1, source_target_pairs={{0,16},{16,32},{32,48},{1,17},{17,33},{33,49},{2,18},{18,34},{34,5... | collective-permute-start | bytes 118568 | tf_op jit(solution)/shard_map/ppermute | solution.py:43
  28.9 0.5 pad_maximum_fusion.18
  29.4 4.3 %collective-permute-start.8 = (f32[19,4,1,130]{3,2,1,0:T(1,128)S(1)}, f32[19,4,1,130]{3,2,1,0:T(1,128)S(1)}, u32[]{:S(2)}, u32[]{:S(2)}) collective-permute-start(f32[19,4,1,130]{3,2,1,0:T(1,128)S(1)} %get-tuple-element.91), channel_id=1, source_target_pairs={{0,16},{16,32},{32,48},{1,17},{17,33},{33,49},{2,18},{18,34},{34,5... | collective-permute-start | bytes 118568 | tf_op jit(solution)/shard_map/ppermute | solution.py:43
  33.7 1.3 collective-permute-start.9
  35.2 0.3 pad_maximum_fusion.10
  35.5 1.3 collective-permute-start.4
  36.8 4.0 %collective-permute-start.5 = (f32[19,1,10,130]{3,2,1,0:T(8,128)S(1)}, f32[19,1,10,130]{3,2,1,0:T(8,128)S(1)}, u32[]{:S(2)}, u32[]{:S(2)}) collective-permute-start(f32[19,1,10,130]{3,2,1,0:T(8,128)S(1)} %get-tuple-element.82), channel_id=1, source_target_pairs={{0,1},{1,2},{2,3},{3,4},{4,5},{5,6},{6,7},{7,8},{8,9},{9,10},{10,1... | collective-permute-start | bytes 296408 | tf_op jit(solution)/shard_map/ppermute | solution.py:43
  40.8 1.4 collective-permute-done.9
  42.2 0.3 pad_maximum_fusion.5
  42.5 2.6 %collective-permute-start.10 = (f32[19,1,10,130]{3,2,1,0:T(8,128)S(1)}, f32[19,1,10,130]{3,2,1,0:T(8,128)S(1)}, u32[]{:S(2)}, u32[]{:S(2)}) collective-permute-start(f32[19,1,10,130]{3,2,1,0:T(8,128)S(1)} %get-tuple-element.85), channel_id=1, source_target_pairs={{0,1},{1,2},{2,3},{3,4},{4,5},{5,6},{6,7},{7,8},{8,9},{9,10},{10,1... | collective-permute-start | bytes 296408 | tf_op jit(solution)/shard_map/ppermute | solution.py:43
  45.2 1.3 collective-permute-start.11
  46.5 0.1 constant_dynamic-update-slice_fusion.15
  46.7 0.6 collective-permute-done.4
  47.3 12.6 %collective-permute-done.5 = f32[19,1,10,130]{3,2,1,0:T(8,128)S(1)} collective-permute-done((f32[19,1,10,130]{3,2,1,0:T(8,128)S(1)}, f32[19,1,10,130]{3,2,1,0:T(8,128)S(1)}, u32[]{:S(2)}, u32[]{:S(2)}) %collective-permute-start.5) | collective-permute-done | bytes 98832 | tf_op jit(solution)/shard_map/ppermute | solution.py:43
  60.1 0.1 constant_dynamic-update-slice_fusion.11
  60.2 0.1 constant_dynamic-update-slice_fusion.9
  60.6 0.1 constant_dynamic-update-slice_fusion.5
  60.8 0.1 constant_dynamic-update-slice_fusion.3
  61.0 0.1 constant_dynamic-update-slice_fusion.55
  61.1 0.1 constant_dynamic-update-slice_fusion.54
  61.4 5.3 %collective-permute-done.10 = f32[19,1,10,130]{3,2,1,0:T(8,128)S(1)} collective-permute-done((f32[19,1,10,130]{3,2,1,0:T(8,128)S(1)}, f32[19,1,10,130]{3,2,1,0:T(8,128)S(1)}, u32[]{:S(2)}, u32[]{:S(2)}) %collective-permute-start.10) | collective-permute-done | bytes 98832 | tf_op jit(solution)/shard_map/ppermute | solution.py:43
  67.8 0.1 constant_dynamic-update-slice_fusion.38
  67.9 0.1 multiply_reduce_fusion.11
  68.0 0.1 add_multiply_fusion
  68.2 0.3 fusion.6
  68.4 1.3 multiply_reduce_fusion.8
  69.7 0.1 add_add_fusion.1
  69.9 0.2 fusion.242
  70.0 2.4 %collective-permute-start.12 = (f32[19,4,8,1]{3,2,1,0:T(8,128)S(1)}, f32[19,4,8,1]{3,2,1,0:T(8,128)S(1)}, u32[]{:S(2)}, u32[]{:S(2)}) collective-permute-start(f32[19,4,8,1]{3,2,1,0:T(8,128)S(1)} %get-tuple-element.93), channel_id=1, source_target_pairs={{64,0},{128,64},{192,128},{256,192},{320,256},{384,320},{448,384},... | collective-permute-start | bytes 7304 | tf_op jit(solution)/shard_map/ppermute | solution.py:46
  72.4 3.2 %collective-permute-start.13 = (f32[19,4,8,1]{3,2,1,0:T(8,128)S(1)}, f32[19,4,8,1]{3,2,1,0:T(8,128)S(1)}, u32[]{:S(2)}, u32[]{:S(2)}) collective-permute-start(f32[19,4,8,1]{3,2,1,0:T(8,128)S(1)} %get-tuple-element.92), channel_id=1, source_target_pairs={{0,64},{64,128},{128,192},{192,256},{256,320},{320,384},{384,448},... | collective-permute-start | bytes 7304 | tf_op jit(solution)/shard_map/ppermute | solution.py:43
  76.3 1.9 collective-permute-done.12
  78.2 1.2 collective-permute-done.13
  79.4 0.5 pad_maximum_fusion.15
  80.0 1.3 collective-permute-start.14
  81.3 5.5 %collective-permute-start.15 = (f32[19,4,1,130]{3,2,1,0:T(1,128)S(1)}, f32[19,4,1,130]{3,2,1,0:T(1,128)S(1)}, u32[]{:S(2)}, u32[]{:S(2)}) collective-permute-start(f32[19,4,1,130]{3,2,1,0:T(1,128)S(1)} %get-tuple-element.86), channel_id=1, source_target_pairs={{0,16},{16,32},{32,48},{1,17},{17,33},{33,49},{2,18},{18,34},{34,5... | collective-permute-start | bytes 118568 | tf_op jit(solution)/shard_map/ppermute | solution.py:43
  86.9 1.2 collective-permute-done.15
  88.2 0.3 pad_maximum_fusion
  88.5 1.3 collective-permute-start.16
  89.8 4.8 %collective-permute-start.17 = (f32[19,1,10,130]{3,2,1,0:T(8,128)S(1)}, f32[19,1,10,130]{3,2,1,0:T(8,128)S(1)}, u32[]{:S(2)}, u32[]{:S(2)}) collective-permute-start(f32[19,1,10,130]{3,2,1,0:T(8,128)S(1)} %get-tuple-element.80), channel_id=1, source_target_pairs={{0,1},{1,2},{2,3},{3,4},{4,5},{5,6},{6,7},{7,8},{8,9},{9,10},{10,1... | collective-permute-start | bytes 296408 | tf_op jit(solution)/shard_map/ppermute | solution.py:43
  94.8 3.1 %collective-permute-done.16 = f32[19,1,10,130]{3,2,1,0:T(8,128)S(1)} collective-permute-done((f32[19,1,10,130]{3,2,1,0:T(8,128)S(1)}, f32[19,1,10,130]{3,2,1,0:T(8,128)S(1)}, u32[]{:S(2)}, u32[]{:S(2)}) %collective-permute-start.16) | collective-permute-done | bytes 98832 | tf_op jit(solution)/shard_map/ppermute | solution.py:46
  98.0 7.4 %collective-permute-done.17 = f32[19,1,10,130]{3,2,1,0:T(8,128)S(1)} collective-permute-done((f32[19,1,10,130]{3,2,1,0:T(8,128)S(1)}, f32[19,1,10,130]{3,2,1,0:T(8,128)S(1)}, u32[]{:S(2)}, u32[]{:S(2)}) %collective-permute-start.17) | collective-permute-done | bytes 98832 | tf_op jit(solution)/shard_map/ppermute | solution.py:43
  105.5 0.1 constant_dynamic-update-slice_fusion.68
  105.7 0.1 constant_dynamic-update-slice_fusion.66
  106.2 0.1 constant_dynamic-update-slice_fusion.60
  106.4 0.1 constant_dynamic-update-slice_fusion.58
  106.6 0.2 fusion.4
  106.9 0.4 multiply_reduce_fusion.4
  107.3 1.2 multiply_reduce_fusion.17
  109.2 105.7 %all-reduce.1 = (f32[1]{0:T(128)}, f32[1]{0:T(128)}) all-reduce(f32[1]{0:T(128)} %bitcast.188, f32[1]{0:T(128)} %bitcast.187), channel_id=1, replica_groups=mesh['gx'=8,'gy'=4,'gz'=16] {'gx','gy','gz'}, use_global_device_ids=true, to_apply=%region_22.23 | all-reduce | flops 2 | bytes 16 | tf_op jit(solution)/shard_map/psum | solution.py:157
  214.8 1.8 pad_maximum_fusion.78
  216.6 0.9 add_add_fusion
  (90 shorter events, 5.3 us)
Async XLA Ops:
  0.6 12.7 %copy-start.1 = (f32[19,4,8,128]{3,2,1,0:T(8,128)S(1)}, f32[19,4,8,128]{3,2,1,0:T(8,128)}, u32[]{:S(2)}) copy-start(f32[19,4,8,128]{3,2,1,0:T(8,128)} %param.13) | copy-start | bytes 933892
  0.6 12.6 %copy-start.3 = (f32[4,8,128]{2,1,0:T(8,128)S(1)}, f32[4,8,128]{2,1,0:T(8,128)}, u32[]{:S(2)}) copy-start(f32[4,8,128]{2,1,0:T(8,128)} %param.15) | copy-start | bytes 49156
  1.9 20.2 %collective-permute-start = (f32[19,4,8,1]{3,2,1,0:T(8,128)S(1)}, f32[19,4,8,1]{3,2,1,0:T(8,128)S(1)}, u32[]{:S(2)}, u32[]{:S(2)}) collective-permute-start(f32[19,4,8,1]{3,2,1,0:T(8,128)S(1)} %get-tuple-element.95), channel_id=1, source_target_pairs={{64,0},{128,64},{192,128},{256,192},{320,256},{384,320},{448,384},... | collective-permute-start | bytes 7304 | tf_op jit(solution)/shard_map/ppermute | solution.py:46
  10.7 11.4 %collective-permute-start.1 = (f32[19,4,8,1]{3,2,1,0:T(8,128)S(1)}, f32[19,4,8,1]{3,2,1,0:T(8,128)S(1)}, u32[]{:S(2)}, u32[]{:S(2)}) collective-permute-start(f32[19,4,8,1]{3,2,1,0:T(8,128)S(1)} %get-tuple-element.94), channel_id=1, source_target_pairs={{0,64},{64,128},{128,192},{192,256},{256,320},{320,384},{384,448},... | collective-permute-start | bytes 7304 | tf_op jit(solution)/shard_map/ppermute | solution.py:43
  13.3 0.7 copy-start.4
  13.3 0.7 copy-start.5
  13.3 0.7 copy-start.6
  14.1 0.7 copy-start.7
  15.1 5.3 %copy-start.2 = (s32[32,1024]{1,0:T(8,128)S(1)}, s32[32,1024]{1,0:T(8,128)}, u32[]{:S(2)}) copy-start(s32[32,1024]{1,0:T(8,128)} %param.17) | copy-start | bytes 393220
  15.9 12.9 %collective-permute-start.6 = (f32[19,4,8,1]{3,2,1,0:T(8,128)}, f32[19,4,8,1]{3,2,1,0:T(8,128)S(1)}, u32[]{:S(2)}, u32[]{:S(2)}) collective-permute-start(f32[19,4,8,1]{3,2,1,0:T(8,128)} %get-tuple-element.97), channel_id=1, source_target_pairs={{0,64},{64,128},{128,192},{192,256},{256,320},{320,384},{384,448},... | collective-permute-start | bytes 7304 | tf_op jit(solution)/shard_map/ppermute | solution.py:43
  17.9 11.0 %collective-permute-start.7 = (f32[19,4,8,1]{3,2,1,0:T(8,128)S(1)}, f32[19,4,8,1]{3,2,1,0:T(8,128)S(1)}, u32[]{:S(2)}, u32[]{:S(2)}) collective-permute-start(f32[19,4,8,1]{3,2,1,0:T(8,128)S(1)} %get-tuple-element.96), channel_id=1, source_target_pairs={{64,0},{128,64},{192,128},{256,192},{320,256},{384,320},{448,384},... | collective-permute-start | bytes 7304 | tf_op jit(solution)/shard_map/ppermute | solution.py:46
  20.9 1.0 copy-start
  22.6 12.5 %collective-permute-start.2 = (f32[19,4,1,130]{3,2,1,0:T(1,128)S(1)}, f32[19,4,1,130]{3,2,1,0:T(1,128)S(1)}, u32[]{:S(2)}, u32[]{:S(2)}) collective-permute-start(f32[19,4,1,130]{3,2,1,0:T(1,128)S(1)} %get-tuple-element.89), channel_id=1, source_target_pairs={{16,0},{32,16},{48,32},{17,1},{33,17},{49,33},{18,2},{34,18},{50,3... | collective-permute-start | bytes 118568 | tf_op jit(solution)/shard_map/ppermute | solution.py:46
  23.9 11.3 %collective-permute-start.3 = (f32[19,4,1,130]{3,2,1,0:T(1,128)S(1)}, f32[19,4,1,130]{3,2,1,0:T(1,128)S(1)}, u32[]{:S(2)}, u32[]{:S(2)}) collective-permute-start(f32[19,4,1,130]{3,2,1,0:T(1,128)S(1)} %get-tuple-element.88), channel_id=1, source_target_pairs={{0,16},{16,32},{32,48},{1,17},{17,33},{33,49},{2,18},{18,34},{34,5... | collective-permute-start | bytes 118568 | tf_op jit(solution)/shard_map/ppermute | solution.py:43
  29.4 11.4 %collective-permute-start.8 = (f32[19,4,1,130]{3,2,1,0:T(1,128)S(1)}, f32[19,4,1,130]{3,2,1,0:T(1,128)S(1)}, u32[]{:S(2)}, u32[]{:S(2)}) collective-permute-start(f32[19,4,1,130]{3,2,1,0:T(1,128)S(1)} %get-tuple-element.91), channel_id=1, source_target_pairs={{0,16},{16,32},{32,48},{1,17},{17,33},{33,49},{2,18},{18,34},{34,5... | collective-permute-start | bytes 118568 | tf_op jit(solution)/shard_map/ppermute | solution.py:43
  33.7 8.5 %collective-permute-start.9 = (f32[19,4,1,130]{3,2,1,0:T(1,128)S(1)}, f32[19,4,1,130]{3,2,1,0:T(1,128)S(1)}, u32[]{:S(2)}, u32[]{:S(2)}) collective-permute-start(f32[19,4,1,130]{3,2,1,0:T(1,128)S(1)} %get-tuple-element.90), channel_id=1, source_target_pairs={{16,0},{32,16},{48,32},{17,1},{33,17},{49,33},{18,2},{34,18},{50,3... | collective-permute-start | bytes 118568 | tf_op jit(solution)/shard_map/ppermute | solution.py:46
  35.5 11.7 %collective-permute-start.4 = (f32[19,1,10,130]{3,2,1,0:T(8,128)S(1)}, f32[19,1,10,130]{3,2,1,0:T(8,128)S(1)}, u32[]{:S(2)}, u32[]{:S(2)}) collective-permute-start(f32[19,1,10,130]{3,2,1,0:T(8,128)S(1)} %get-tuple-element.83), channel_id=1, source_target_pairs={{1,0},{2,1},{3,2},{4,3},{5,4},{6,5},{7,6},{8,7},{9,8},{10,9},{11,1... | collective-permute-start | bytes 296408 | tf_op jit(solution)/shard_map/ppermute | solution.py:46
  36.8 23.1 %collective-permute-start.5 = (f32[19,1,10,130]{3,2,1,0:T(8,128)S(1)}, f32[19,1,10,130]{3,2,1,0:T(8,128)S(1)}, u32[]{:S(2)}, u32[]{:S(2)}) collective-permute-start(f32[19,1,10,130]{3,2,1,0:T(8,128)S(1)} %get-tuple-element.82), channel_id=1, source_target_pairs={{0,1},{1,2},{2,3},{3,4},{4,5},{5,6},{6,7},{7,8},{8,9},{9,10},{10,1... | collective-permute-start | bytes 296408 | tf_op jit(solution)/shard_map/ppermute | solution.py:43
  42.5 24.1 %collective-permute-start.10 = (f32[19,1,10,130]{3,2,1,0:T(8,128)S(1)}, f32[19,1,10,130]{3,2,1,0:T(8,128)S(1)}, u32[]{:S(2)}, u32[]{:S(2)}) collective-permute-start(f32[19,1,10,130]{3,2,1,0:T(8,128)S(1)} %get-tuple-element.85), channel_id=1, source_target_pairs={{0,1},{1,2},{2,3},{3,4},{4,5},{5,6},{6,7},{7,8},{8,9},{9,10},{10,1... | collective-permute-start | bytes 296408 | tf_op jit(solution)/shard_map/ppermute | solution.py:43
  45.2 21.5 %collective-permute-start.11 = (f32[19,1,10,130]{3,2,1,0:T(8,128)S(1)}, f32[19,1,10,130]{3,2,1,0:T(8,128)S(1)}, u32[]{:S(2)}, u32[]{:S(2)}) collective-permute-start(f32[19,1,10,130]{3,2,1,0:T(8,128)S(1)} %get-tuple-element.84), channel_id=1, source_target_pairs={{1,0},{2,1},{3,2},{4,3},{5,4},{6,5},{7,6},{8,7},{9,8},{10,9},{11,1... | collective-permute-start | bytes 296408 | tf_op jit(solution)/shard_map/ppermute | solution.py:46
  70.0 8.2 %collective-permute-start.12 = (f32[19,4,8,1]{3,2,1,0:T(8,128)S(1)}, f32[19,4,8,1]{3,2,1,0:T(8,128)S(1)}, u32[]{:S(2)}, u32[]{:S(2)}) collective-permute-start(f32[19,4,8,1]{3,2,1,0:T(8,128)S(1)} %get-tuple-element.93), channel_id=1, source_target_pairs={{64,0},{128,64},{192,128},{256,192},{320,256},{384,320},{448,384},... | collective-permute-start | bytes 7304 | tf_op jit(solution)/shard_map/ppermute | solution.py:46
  72.4 7.0 %collective-permute-start.13 = (f32[19,4,8,1]{3,2,1,0:T(8,128)S(1)}, f32[19,4,8,1]{3,2,1,0:T(8,128)S(1)}, u32[]{:S(2)}, u32[]{:S(2)}) collective-permute-start(f32[19,4,8,1]{3,2,1,0:T(8,128)S(1)} %get-tuple-element.92), channel_id=1, source_target_pairs={{0,64},{64,128},{128,192},{192,256},{256,320},{320,384},{384,448},... | collective-permute-start | bytes 7304 | tf_op jit(solution)/shard_map/ppermute | solution.py:43
  80.0 7.0 %collective-permute-start.14 = (f32[19,4,1,130]{3,2,1,0:T(1,128)S(1)}, f32[19,4,1,130]{3,2,1,0:T(1,128)S(1)}, u32[]{:S(2)}, u32[]{:S(2)}) collective-permute-start(f32[19,4,1,130]{3,2,1,0:T(1,128)S(1)} %get-tuple-element.87), channel_id=1, source_target_pairs={{16,0},{32,16},{48,32},{17,1},{33,17},{49,33},{18,2},{34,18},{50,3... | collective-permute-start | bytes 118568 | tf_op jit(solution)/shard_map/ppermute | solution.py:46
  81.3 6.9 %collective-permute-start.15 = (f32[19,4,1,130]{3,2,1,0:T(1,128)S(1)}, f32[19,4,1,130]{3,2,1,0:T(1,128)S(1)}, u32[]{:S(2)}, u32[]{:S(2)}) collective-permute-start(f32[19,4,1,130]{3,2,1,0:T(1,128)S(1)} %get-tuple-element.86), channel_id=1, source_target_pairs={{0,16},{16,32},{32,48},{1,17},{17,33},{33,49},{2,18},{18,34},{34,5... | collective-permute-start | bytes 118568 | tf_op jit(solution)/shard_map/ppermute | solution.py:43
  88.5 9.4 %collective-permute-start.16 = (f32[19,1,10,130]{3,2,1,0:T(8,128)S(1)}, f32[19,1,10,130]{3,2,1,0:T(8,128)S(1)}, u32[]{:S(2)}, u32[]{:S(2)}) collective-permute-start(f32[19,1,10,130]{3,2,1,0:T(8,128)S(1)} %get-tuple-element.81), channel_id=1, source_target_pairs={{1,0},{2,1},{3,2},{4,3},{5,4},{6,5},{7,6},{8,7},{9,8},{10,9},{11,1... | collective-permute-start | bytes 296408 | tf_op jit(solution)/shard_map/ppermute | solution.py:46
  89.8 15.6 %collective-permute-start.17 = (f32[19,1,10,130]{3,2,1,0:T(8,128)S(1)}, f32[19,1,10,130]{3,2,1,0:T(8,128)S(1)}, u32[]{:S(2)}, u32[]{:S(2)}) collective-permute-start(f32[19,1,10,130]{3,2,1,0:T(8,128)S(1)} %get-tuple-element.80), channel_id=1, source_target_pairs={{0,1},{1,2},{2,3},{3,4},{4,5},{5,6},{6,7},{7,8},{8,9},{9,10},{10,1... | collective-permute-start | bytes 296408 | tf_op jit(solution)/shard_map/ppermute | solution.py:43
where the time goes:
time: 218 us; the launch traced here: 217 us
  blocking collectives  106 us (49%)
  starting transfers between devices  54.4 us (25%)
  waiting for transfers between devices  34.7 us (16%)
  other arithmetic  15.7 us (7%)
  local copies, waits for them, and re-layouts  3.7 us (2%)
  between operations  3.27 us (2%)
    psum x1, blocking collectives, on_device(): sensitivity = lax.psum(sens_local, ('gx', 'gy', 'gz'))  106 us
    ppermute x9, starting transfers between devices, extended_2(): lax.ppermute(lax.slice_in_dim(block, block.shape[dim] - width, None, axis...  33.1 us
    ppermute x9, waiting for transfers between devices, extended_2(): lax.ppermute(lax.slice_in_dim(block, block.shape[dim] - width, None, axis...  27.7 us
    ppermute x9, starting transfers between devices, extended_2(): lax.ppermute(lax.slice_in_dim(block, 0, width, axis=dim), axis, backward)  21.3 us
    ppermute x9, waiting for transfers between devices, extended_2(): lax.ppermute(lax.slice_in_dim(block, 0, width, axis=dim), axis, backward)  7.02 us
    unnamed x69, other arithmetic  5.83 us
  transfers between devices with their start and end apart: 18, of which 9 were waited for; matrix products, arithmetic and copies ran while one was open for 3% of the time, Pallas kernels for 0%

commit v1 on v0

v1 whole, which is shorter than its diff:
```python
import math

import jax
import jax.numpy as jnp
import numpy as np
from jax import lax
from jax.sharding import PartitionSpec as P

VEL = [
    (0, 0, 0),
    (1, 0, 0),
    (-1, 0, 0),
    (0, 1, 0),
    (0, -1, 0),
    (0, 0, 1),
    (0, 0, -1),
    (1, 1, 0),
    (-1, -1, 0),
    (1, -1, 0),
    (-1, 1, 0),
    (1, 0, 1),
    (-1, 0, -1),
    (1, 0, -1),
    (-1, 0, 1),
    (0, 1, 1),
    (0, -1, -1),
    (0, 1, -1),
    (0, -1, 1),
]
OPPOSITE = [0, 2, 1, 4, 3, 6, 5, 8, 7, 10, 9, 12, 11, 14, 13, 16, 15, 18, 17]
LATTICE_WEIGHTS = [1.0 / 3.0] + [1.0 / 18.0] * 6 + [1.0 / 36.0] * 12
UREF = 0.08
NU_BASE = 0.004
Q = 19


def signed(terms):
    total = None
    for factor, value in terms:
        if factor == 0:
            continue
        piece = value if factor == 1 else (-value if factor == -1 else factor * value)
        total = piece if total is None else total + piece
    return total


def along(idx, vec):
    return signed([(VEL[idx][axis], vec[axis]) for axis in range(3)])


def flow(pops):
    rho = signed([(1, p) for p in pops])
    inverse = 1.0 / rho
    vel = [signed([(VEL[i][axis], pops[i]) for i in range(Q)]) * inverse for axis in range(3)]
    return rho, vel


def shapes(vel):
    base = 1.0 - 1.5 * (vel[0] * vel[0] + vel[1] * vel[1] + vel[2] * vel[2])
    out = [base] + [None] * (Q - 1)
    for i in range(1, Q, 2):
        cu = along(i, vel)
        even = base + 4.5 * cu * cu
        out[i] = even + 3.0 * cu
        out[i + 1] = even - 3.0 * cu
    return out


def departures(pops):
    rho, vel = flow(pops)
    shape = shapes(vel)
    return [LATTICE_WEIGHTS[i] * rho * shape[i] - pops[i] for i in range(Q)]


def collide_adjoint(pops, omega, cot):
    rho, vel = flow(pops)
    shape = shapes(vel)
    weighted = [LATTICE_WEIGHTS[i] * cot[i] for i in range(Q)]
    level = signed([(1, weighted[i] * shape[i]) for i in range(Q)])
    mass = signed([(1, w) for w in weighted])
    first = [signed([(VEL[i][axis], weighted[i]) for i in range(Q)]) for axis in range(3)]

    def second(a, b):
        return signed([(VEL[i][a] * VEL[i][b], weighted[i]) for i in range(Q)])

    slope = []
    for a in range(3):
        mixed = signed([(1, second(a, b) * vel[b]) for b in range(3)])
        slope.append(3.0 * first[a] + 9.0 * mixed - 3.0 * mass * vel[a])
    base = omega * (level - (slope[0] * vel[0] + slope[1] * vel[1] + slope[2] * vel[2]))
    tilt = [omega * s for s in slope]
    keep = 1.0 - omega
    adjoint = []
    for i in range(Q):
        part = along(i, tilt)
        adjoint.append(keep * cot[i] + (base if part is None else base + part))
    away = [LATTICE_WEIGHTS[i] * rho * shape[i] - pops[i] for i in range(Q)]
    grad = signed([(1, cot[i] * away[i]) for i in range(Q)])
    return adjoint, grad, away


def plus_one(axis):
    count = lax.axis_size(axis)
    return [(i, (i + 1) % count) for i in range(count)]


def minus_one(axis):
    return [(target, source) for source, target in plus_one(axis)]


def pair_pairs(first, second):
    count = lax.axis_size("gz")
    return [(a * count + b, c * count + d) for a, c in first for b, d in second]


def solid_around(heights, depth, rows, cols):
    total_z = depth * lax.axis_size("gz")
    total_y, total_x = heights.shape
    start_z = lax.axis_index("gz") * depth
    start_y = lax.axis_index("gy") * rows
    start_x = lax.axis_index("gx") * cols
    padded = jnp.pad(heights, ((1, 2), (1, 2)), mode="wrap")
    columns = lax.dynamic_slice(padded, (start_y, start_x), (rows + 3, cols + 3))
    z = start_z - 1 + lax.iota(jnp.int32, depth + 3)
    y = start_y - 1 + lax.iota(jnp.int32, rows + 3)
    x = start_x - 1 + lax.iota(jnp.int32, cols + 3)
    wrapped = jnp.where(z < 0, z + total_z, jnp.where(z >= total_z, z - total_z, z))
    solid = wrapped.reshape(-1, 1, 1) < columns[None]

    def border(coord, total):
        return (coord == -1) | (coord == total - 1)

    walls = (
        border(x, total_x).reshape(1, 1, -1),
        border(y, total_y).reshape(1, -1, 1),
        border(z, total_z).reshape(-1, 1, 1),
    )
    return solid, walls


def on_device(state, adjoint_seed, eddy_rate, smag_coeff, heights):
    depth, rows, cols = eddy_rate.shape
    total_x = cols * lax.axis_size("gx")
    total_y = rows * lax.axis_size("gy")
    total_z = depth * lax.axis_size("gz")
    scale = 1.0 / (2.0 * UREF * total_x * total_y)
    solid, walls = solid_around(heights, depth, rows, cols)
    sizes = (cols, rows, depth)

    def box(start, offset):
        return tuple(
            slice(start + offset[a] + 1, start + offset[a] + 1 + sizes[a]) for a in (2, 1, 0)
        )

    def crossing(start, offset):
        flags = None
        for a in range(3):
            if offset[a] == 0:
                continue
            low = start + 1 + (0 if offset[a] > 0 else -1)
            part = lax.slice_in_dim(walls[a], low, low + sizes[a], axis=2 - a)
            flags = part if flags is None else flags | part
        return flags

    def blocked(start, idx, sign):
        offset = tuple(sign * v for v in VEL[idx])
        wet = solid[box(start, offset)]
        return wet if idx == 0 else wet | crossing(start, offset)

    def extend_up(block):
        high = lax.ppermute(block[..., :2], "gx", minus_one("gx"))
        block = jnp.concatenate([block, high], axis=-1)
        y_msg, z_msg, yz_msg = block[:, :, :2], block[:, :2], block[:, :2, :2]
        z_high = lax.ppermute(z_msg, "gz", minus_one("gz"))
        y_high = lax.ppermute(y_msg, "gy", minus_one("gy"))
        yz_high = lax.ppermute(yz_msg, ("gy", "gz"), pair_pairs(minus_one("gy"), minus_one("gz")))
        low_half = jnp.concatenate([block, y_high], axis=2)
        high_half = jnp.concatenate([z_high, yz_high], axis=2)
        return jnp.concatenate([low_half, high_half], axis=1)

    both = jnp.concatenate([state, adjoint_seed, eddy_rate[None]], axis=0)
    ext = extend_up(both)
    eddy_ext = ext[2 * Q]
    omega_ext = 1.0 / (0.5 + 3.0 * (NU_BASE + smag_coeff * eddy_ext))
    pops_ext = [ext[i] for i in range(Q)]
    seed_ext = [ext[Q + i] for i in range(Q)]
    away_ext = departures(pops_ext)
    post_ext = [pops_ext[i] + omega_ext * away_ext[i] for i in range(Q)]
    heat_ext = omega_ext * omega_ext * eddy_ext
    tangent_ext = [heat_ext * away_ext[i] for i in range(Q)]

    def window(field, offset):
        return field[
            tuple(slice(1 + offset[a], 1 + offset[a] + sizes[a]) for a in (2, 1, 0))
        ]

    here = (0, 0, 0)

    def pull(field):
        out = []
        for i in range(Q):
            offset = tuple(-v for v in VEL[i])
            out.append(
                jnp.where(
                    blocked(1, i, -1), window(field[OPPOSITE[i]], here), window(field[i], offset)
                )
            )
        return out

    def push(start, own, target):
        out = []
        fluid = ~solid[box(start, here)]
        for i in range(Q):
            open_way = fluid if i == 0 else fluid & ~crossing(start, VEL[i])
            out.append(
                jnp.where(open_way, target(i), 0.0)
                + jnp.where(blocked(start, i, 1), own(OPPOSITE[i]), 0.0)
            )
        return out

    def drag_links(start):
        fluid = ~solid[box(start, here)]
        return {
            i: jnp.where(fluid & blocked(start, i, 1), 2.0 * scale * VEL[i][0], 0.0)
            for i in range(Q)
            if VEL[i][0] != 0
        }

    links = drag_links(1)
    f_one = pull(post_ext)
    tangent_one = pull(tangent_ext)
    cot_one = push(
        1, lambda i: window(seed_ext[i], here), lambda i: window(seed_ext[i], VEL[i])
    )
    cot_one = [cot_one[i] + links[i] if i in links else cot_one[i] for i in range(Q)]
    omega_one = window(omega_ext, here)
    adjoint_one, grad_one, away_one = collide_adjoint(f_one, omega_one, cot_one)
    drag_local = jnp.sum(
        signed(
            [
                (1, links[i] * (window(post_ext[i], here) + f_one[i] + omega_one * away_one[i]))
                for i in links
            ]
        )
    )
    sens_local = jnp.sum(
        signed([(1, adjoint_one[i] * tangent_one[i]) for i in range(Q)])
        + signed([(1, links[i] * window(tangent_ext[i], here)) for i in links])
        + window(heat_ext, here) * grad_one
    ) * (-3.0 / math.sqrt(total_x * total_y * total_z))

    back = jnp.stack(adjoint_one + [grad_one])
    lanes = lax.iota(jnp.int32, 128).reshape(1, 128)
    sums = jnp.where(lanes == 0, drag_local, jnp.where(lanes == 1, sens_local, 0.0))

    def total_over(axes, row):
        count = math.prod(lax.axis_size(a) for a in axes)
        parts = lax.all_to_all(
            jnp.broadcast_to(row, (count, 128)), axes, split_axis=0, concat_axis=0, tiled=True
        )
        return jnp.sum(parts, 0, keepdims=True)

    back, sums = lax.optimization_barrier((back, sums))
    low = lax.ppermute(back[..., -2:], "gx", plus_one("gx"))
    sums = total_over(("gy", "gz"), sums)
    wide = jnp.concatenate([low, back], axis=-1)
    y_msg, z_msg, yz_msg, sums = lax.optimization_barrier(
        (wide[:, :, -2:], wide[:, -2:], wide[:, -2:, -2:], sums)
    )
    z_low = lax.ppermute(z_msg, "gz", plus_one("gz"))
    y_low = lax.ppermute(y_msg, "gy", plus_one("gy"))
    yz_low = lax.ppermute(yz_msg, ("gy", "gz"), pair_pairs(plus_one("gy"), plus_one("gz")))
    sums = total_over(("gx",), sums)
    high_half = jnp.concatenate([y_low, wide], axis=2)
    low_half = jnp.concatenate([yz_low, z_low], axis=2)
    back_ext = jnp.concatenate([low_half, high_half], axis=1)

    links = drag_links(0)
    cot_zero = push(
        0,
        lambda i: window(back_ext[i], here),
        lambda i: window(back_ext[i], VEL[i]),
    )
    cot_zero = [cot_zero[i] + links[i] if i in links else cot_zero[i] for i in range(Q)]
    omega = 1.0 / (0.5 + 3.0 * (NU_BASE + smag_coeff * eddy_rate))
    adjoint_zero, grad_zero, _ = collide_adjoint([state[i] for i in range(Q)], omega, cot_zero)
    grad = grad_zero + window(back_ext[Q], here)
    return jnp.stack(adjoint_zero), -3.0 * omega * omega * grad, sums[0, :2]


def solution(mesh):
    return jax.shard_map(
        on_device,
        mesh=mesh,
        in_specs=(
            P(None, "gz", "gy", "gx"),
            P(None, "gz", "gy", "gx"),
            P("gz", "gy", "gx"),
            P(),
            P(),
        ),
        out_specs=(P(None, "gz", "gy", "gx"), P("gz", "gy", "gx"), P()),
        check_vma=False,
    )
```

time: 218 us -> 120 us (0.55)
  blocking collectives: 106 us -> 0 us
  waiting for transfers between devices: 34.7 us -> 40.2 us
  local copies, waits for them, and re-layouts: 3.7 us -> 6.21 us
    psum x1 -> x0, blocking collectives: 106 us -> none  [on_device(): sensitivity = lax.psum(sens_local, ('gx', 'gy', 'gz'))]
    ppermute x18 -> x8, starting transfers between devices: 54.4 us -> 32.5 us  [the longest x1 8.2 us: extend_up(): lax.ppermute(yz_msg, ('gy', 'gz'), pair_pairs(minus_one('gy'), minus_one(...]
    all_to_all x0 -> x2, starting transfers between devices: none -> 21.9 us  [total_over(): lax.all_to_all(jnp.broadcast_to(row, (count, 128)), axes, split_axis=0, c...]
    all_to_all x0 -> x2, waiting for transfers between devices: none -> 9.96 us  [total_over(): lax.all_to_all(jnp.broadcast_to(row, (count, 128)), axes, split_axis=0, c...]
    unnamed x69 -> x25, other arithmetic: 5.83 us -> 1.12 us
    ppermute x18 -> x8, waiting for transfers between devices: 34.7 us -> 30.2 us  [the longest x1 11.4 us: extend_up(): z_high = lax.ppermute(z_msg, 'gz', minus_one('gz'))]
    mul x2 -> x5, other arithmetic: 0.13 us -> 2.43 us  [the longest x1 1.19 us: on_device(): return (jnp.stack(adjoint_zero), -3.0 * omega * omega * grad, sums[0, :2])]
  transfers between devices with their start and end apart: 18 -> 10, of which waited for: 9 -> 6; matrix products, arithmetic and copies ran while one was open for 3% -> 7% of each run, Pallas kernels for 0% -> 0%
where the time goes in v1:
time: 120 us
  starting transfers between devices  54.4 us (45%)
  waiting for transfers between devices  40.2 us (34%)
  other arithmetic  16 us (13%)
  local copies, waits for them, and re-layouts  6.21 us (5%)
  between operations  2.82 us (2%)
    all_to_all x2, starting transfers between devices, total_over(): lax.all_to_all(jnp.broadcast_to(row, (count, 128)), axes, split_axis=0, c...  21.9 us
    ppermute x1, waiting for transfers between devices, extend_up(): z_high = lax.ppermute(z_msg, 'gz', minus_one('gz'))  11.4 us
    all_to_all x2, waiting for transfers between devices, total_over(): lax.all_to_all(jnp.broadcast_to(row, (count, 128)), axes, split_axis=0, c...  9.96 us
    ppermute x1, starting transfers between devices, extend_up(): lax.ppermute(yz_msg, ('gy', 'gz'), pair_pairs(minus_one('gy'), minus_one(...  8.2 us
    ppermute x1, starting transfers between devices, extend_up(): high = lax.ppermute(block[..., :2], 'gx', minus_one('gx'))  6.88 us
    ppermute x1, waiting for transfers between devices, on_device(): y_low = lax.ppermute(y_msg, 'gy', plus_one('gy'))  6.81 us
    ppermute x1, waiting for transfers between devices, extend_up(): y_high = lax.ppermute(y_msg, 'gy', minus_one('gy'))  5.62 us
    ppermute x1, waiting for transfers between devices, on_device(): z_low = lax.ppermute(z_msg, 'gz', plus_one('gz'))  4.75 us
  transfers between devices with their start and end apart: 10, of which 6 were waited for; matrix products, arithmetic and copies ran while one was open for 7% of the time, Pallas kernels for 0%

profile of v1, /device:TPU:1, one launch (start us, length us, event | category | flops | bytes accessed | tf_op | source)
XLA Modules:
  0.0 119.6 jit_solution(14129638795194710514)
XLA Ops:
  0.7 1.2 pad_maximum_fusion.1
  1.8 0.5 copy.159
  2.3 6.9 %collective-permute-start = (f32[39,4,8,2]{0,2,3,1:T(8,128)S(1)}, f32[39,4,8,2]{0,2,3,1:T(8,128)S(1)}, u32[]{:S(2)}, u32[]{:S(2)}) collective-permute-start(f32[39,4,8,2]{0,2,3,1:T(8,128)S(1)} %copy.159), channel_id=1, source_target_pairs={{64,0},{128,64},{192,128},{256,192},{320,256},{384,320},{448,384},... | collective-permute-start | bytes 29960 | tf_op jit(solution)/shard_map/ppermute | solution.py:171
  9.2 0.8 slice.577
  10.0 0.8 slice.578
  10.7 0.9 pad_add_fusion
  11.8 0.6 not_bitcast_fusion.1
  12.4 0.6 slice_not_fusion.2
  12.9 0.6 not_bitcast_fusion
  13.5 0.1 concatenate.36
  13.7 0.1 dynamic_slice.3
  13.8 0.1 broadcast_compare_fusion
  13.9 0.1 fusion.213
  13.9 0.7 fusion.243
  14.6 0.7 copy.160
  15.3 1.1 pad_maximum_fusion.5
  16.4 0.1 pad_maximum_fusion
  16.5 8.2 %collective-permute-start.3 = (f32[39,2,2,130]{3,2,1,0:T(2,128)S(1)}, f32[39,2,2,130]{3,2,1,0:T(2,128)}, u32[]{:S(2)}, u32[]{:S(2)}) collective-permute-start(f32[39,2,2,130]{3,2,1,0:T(2,128)S(1)} %pad_maximum_fusion.5), channel_id=1, source_target_pairs={{17,0},{18,1},{19,2},{20,3},{21,4},{22,5},{23,6},{24,7},{25,8},{26... | collective-permute-start | bytes 243368 | tf_op jit(solution)/shard_map/ppermute | solution.py:176
  24.8 3.1 %collective-permute-start.2 = (f32[39,2,8,130]{3,2,1,0:T(8,128)S(1)}, f32[39,2,8,130]{3,2,1,0:T(8,128)S(1)}, u32[]{:S(2)}, u32[]{:S(2)}) collective-permute-start(f32[39,2,8,130]{3,2,1,0:T(8,128)S(1)} %slice.1460), channel_id=1, source_target_pairs={{1,0},{2,1},{3,2},{4,3},{5,4},{6,5},{7,6},{8,7},{9,8},{10,9},{11,1... | collective-permute-start | bytes 973448 | tf_op jit(solution)/shard_map/ppermute | solution.py:174
  27.9 0.1 pad_maximum_fusion.3
  28.0 2.2 %collective-permute-start.1 = (f32[39,4,2,130]{3,2,1,0:T(2,128)S(1)}, f32[39,4,2,130]{3,2,1,0:T(2,128)S(1)}, u32[]{:S(2)}, u32[]{:S(2)}) collective-permute-start(f32[39,4,2,130]{3,2,1,0:T(2,128)S(1)} %pad_maximum_fusion.3), channel_id=1, source_target_pairs={{16,0},{32,16},{48,32},{0,48},{17,1},{33,17},{49,33},{1,49},{18,2}... | collective-permute-start | bytes 486728 | tf_op jit(solution)/shard_map/ppermute | solution.py:175
  30.2 0.7 fusion.240
  31.5 5.6 %collective-permute-done.1 = f32[39,4,2,130]{3,2,1,0:T(2,128)S(1)} collective-permute-done((f32[39,4,2,130]{3,2,1,0:T(2,128)S(1)}, f32[39,4,2,130]{3,2,1,0:T(2,128)S(1)}, u32[]{:S(2)}, u32[]{:S(2)}) %collective-permute-start.1) | collective-permute-done | bytes 162272 | tf_op jit(solution)/shard_map/ppermute | solution.py:175
  37.1 11.4 %collective-permute-done.2 = f32[39,2,8,130]{3,2,1,0:T(8,128)S(1)} collective-permute-done((f32[39,2,8,130]{3,2,1,0:T(8,128)S(1)}, f32[39,2,8,130]{3,2,1,0:T(8,128)S(1)}, u32[]{:S(2)}, u32[]{:S(2)}) %collective-permute-start.2) | collective-permute-done | bytes 324512 | tf_op jit(solution)/shard_map/ppermute | solution.py:174
  48.5 1.3 %maximum_maximum_fusion = f32[39,6,10,130]{3,2,1,0:T(8,128)S(1)} fusion(f32[39,2,2,130]{3,2,1,0:T(2,128)} %collective-permute-done.3, f32[39,2,8,130]{3,2,1,0:T(8,128)S(1)} %collective-permute-done.2, f32[39,4,2,130]{3,2,1,0:T(2,128)S(1)} %collective-permute-done.1, f32[39,4,8,2]{3,2,1,0:T(8,128)S(1)} %copy.160, f32[1,4,8,128]{3,2,1,0:T(8,128)S(1)} %bitcast.822, ...), kind=kLoop, calls=%fused_computation | loop fusion | flops 1825200 | bytes 2433600 | tf_op jit(solution)/shard_map/concatenate | solution.py:179
  49.9 0.2 slice_bitcast_fusion.55
  50.1 0.3 fusion.247
  50.4 0.1 fusion.249
  50.5 0.4 fusion.248
  51.1 0.2 multiply_add_fusion.1
  51.3 0.2 multiply_add_fusion.17
  51.5 1.1 fusion.199
  52.6 0.4 add_multiply_fusion.4
  53.0 1.2 %fusion.200 = (f32[]{:T(128)}, f32[4,8,128]{2,1,0:T(8,128)S(1)}, f32[4,8,128]{2,1,0:T(8,128)S(1)}, f32[4,8,128]{2,1,0:T(8,128)S(1)}, f32[4,8,128]{2,1,0:T(8,128)...) fusion(f32[6,10,130]{2,1,0:T(8,128)S(1)} %get-tuple-element.219, ...), kind=kLoop, calls=%fused_computation.661 | loop fusion | flops 2101247 | bytes 1706396 | tf_op jit(solution)/shard_map/reduce_sum | solution.py:246
  54.2 0.1 constant_dynamic-update-slice_fusion.19
  54.3 0.1 constant_dynamic-update-slice_fusion.18
  54.4 0.1 constant_dynamic-update-slice_fusion.17
  54.5 0.1 constant_dynamic-update-slice_fusion.16
  54.6 0.1 constant_dynamic-update-slice_fusion.15
  54.6 0.1 constant_dynamic-update-slice_fusion.14
  54.7 0.1 constant_dynamic-update-slice_fusion.13
  55.5 0.6 compare_select_fusion.2
  56.2 0.1 slice.1360
  56.4 4.5 %collective-permute-start.4 = (f32[20,4,8,2]{3,2,1,0:T(8,128)S(1)}, f32[20,4,8,2]{3,2,1,0:T(8,128)S(1)}, u32[]{:S(2)}, u32[]{:S(2)}) collective-permute-start(f32[20,4,8,2]{3,2,1,0:T(8,128)S(1)} %slice.1360), channel_id=1, source_target_pairs={{0,64},{64,128},{128,192},{192,256},{256,320},{320,384},{384,448},... | collective-permute-start | bytes 15368 | tf_op jit(solution)/shard_map/ppermute | solution.py:264
  60.9 0.6 broadcast_in_dim.164
  61.5 17.1 %all-to-all-start = ((f32[64,1,128]{2,1,0:T(1,128)}), f32[64,1,128]{2,1,0:T(1,128)S(1)}, u32[]{:S(2)}, u32[]{:S(2)}) async-start(f32[64,1,128]{2,1,0:T(1,128)} %broadcast_in_dim.164), calls=%async_computation | async-start | bytes 65536 | tf_op jit(solution)/shard_map/all_to_all | solution.py:258
  78.7 0.2 pad_maximum_fusion.4
  78.9 0.1 fusion
  79.2 0.2 pad_maximum_fusion.6
  79.3 10.0 %all-to-all-done = f32[64,1,128]{2,1,0:T(1,128)S(1)} async-done(((f32[64,1,128]{2,1,0:T(1,128)}), f32[64,1,128]{2,1,0:T(1,128)S(1)}, u32[]{:S(2)}, u32[]{:S(2)}) %all-to-all-start) | async-done | bytes 32800 | tf_op jit(solution)/shard_map/all_to_all | solution.py:258
  89.3 0.6 broadcast_in_dim.166
  89.9 4.8 %all-to-all-start.1 = ((f32[8,1,128]{2,1,0:T(1,128)}), f32[8,1,128]{2,1,0:T(1,128)S(1)}, u32[]{:S(2)}, u32[]{:S(2)}) async-start(f32[8,1,128]{2,1,0:T(1,128)} %broadcast_in_dim.166), calls=%async_computation.1 | async-start | bytes 8192 | tf_op jit(solution)/shard_map/all_to_all | solution.py:258
  94.7 2.4 %collective-permute-start.5 = (f32[20,2,2,130]{3,2,1,0:T(2,128)S(1)}, f32[20,2,2,130]{3,2,1,0:T(2,128)S(1)}, u32[]{:S(2)}, u32[]{:S(2)}) collective-permute-start(f32[20,2,2,130]{3,2,1,0:T(2,128)S(1)} %pad_maximum_fusion.6), channel_id=1, source_target_pairs={{0,17},{1,18},{2,19},{3,20},{4,21},{5,22},{6,23},{7,24},{8,25},{9,... | collective-permute-start | bytes 124808 | tf_op jit(solution)/shard_map/ppermute | solution.py:272
  97.1 3.3 %collective-permute-start.7 = (f32[20,4,2,130]{3,2,1,0:T(2,128)S(1)}, f32[20,4,2,130]{3,2,1,0:T(2,128)S(1)}, u32[]{:S(2)}, u32[]{:S(2)}) collective-permute-start(f32[20,4,2,130]{3,2,1,0:T(2,128)S(1)} %pad_maximum_fusion.4), channel_id=1, source_target_pairs={{0,16},{16,32},{32,48},{48,0},{1,17},{17,33},{33,49},{49,1},{2,18}... | collective-permute-start | bytes 249608 | tf_op jit(solution)/shard_map/ppermute | solution.py:271
  100.4 1.9 %collective-permute-start.6 = (f32[20,2,8,130]{3,2,1,0:T(8,128)S(1)}, f32[20,2,8,130]{3,2,1,0:T(8,128)S(1)}, u32[]{:S(2)}, u32[]{:S(2)}) collective-permute-start(f32[20,2,8,130]{3,2,1,0:T(8,128)S(1)} %fusion), channel_id=1, source_target_pairs={{0,1},{1,2},{2,3},{3,4},{4,5},{5,6},{6,7},{7,8},{8,9},{9,10},{10,1... | collective-permute-start | bytes 499208 | tf_op jit(solution)/shard_map/ppermute | solution.py:270
  102.4 0.5 slice_bitcast_fusion.65
  102.9 1.7 %collective-permute-done.5 = f32[20,2,2,130]{3,2,1,0:T(2,128)S(1)} collective-permute-done((f32[20,2,2,130]{3,2,1,0:T(2,128)S(1)}, f32[20,2,2,130]{3,2,1,0:T(2,128)S(1)}, u32[]{:S(2)}, u32[]{:S(2)}) %collective-permute-start.5) | collective-permute-done | bytes 41632 | tf_op jit(solution)/shard_map/ppermute | solution.py:272
  104.6 6.8 %collective-permute-done.7 = f32[20,4,2,130]{3,2,1,0:T(2,128)S(1)} collective-permute-done((f32[20,4,2,130]{3,2,1,0:T(2,128)S(1)}, f32[20,4,2,130]{3,2,1,0:T(2,128)S(1)}, u32[]{:S(2)}, u32[]{:S(2)}) %collective-permute-start.7) | collective-permute-done | bytes 83232 | tf_op jit(solution)/shard_map/ppermute | solution.py:271
  111.4 4.8 %collective-permute-done.6 = f32[20,2,8,130]{3,2,1,0:T(8,128)S(1)} collective-permute-done((f32[20,2,8,130]{3,2,1,0:T(8,128)S(1)}, f32[20,2,8,130]{3,2,1,0:T(8,128)S(1)}, u32[]{:S(2)}, u32[]{:S(2)}) %collective-permute-start.6) | collective-permute-done | bytes 166432 | tf_op jit(solution)/shard_map/ppermute | solution.py:270
  116.1 0.4 maximum_maximum_fusion.1
  116.6 0.2 slice_bitcast_fusion.14
  116.9 1.2 fusion.28
  118.1 0.2 constant_dynamic-update-slice_fusion.38
  118.9 0.7 copy-done.25
  (97 shorter events, 0.8 us)
Async XLA Ops:
  0.6 15.7 %copy-start = (f32[19,4,8,128]{3,2,1,0:T(8,128)S(1)}, f32[19,4,8,128]{3,2,1,0:T(8,128)}, u32[]{:S(2)}) copy-start(f32[19,4,8,128]{3,2,1,0:T(8,128)} %param.5) | copy-start | bytes 933892
  0.6 15.7 %copy-start.1 = (f32[4,8,128]{2,1,0:T(8,128)S(1)}, f32[4,8,128]{2,1,0:T(8,128)}, u32[]{:S(2)}) copy-start(f32[4,8,128]{2,1,0:T(8,128)} %param.7) | copy-start | bytes 49156
  0.7 15.7 %copy-start.2 = (f32[19,4,8,128]{3,2,1,0:T(8,128)S(1)}, f32[19,4,8,128]{3,2,1,0:T(8,128)}, u32[]{:S(2)}) copy-start(f32[19,4,8,128]{3,2,1,0:T(8,128)} %param.6) | copy-start | bytes 933892
  2.3 12.3 %collective-permute-start = (f32[39,4,8,2]{0,2,3,1:T(8,128)S(1)}, f32[39,4,8,2]{0,2,3,1:T(8,128)S(1)}, u32[]{:S(2)}, u32[]{:S(2)}) collective-permute-start(f32[39,4,8,2]{0,2,3,1:T(8,128)S(1)} %copy.159), channel_id=1, source_target_pairs={{64,0},{128,64},{192,128},{256,192},{320,256},{384,320},{448,384},... | collective-permute-start | bytes 29960 | tf_op jit(solution)/shard_map/ppermute | solution.py:171
  16.5 15.0 %collective-permute-start.3 = (f32[39,2,2,130]{3,2,1,0:T(2,128)S(1)}, f32[39,2,2,130]{3,2,1,0:T(2,128)}, u32[]{:S(2)}, u32[]{:S(2)}) collective-permute-start(f32[39,2,2,130]{3,2,1,0:T(2,128)S(1)} %pad_maximum_fusion.5), channel_id=1, source_target_pairs={{17,0},{18,1},{19,2},{20,3},{21,4},{22,5},{23,6},{24,7},{25,8},{26... | collective-permute-start | bytes 243368 | tf_op jit(solution)/shard_map/ppermute | solution.py:176
  24.8 23.7 %collective-permute-start.2 = (f32[39,2,8,130]{3,2,1,0:T(8,128)S(1)}, f32[39,2,8,130]{3,2,1,0:T(8,128)S(1)}, u32[]{:S(2)}, u32[]{:S(2)}) collective-permute-start(f32[39,2,8,130]{3,2,1,0:T(8,128)S(1)} %slice.1460), channel_id=1, source_target_pairs={{1,0},{2,1},{3,2},{4,3},{5,4},{6,5},{7,6},{8,7},{9,8},{10,9},{11,1... | collective-permute-start | bytes 973448 | tf_op jit(solution)/shard_map/ppermute | solution.py:174
  28.0 9.2 %collective-permute-start.1 = (f32[39,4,2,130]{3,2,1,0:T(2,128)S(1)}, f32[39,4,2,130]{3,2,1,0:T(2,128)S(1)}, u32[]{:S(2)}, u32[]{:S(2)}) collective-permute-start(f32[39,4,2,130]{3,2,1,0:T(2,128)S(1)} %pad_maximum_fusion.3), channel_id=1, source_target_pairs={{16,0},{32,16},{48,32},{0,48},{17,1},{33,17},{49,33},{1,49},{18,2}... | collective-permute-start | bytes 486728 | tf_op jit(solution)/shard_map/ppermute | solution.py:175
  51.0 1.6 %copy-start.16 = (pred[128]{0:T(512)(128)(4,1)S(1)}, pred[128]{0:T(512)(128)(4,1)}, u32[]{:S(2)}) copy-start(pred[128]{0:T(512)(128)(4,1)} %get-tuple-element.298) | copy-start | bytes 388
  51.0 1.6 %copy-start.17 = (pred[4]{0:T(512)(128)(4,1)S(1)}, pred[4]{0:T(512)(128)(4,1)}, u32[]{:S(2)}) copy-start(pred[4]{0:T(512)(128)(4,1)} %get-tuple-element.318) | copy-start | bytes 16
  51.0 1.6 %copy-start.18 = (pred[8]{0:T(512)(128)(4,1)S(1)}, pred[8]{0:T(512)(128)(4,1)}, u32[]{:S(2)}) copy-start(pred[8]{0:T(512)(128)(4,1)} %get-tuple-element.324) | copy-start | bytes 28
  51.0 1.6 %copy-start.19 = (pred[4,8]{1,0:T(4,128)(4,1)S(1)}, pred[4,8]{1,0:T(4,128)(4,1)}, u32[]{:S(2)}) copy-start(pred[4,8]{1,0:T(4,128)(4,1)} %get-tuple-element.334) | copy-start | bytes 100
  51.0 1.6 %copy-start.20 = (pred[4,8]{1,0:T(4,128)(4,1)S(1)}, pred[4,8]{1,0:T(4,128)(4,1)}, u32[]{:S(2)}) copy-start(pred[4,8]{1,0:T(4,128)(4,1)} %get-tuple-element.336) | copy-start | bytes 100
  51.0 1.6 %copy-start.21 = (pred[4,8]{1,0:T(4,128)(4,1)S(1)}, pred[4,8]{1,0:T(4,128)(4,1)}, u32[]{:S(2)}) copy-start(pred[4,8]{1,0:T(4,128)(4,1)} %get-tuple-element.338) | copy-start | bytes 100
  51.0 1.6 %copy-start.22 = (pred[4,128]{1,0:T(4,128)(4,1)S(1)}, pred[4,128]{1,0:T(4,128)(4,1)}, u32[]{:S(2)}) copy-start(pred[4,128]{1,0:T(4,128)(4,1)} %get-tuple-element.346) | copy-start | bytes 1540
  51.0 1.6 %copy-start.23 = (pred[4,128]{1,0:T(4,128)(4,1)S(1)}, pred[4,128]{1,0:T(4,128)(4,1)}, u32[]{:S(2)}) copy-start(pred[4,128]{1,0:T(4,128)(4,1)} %get-tuple-element.348) | copy-start | bytes 1540
  51.0 1.6 %copy-start.24 = (pred[4,128]{1,0:T(4,128)(4,1)S(1)}, pred[4,128]{1,0:T(4,128)(4,1)}, u32[]{:S(2)}) copy-start(pred[4,128]{1,0:T(4,128)(4,1)} %get-tuple-element.350) | copy-start | bytes 1540
  56.4 22.3 %collective-permute-start.4 = (f32[20,4,8,2]{3,2,1,0:T(8,128)S(1)}, f32[20,4,8,2]{3,2,1,0:T(8,128)S(1)}, u32[]{:S(2)}, u32[]{:S(2)}) collective-permute-start(f32[20,4,8,2]{3,2,1,0:T(8,128)S(1)} %slice.1360), channel_id=1, source_target_pairs={{0,64},{64,128},{128,192},{192,256},{256,320},{320,384},{384,448},... | collective-permute-start | bytes 15368 | tf_op jit(solution)/shard_map/ppermute | solution.py:264
  61.5 27.8 %all-to-all-start = ((f32[64,1,128]{2,1,0:T(1,128)}), f32[64,1,128]{2,1,0:T(1,128)S(1)}, u32[]{:S(2)}, u32[]{:S(2)}) async-start(f32[64,1,128]{2,1,0:T(1,128)} %broadcast_in_dim.164), calls=%async_computation | async-start | bytes 65536 | tf_op jit(solution)/shard_map/all_to_all | solution.py:258
  79.1 37.7 %copy-start.3 = (pred[8]{0:T(512)(128)(4,1)S(1)}, pred[8]{0:T(512)(128)(4,1)}, u32[]{:S(2)}) copy-start(pred[8]{0:T(512)(128)(4,1)} %get-tuple-element.322) | copy-start | bytes 28
  79.1 37.7 %copy-start.4 = (pred[4,8]{1,0:T(4,128)(4,1)S(1)}, pred[4,8]{1,0:T(4,128)(4,1)}, u32[]{:S(2)}) copy-start(pred[4,8]{1,0:T(4,128)(4,1)} %get-tuple-element.68) | copy-start | bytes 100
  79.1 37.7 %copy-start.5 = (pred[4,8]{1,0:T(4,128)(4,1)S(1)}, pred[4,8]{1,0:T(4,128)(4,1)}, u32[]{:S(2)}) copy-start(pred[4,8]{1,0:T(4,128)(4,1)} %get-tuple-element.69) | copy-start | bytes 100
  79.1 37.7 %copy-start.6 = (pred[4,8]{1,0:T(4,128)(4,1)S(1)}, pred[4,8]{1,0:T(4,128)(4,1)}, u32[]{:S(2)}) copy-start(pred[4,8]{1,0:T(4,128)(4,1)} %get-tuple-element.328) | copy-start | bytes 100
  79.1 37.7 %copy-start.7 = (pred[4,8]{1,0:T(4,128)(4,1)S(1)}, pred[4,8]{1,0:T(4,128)(4,1)}, u32[]{:S(2)}) copy-start(pred[4,8]{1,0:T(4,128)(4,1)} %get-tuple-element.329) | copy-start | bytes 100
  79.1 37.7 %copy-start.8 = (pred[4,8]{1,0:T(4,128)(4,1)S(1)}, pred[4,8]{1,0:T(4,128)(4,1)}, u32[]{:S(2)}) copy-start(pred[4,8]{1,0:T(4,128)(4,1)} %get-tuple-element.330) | copy-start | bytes 100
  79.1 37.7 %copy-start.9 = (pred[4,8]{1,0:T(4,128)(4,1)S(1)}, pred[4,8]{1,0:T(4,128)(4,1)}, u32[]{:S(2)}) copy-start(pred[4,8]{1,0:T(4,128)(4,1)} %get-tuple-element.331) | copy-start | bytes 100
  79.1 37.7 %copy-start.10 = (pred[4,128]{1,0:T(4,128)(4,1)S(1)}, pred[4,128]{1,0:T(4,128)(4,1)}, u32[]{:S(2)}) copy-start(pred[4,128]{1,0:T(4,128)(4,1)} %get-tuple-element.62) | copy-start | bytes 1540
  79.1 37.7 %copy-start.11 = (pred[4,128]{1,0:T(4,128)(4,1)S(1)}, pred[4,128]{1,0:T(4,128)(4,1)}, u32[]{:S(2)}) copy-start(pred[4,128]{1,0:T(4,128)(4,1)} %get-tuple-element.63) | copy-start | bytes 1540
  79.2 37.7 %copy-start.12 = (pred[4,128]{1,0:T(4,128)(4,1)S(1)}, pred[4,128]{1,0:T(4,128)(4,1)}, u32[]{:S(2)}) copy-start(pred[4,128]{1,0:T(4,128)(4,1)} %get-tuple-element.340) | copy-start | bytes 1540
  79.2 37.7 %copy-start.13 = (pred[4,128]{1,0:T(4,128)(4,1)S(1)}, pred[4,128]{1,0:T(4,128)(4,1)}, u32[]{:S(2)}) copy-start(pred[4,128]{1,0:T(4,128)(4,1)} %get-tuple-element.341) | copy-start | bytes 1540
  79.2 37.7 %copy-start.14 = (pred[4,128]{1,0:T(4,128)(4,1)S(1)}, pred[4,128]{1,0:T(4,128)(4,1)}, u32[]{:S(2)}) copy-start(pred[4,128]{1,0:T(4,128)(4,1)} %get-tuple-element.342) | copy-start | bytes 1540
  79.2 37.7 %copy-start.15 = (pred[4,128]{1,0:T(4,128)(4,1)S(1)}, pred[4,128]{1,0:T(4,128)(4,1)}, u32[]{:S(2)}) copy-start(pred[4,128]{1,0:T(4,128)(4,1)} %get-tuple-element.343) | copy-start | bytes 1540
  89.9 12.4 %all-to-all-start.1 = ((f32[8,1,128]{2,1,0:T(1,128)}), f32[8,1,128]{2,1,0:T(1,128)S(1)}, u32[]{:S(2)}, u32[]{:S(2)}) async-start(f32[8,1,128]{2,1,0:T(1,128)} %broadcast_in_dim.166), calls=%async_computation.1 | async-start | bytes 8192 | tf_op jit(solution)/shard_map/all_to_all | solution.py:258
  94.7 9.9 %collective-permute-start.5 = (f32[20,2,2,130]{3,2,1,0:T(2,128)S(1)}, f32[20,2,2,130]{3,2,1,0:T(2,128)S(1)}, u32[]{:S(2)}, u32[]{:S(2)}) collective-permute-start(f32[20,2,2,130]{3,2,1,0:T(2,128)S(1)} %pad_maximum_fusion.6), channel_id=1, source_target_pairs={{0,17},{1,18},{2,19},{3,20},{4,21},{5,22},{6,23},{7,24},{8,25},{9,... | collective-permute-start | bytes 124808 | tf_op jit(solution)/shard_map/ppermute | solution.py:272
  97.1 14.3 %collective-permute-start.7 = (f32[20,4,2,130]{3,2,1,0:T(2,128)S(1)}, f32[20,4,2,130]{3,2,1,0:T(2,128)S(1)}, u32[]{:S(2)}, u32[]{:S(2)}) collective-permute-start(f32[20,4,2,130]{3,2,1,0:T(2,128)S(1)} %pad_maximum_fusion.4), channel_id=1, source_target_pairs={{0,16},{16,32},{32,48},{48,0},{1,17},{17,33},{33,49},{49,1},{2,18}... | collective-permute-start | bytes 249608 | tf_op jit(solution)/shard_map/ppermute | solution.py:271
  100.4 15.7 %collective-permute-start.6 = (f32[20,2,8,130]{3,2,1,0:T(8,128)S(1)}, f32[20,2,8,130]{3,2,1,0:T(8,128)S(1)}, u32[]{:S(2)}, u32[]{:S(2)}) collective-permute-start(f32[20,2,8,130]{3,2,1,0:T(8,128)S(1)} %fusion), channel_id=1, source_target_pairs={{0,1},{1,2},{2,3},{3,4},{4,5},{5,6},{6,7},{7,8},{8,9},{9,10},{10,1... | collective-permute-start | bytes 499208 | tf_op jit(solution)/shard_map/ppermute | solution.py:270
  118.8 0.7 copy-start.25

commit v2 on v1

v2 whole, which is shorter than its diff:
```python
import functools
import math

import jax
import jax.numpy as jnp
from jax import lax
from jax.experimental import pallas as pl
from jax.experimental.pallas import tpu as pltpu
from jax.sharding import PartitionSpec as P

VEL = [
    (0, 0, 0),
    (1, 0, 0),
    (-1, 0, 0),
    (0, 1, 0),
    (0, -1, 0),
    (0, 0, 1),
    (0, 0, -1),
    (1, 1, 0),
    (-1, -1, 0),
    (1, -1, 0),
    (-1, 1, 0),
    (1, 0, 1),
    (-1, 0, -1),
    (1, 0, -1),
    (-1, 0, 1),
    (0, 1, 1),
    (0, -1, -1),
    (0, 1, -1),
    (0, -1, 1),
]
OPPOSITE = [0, 2, 1, 4, 3, 6, 5, 8, 7, 10, 9, 12, 11, 14, 13, 16, 15, 18, 17]
LATTICE_WEIGHTS = [1.0 / 3.0] + [1.0 / 18.0] * 6 + [1.0 / 36.0] * 12
UREF = 0.08
NU_BASE = 0.004
Q = 19
DEPTH = 4
ROWS = 8
COLS = 128
FAR = 1 << 20
UP = [i for i in range(Q) if VEL[i][2] == 1]
DOWN = [i for i in range(Q) if VEL[i][2] == -1]
SIDES = [(dy, dx) for dy in (-1, 0, 1) for dx in (-1, 0, 1)]

N_UP = 2 * Q + 1
N_BACK = Q + 1
UP_Z = [(c, 0) for c in range(N_UP)] + [
    (c, 1) for c in range(N_UP) if c < Q or c == 2 * Q or c - Q in UP
]
BACK_Z = [(c, 2) for c in DOWN] + [(c, 3) for c in range(N_BACK)]


def strips(fields):
    return -(-fields * DEPTH * 2 // COLS)


def signed(terms):
    total = None
    for factor, value in terms:
        if factor == 0:
            continue
        piece = value if factor == 1 else (-value if factor == -1 else factor * value)
        total = piece if total is None else total + piece
    return total


def along(idx, vec):
    return signed([(VEL[idx][axis], vec[axis]) for axis in range(3)])


def flow(pops):
    rho = signed([(1, p) for p in pops])
    inverse = 1.0 / rho
    vel = [signed([(VEL[i][axis], pops[i]) for i in range(Q)]) * inverse for axis in range(3)]
    return rho, vel


def shapes(vel):
    base = 1.0 - 1.5 * (vel[0] * vel[0] + vel[1] * vel[1] + vel[2] * vel[2])
    out = [base] + [None] * (Q - 1)
    for i in range(1, Q, 2):
        cu = along(i, vel)
        even = base + 4.5 * cu * cu
        out[i] = even + 3.0 * cu
        out[i + 1] = even - 3.0 * cu
    return out


def departures(pops):
    rho, vel = flow(pops)
    shape = shapes(vel)
    return [LATTICE_WEIGHTS[i] * rho * shape[i] - pops[i] for i in range(Q)]


def collide_adjoint(pops, omega, cot):
    rho, vel = flow(pops)
    shape = shapes(vel)
    weighted = [LATTICE_WEIGHTS[i] * cot[i] for i in range(Q)]
    level = signed([(1, weighted[i] * shape[i]) for i in range(Q)])
    mass = signed([(1, w) for w in weighted])
    first = [signed([(VEL[i][axis], weighted[i]) for i in range(Q)]) for axis in range(3)]

    def second(a, b):
        return signed([(VEL[i][a] * VEL[i][b], weighted[i]) for i in range(Q)])

    pair = {(a, b): second(a, b) for a in range(3) for b in range(a, 3)}
    slope = []
    for a in range(3):
        mixed = signed([(1, pair[min(a, b), max(a, b)] * vel[b]) for b in range(3)])
        slope.append(3.0 * first[a] + 9.0 * mixed - 3.0 * mass * vel[a])
    base = omega * (level - (slope[0] * vel[0] + slope[1] * vel[1] + slope[2] * vel[2]))
    tilt = [omega * s for s in slope]
    keep = 1.0 - omega
    adjoint = []
    for i in range(Q):
        part = along(i, tilt)
        adjoint.append(keep * cot[i] + (base if part is None else base + part))
    away = [LATTICE_WEIGHTS[i] * rho * shape[i] - pops[i] for i in range(Q)]
    grad = signed([(1, cot[i] * away[i]) for i in range(Q)])
    return adjoint, grad, away


def relaxation(smag, eddy):
    return 1.0 / (0.5 + 3.0 * (NU_BASE + smag * eddy))


def row_ids():
    return lax.broadcasted_iota(jnp.int32, (ROWS, COLS), 0)


def lane_ids():
    return lax.broadcasted_iota(jnp.int32, (ROWS, COLS), 1)


def turn(tile, amount, axis):
    size = tile.shape[axis]
    if isinstance(amount, int):
        amount %= size
        return tile if amount == 0 else pltpu.roll(tile, amount, axis)
    return pltpu.roll(tile, lax.rem(amount + size, size), axis)


def pack_columns(out_ref, planes, start):
    lanes = lane_ids()
    per = COLS // 2
    for strip in range(-(-len(planes) // per)):
        total = None
        for j, plane in enumerate(planes[strip * per : (strip + 1) * per]):
            moved = turn(plane(), 2 * j - start, 1)
            total = moved if total is None else jnp.where(lanes >= 2 * j, moved, total)
        out_ref[:, strip * COLS : (strip + 1) * COLS] = total


def pack_rows(planes, start):
    rows = row_ids()
    total = None
    for j, plane in enumerate(planes):
        moved = turn(plane, 2 * j - start, 0)
        total = moved if total is None else jnp.where(rows >= 2 * j, moved, total)
    return total


def pack_faces(plane, fields, strip, n_strips, layers, z_list, start, z_ref, y_ref, yz_ref):
    for at, (c, z) in enumerate(z_list):
        z_ref[at] = plane(c, z)
    columns = [strip(v) for v in range(n_strips)]
    for v in range(n_strips):
        z_ref[len(z_list) + v] = columns[v]
    for c in range(fields):
        y_ref[c] = pack_rows([plane(c, z) for z in range(DEPTH)], start)
    y_ref[fields] = pack_rows(columns, start)
    pairs = [(c, z) for c in range(fields) for z in layers]
    for at in range(0, len(pairs), 4):
        yz_ref[at // 4] = pack_rows([plane(c, z) for c, z in pairs[at : at + 4]], start)
    yz_ref[-(-len(pairs) // 4)] = pack_rows(columns, start)


def up_columns_kernel(state_ref, seed_ref, eddy_ref, out_ref):
    planes = [
        functools.partial(lambda r, c, z: r[c, z], ref, c, z)
        for ref in (state_ref, seed_ref)
        for c in range(Q)
        for z in range(DEPTH)
    ] + [functools.partial(lambda z: eddy_ref[z], z) for z in range(DEPTH)]
    pack_columns(out_ref, planes, 0)


def up_faces_kernel(state_ref, seed_ref, eddy_ref, x_ref, z_ref, y_ref, yz_ref):
    def plane(c, z):
        if c == 2 * Q:
            return eddy_ref[z]
        return state_ref[c, z] if c < Q else seed_ref[c - Q, z]

    def strip(v):
        return x_ref[:, v * COLS : (v + 1) * COLS]

    pack_faces(plane, N_UP, strip, strips(N_UP), (0, 1), UP_Z, 0, z_ref, y_ref, yz_ref)


def back_faces_kernel(back_ref, x_ref, z_ref, y_ref, yz_ref):
    def plane(c, z):
        return back_ref[c, z]

    def strip(v):
        return x_ref[:, v * COLS : (v + 1) * COLS]

    pack_faces(
        plane, N_BACK, strip, strips(N_BACK), (2, 3), BACK_Z, ROWS - 1, z_ref, y_ref, yz_ref
    )


def level_of(start_z, total_z, plane):
    level = start_z + plane
    return lax.rem(level + total_z, total_z)


def wall_between(start_z, total_z, plane, step):
    upper = start_z + plane + (1 if step > 0 else 0)
    return (upper == total_z) | (upper == 0)


def masks_at(high_ref, own_ref, start_z, total_z, plane):
    solid, way = {}, {}
    here = level_of(start_z, total_z, plane)
    for i in range(Q):
        dx, dy, dz = VEL[i]
        side = SIDES.index((dy, dx))
        there, mine = here, here
        if dz:
            wall = wall_between(start_z, total_z, plane, dz)
            there = jnp.where(wall, -1, level_of(start_z, total_z, plane + dz))
            mine = jnp.where(wall, -1, here)
        solid[VEL[i]] = there < high_ref[side]
        way[VEL[i]] = mine >= own_ref[side]
    return solid, way


def drag_links(solid, way, scale):
    fluid = way[VEL[0]]
    return {
        i: jnp.where(fluid & solid[VEL[i]], 2.0 * scale * VEL[i][0], 0.0)
        for i in range(Q)
        if VEL[i][0] != 0
    }


def pushed(i, own, target, solid, way, links):
    value = jnp.where(way[VEL[i]], target, 0.0) + jnp.where(solid[VEL[i]], own, 0.0)
    return value + links[i] if i in links else value


def middle_kernel(
    total_z,
    scale,
    sens_scale,
    place_ref,
    smag_ref,
    state_ref,
    seed_ref,
    eddy_ref,
    x_ref,
    y_ref,
    z_ref,
    yz_ref,
    high_ref,
    own_ref,
    back_ref,
    columns_ref,
    sums_ref,
    post_main,
    tang_main,
    seed_main,
    post_y,
    tang_y,
    seed_y,
    post_x,
    tang_x,
    seed_x,
):
    smag = smag_ref[0]
    start_z = place_ref[0]
    rows, lanes = row_ids(), lane_ids()
    z_at = {key: at for at, key in enumerate(UP_Z)}
    per = COLS // (2 * DEPTH)

    def collide_into(pops, eddy, store):
        omega = relaxation(smag, eddy)
        away = departures(pops)
        heat = omega * omega * eddy
        for i in range(Q):
            store(i, pops[i] + omega * away[i], heat * away[i])

    def body(z, carry):
        def store(i, post, tang):
            post_main[i, z] = post
            tang_main[i, z] = tang

        collide_into([state_ref[i, z] for i in range(Q)], eddy_ref[z], store)
        for i in range(Q):
            seed_main[i, z] = seed_ref[i, z]
        return carry

    lax.fori_loop(0, DEPTH, body, 0)
    for k in (0, 1):

        def store(i, post, tang, k=k):
            post_main[i, DEPTH + k] = post
            tang_main[i, DEPTH + k] = tang

        collide_into(
            [z_ref[z_at[i, k]] for i in range(Q)], z_ref[z_at[2 * Q, k]], store
        )
        for i in range(Q):
            if (Q + i, k) in z_at:
                seed_main[i, DEPTH + k] = z_ref[z_at[Q + i, k]]

    def corner_rows(c):
        return turn(yz_ref[c // 2], -4 * (c % 2), 0)

    for k, tile in ((0, lambda c: y_ref[c]), (1, corner_rows)):

        def store(i, post, tang, k=k):
            post_y[i, k] = post
            tang_y[i, k] = tang

        collide_into([tile(i) for i in range(Q)], tile(2 * Q), store)
        for i in range(Q):
            seed_y[i, k] = tile(Q + i)

    n_strips = strips(N_UP)
    yx_tiles = [turn(y_ref[N_UP], -2 * v, 0) for v in range(n_strips)]
    yzx_tiles = [turn(yz_ref[-(-N_UP // 2)], -2 * v, 0) for v in range(n_strips)]

    def column_tile(c):
        v, at = c // per, 2 * DEPTH * (c % per)
        near = turn(x_ref[:, v * COLS : (v + 1) * COLS], -at, 1)
        above = turn(z_ref[len(UP_Z) + v], 8 - at, 1)
        near_rows = turn(yx_tiles[v], 16 - at, 1)
        above_rows = turn(yzx_tiles[v], 24 - at, 1)
        return jnp.where(
            lanes < 16,
            jnp.where(lanes < 8, near, above),
            jnp.where(lanes < 24, near_rows, above_rows),
        )

    def store(i, post, tang):
        post_x[i] = post
        tang_x[i] = tang

    collide_into([column_tile(i) for i in range(Q)], column_tile(2 * Q), store)
    for i in range(Q):
        seed_x[i] = column_tile(Q + i)

    def viewer(main, y_tiles, x_tiles, cache):
        def view(c, plane, dy, dx):
            key = (c, id(plane), dy, dx)
            if key in cache:
                return cache[key]
            tile = main[c, plane]
            if dx >= 0:
                tile = jnp.where(lanes <= dx, turn(x_tiles[c], -2 * plane, 1), tile)
            if dy >= 0:
                low = turn(y_tiles[c, plane // DEPTH], -2 * (plane % DEPTH), 0)
                if dx >= 0:
                    low = jnp.where(lanes <= dx, turn(x_tiles[c], -16 - 2 * plane, 1), low)
                tile = jnp.where(rows <= dy, low, tile)
            tile = turn(turn(tile, -dx, 1), -dy, 0)
            cache[key] = tile
            return tile

        return view

    def middle(z, carry):
        drag, sens = carry
        planes = {dz: z + 1 + dz for dz in (-1, 0, 1)}
        solid, way = masks_at(high_ref, own_ref, start_z, total_z, planes[0])
        links = drag_links(solid, way, scale)
        view_post = viewer(post_main, post_y, post_x, {})
        view_tang = viewer(tang_main, tang_y, tang_x, {})
        view_seed = viewer(seed_main, seed_y, seed_x, {})

        def pulled(view, i):
            dx, dy, dz = VEL[i]
            if i == 0:
                return view(0, planes[0], 0, 0)
            return jnp.where(
                solid[-dx, -dy, -dz],
                view(OPPOSITE[i], planes[0], 0, 0),
                view(i, planes[-dz], -dy, -dx),
            )

        f_one = [pulled(view_post, i) for i in range(Q)]
        cot = []
        for i in range(Q):
            dx, dy, dz = VEL[i]
            own = view_seed(OPPOSITE[i], planes[0], 0, 0)
            cot.append(pushed(i, own, view_seed(i, planes[dz], dy, dx), solid, way, links))

        own_plane = z + 1
        last = z == DEPTH - 1
        inside = eddy_ref[lax.rem(own_plane, DEPTH)]
        tile = jnp.where(last, z_ref[z_at[2 * Q, 0]], inside)
        columns = jnp.where(
            last,
            turn(z_ref[len(UP_Z) + 2 * Q // per], -2 * DEPTH * (2 * Q % per), 1),
            turn(
                x_ref[:, (2 * Q // per) * COLS : (2 * Q // per + 1) * COLS],
                -2 * DEPTH * (2 * Q % per) - 2 * own_plane,
                1,
            ),
        )
        low = jnp.where(
            last, corner_rows(2 * Q), turn(y_ref[2 * Q], -2 * lax.rem(own_plane, DEPTH), 0)
        )
        low_columns = jnp.where(
            last,
            turn(yzx_tiles[2 * Q // per], -2 * DEPTH * (2 * Q % per), 1),
            turn(yx_tiles[2 * Q // per], -2 * DEPTH * (2 * Q % per) - 2 * own_plane, 1),
        )
        tile = jnp.where(lanes == 0, columns, tile)
        low = jnp.where(lanes == 0, low_columns, low)
        eddy = jnp.where(rows == 0, low, tile)

        omega = relaxation(smag, eddy)
        adjoint, grad, away = collide_adjoint(f_one, omega, cot)
        for i in range(Q):
            back_ref[i, z] = adjoint[i]
        back_ref[Q, z] = grad
        for i in links:
            drag = drag + links[i] * (
                view_post(i, planes[0], 0, 0) + f_one[i] + omega * away[i]
            )
            sens = sens + links[i] * view_tang(i, planes[0], 0, 0)
        sens = sens + omega * omega * eddy * grad
        for i in range(Q):
            sens = sens + adjoint[i] * pulled(view_tang, i)
        return drag, sens

    zero = jnp.zeros((ROWS, COLS), jnp.float32)
    drag, sens = lax.fori_loop(0, DEPTH, middle, (zero, zero))
    both = jnp.where(
        lax.broadcasted_iota(jnp.int32, sums_ref.shape, 1) == 0,
        jnp.sum(drag),
        jnp.sum(sens) * sens_scale,
    )
    sums_ref[...] = both
    planes = [
        functools.partial(lambda c, z: back_ref[c, z], c, z)
        for c in range(N_BACK)
        for z in range(DEPTH)
    ]
    pack_columns(columns_ref, planes, COLS - 1)


def last_kernel(
    total_z,
    scale,
    place_ref,
    smag_ref,
    state_ref,
    eddy_ref,
    back_ref,
    x_ref,
    y_ref,
    z_ref,
    yz_ref,
    high_ref,
    own_ref,
    out_ref,
    grad_ref,
):
    smag = smag_ref[0]
    start_z = place_ref[0]
    rows, lanes = row_ids(), lane_ids()
    z_at = {key: at for at, key in enumerate(BACK_Z)}
    n_strips = strips(N_BACK)
    per = COLS // 2

    @functools.cache
    def strip(kind, v):
        if kind == "x":
            return x_ref[:, v * COLS : (v + 1) * COLS]
        if kind == "z":
            return z_ref[len(BACK_Z) + v]
        tile = y_ref[N_BACK] if kind == "y" else yz_ref[-(-N_BACK // 2)]
        return turn(tile, -2 * v - 1, 0)

    @functools.cache
    def columns(kind, c, layer):
        p = c * DEPTH + layer
        return turn(strip(kind, p // per), -2 * (p % per) - 1, 1)

    @functools.cache
    def view(c, plane, dy, dx):
        inner = plane >= 1
        layer = plane - 1 if inner else plane + 3
        tile = back_ref[c, layer] if inner else z_ref[z_at[c, layer]]

        def with_columns(tile, kind):
            if dx > 0:
                return tile
            keep = (lanes == 0) if dx == 0 else (lanes == 0) | (lanes == COLS - 1)
            return jnp.where(keep, columns(kind, c, layer), tile)

        tile = with_columns(tile, "x" if inner else "z")
        if dy <= 0:
            if inner:
                low = turn(y_ref[c], -2 * layer - 1, 0)
            else:
                low = turn(yz_ref[c // 2], -4 * (c % 2) - 2 * (layer - 2) - 1, 0)
            low = with_columns(low, "y" if inner else "yz")
            keep = (rows == 0) if dy == 0 else (rows == 0) | (rows == ROWS - 1)
            tile = jnp.where(keep, low, tile)
        return turn(turn(tile, -dx, 1), -dy, 0)

    for z in range(DEPTH):
        solid, way = masks_at(high_ref, own_ref, start_z, total_z, z)
        links = drag_links(solid, way, scale)
        cot = []
        for i in range(Q):
            dx, dy, dz = VEL[i]
            own = view(OPPOSITE[i], z, 0, 0)
            cot.append(pushed(i, own, view(i, z + dz, dy, dx), solid, way, links))
        omega = relaxation(smag, eddy_ref[z])
        adjoint, grad, _ = collide_adjoint([state_ref[i, z] for i in range(Q)], omega, cot)
        for i in range(Q):
            out_ref[i, z] = adjoint[i]
        grad_ref[z] = -3.0 * omega * omega * (grad + view(Q, z, 0, 0))


def plus_one(axis):
    count = lax.axis_size(axis)
    return [(i, (i + 1) % count) for i in range(count)]


def minus_one(axis):
    return [(target, source) for source, target in plus_one(axis)]


def pair_pairs(first, second):
    count = lax.axis_size("gz")
    return [(a * count + b, c * count + d) for a, c in first for b, d in second]


def heights_by_side(heights):
    total_y, total_x = heights.shape
    start_y = lax.axis_index("gy") * ROWS
    start_x = lax.axis_index("gx") * COLS
    padded = jnp.pad(heights, ((1, 2), (1, 2)), mode="wrap")
    near = lax.dynamic_slice(padded, (start_y, start_x), (ROWS + 3, COLS + 3))
    y = start_y - 1 + lax.broadcasted_iota(jnp.int32, near.shape, 0)
    x = start_x - 1 + lax.broadcasted_iota(jnp.int32, near.shape, 1)
    edge_y = (y == -1) | (y == total_y - 1)
    edge_x = (x == -1) | (x == total_x - 1)

    def cut(array, first, dy, dx):
        row, col = first + 1 + dy, first + 1 + dx
        return array[row : row + ROWS, col : col + COLS]

    out = []
    for first in (1, 0):
        high, own = [], []
        for dy, dx in SIDES:
            wall = jnp.zeros((ROWS, COLS), bool)
            if dy:
                wall = wall | cut(edge_y, first, min(dy, 0), 0)
            if dx:
                wall = wall | cut(edge_x, first, 0, min(dx, 0))
            high.append(jnp.where(wall, FAR, cut(near, first, dy, dx)))
            own.append(jnp.where(wall, FAR, cut(near, first, 0, 0)))
        for part in (high, own):
            stacked = jnp.stack(part)
            out.append(jnp.roll(stacked, (first, first), (1, 2)) if first else stacked)
    return out


def call(kernel, outs, n_scalars, operands, scratch=(), flops=0):
    specs = [
        pl.BlockSpec(memory_space=pltpu.SMEM if k < n_scalars else pltpu.VMEM)
        for k in range(len(operands))
    ]
    return pl.pallas_call(
        kernel,
        out_shape=[jax.ShapeDtypeStruct(shape, jnp.float32) for shape in outs],
        in_specs=specs,
        out_specs=[pl.BlockSpec(memory_space=pltpu.VMEM)] * len(outs),
        scratch_shapes=[pltpu.VMEM(shape, jnp.float32) for shape in scratch],
        compiler_params=pltpu.CompilerParams(vmem_limit_bytes=32 << 20),
        cost_estimate=pl.CostEstimate(flops=flops, bytes_accessed=1 << 20, transcendentals=0),
    )(*operands)


def total_over(axes, rows):
    parts = lax.all_to_all(rows, axes, split_axis=0, concat_axis=0, tiled=True)
    return jnp.sum(parts, 0, keepdims=True)


def on_device(state, adjoint_seed, eddy_rate, smag_coeff, heights):
    total_x = COLS * lax.axis_size("gx")
    total_y = ROWS * lax.axis_size("gy")
    total_z = DEPTH * lax.axis_size("gz")
    scale = 1.0 / (2.0 * UREF * total_x * total_y)
    sens_scale = -3.0 / math.sqrt(total_x * total_y * total_z)
    place = (lax.axis_index("gz") * DEPTH).astype(jnp.int32).reshape(1)
    smag = smag_coeff.reshape(1)
    mid_high, mid_own, end_high, end_own = heights_by_side(heights)

    tile = (ROWS, COLS)
    (columns,) = call(
        up_columns_kernel,
        [(ROWS, strips(N_UP) * COLS)],
        0,
        (state, adjoint_seed, eddy_rate),
    )
    columns = lax.ppermute(columns, "gx", minus_one("gx"))
    z_msg, y_msg, yz_msg = call(
        up_faces_kernel,
        [
            (len(UP_Z) + strips(N_UP), *tile),
            (N_UP + 1, *tile),
            (-(-N_UP // 2) + 1, *tile),
        ],
        0,
        (state, adjoint_seed, eddy_rate, columns),
    )
    z_msg = lax.ppermute(z_msg, "gz", minus_one("gz"))
    y_msg = lax.ppermute(y_msg, "gy", minus_one("gy"))
    yz_msg = lax.ppermute(yz_msg, ("gy", "gz"), pair_pairs(minus_one("gy"), minus_one("gz")))

    n_first = lax.axis_size("gy") * lax.axis_size("gz")
    back, back_columns, sums = call(
        functools.partial(middle_kernel, total_z, scale, sens_scale),
        [(N_BACK, DEPTH, *tile), (ROWS, strips(N_BACK) * COLS), (n_first, COLS)],
        2,
        (
            place,
            smag,
            state,
            adjoint_seed,
            eddy_rate,
            columns,
            y_msg,
            z_msg,
            yz_msg,
            mid_high,
            mid_own,
        ),
        [(Q, DEPTH + 2, *tile)] * 3 + [(Q, 2, *tile)] * 3 + [(Q, *tile)] * 3,
        flops=20_000_000,
    )
    back_columns = lax.ppermute(back_columns, "gx", plus_one("gx"))
    sums = total_over(("gy", "gz"), sums)
    z_msg, y_msg, yz_msg = call(
        back_faces_kernel,
        [
            (len(BACK_Z) + strips(N_BACK), *tile),
            (N_BACK + 1, *tile),
            (-(-N_BACK // 2) + 1, *tile),
        ],
        0,
        (back, back_columns),
    )
    z_msg = lax.ppermute(z_msg, "gz", plus_one("gz"))
    y_msg = lax.ppermute(y_msg, "gy", plus_one("gy"))
    yz_msg = lax.ppermute(yz_msg, ("gy", "gz"), pair_pairs(plus_one("gy"), plus_one("gz")))
    sums = total_over(("gx",), jnp.broadcast_to(sums, (lax.axis_size("gx"), COLS)))
    adjoint_state, gradient = call(
        functools.partial(last_kernel, total_z, scale),
        [(Q, DEPTH, *tile), (DEPTH, *tile)],
        2,
        (
            place,
            smag,
            state,
            eddy_rate,
            back,
            back_columns,
            y_msg,
            z_msg,
            yz_msg,
            end_high,
            end_own,
        ),
        flops=20_000_000,
    )
    return adjoint_state, gradient, sums[0, :2]


def solution(mesh):
    return jax.shard_map(
        on_device,
        mesh=mesh,
        in_specs=(
            P(None, "gz", "gy", "gx"),
            P(None, "gz", "gy", "gx"),
            P("gz", "gy", "gx"),
            P(),
            P(),
        ),
        out_specs=(P(None, "gz", "gy", "gx"), P("gz", "gy", "gx"), P()),
        check_vma=False,
    )
```

time: 120 us -> 84.7 us (0.71)
  waiting for transfers between devices: 40.2 us -> 16.3 us
  other arithmetic: 16 us -> 2 us
  Pallas kernels: 0 us -> 4.76 us
  between operations: 2.82 us -> 1.52 us
    ppermute x7, waiting for transfers between devices: 28.6 us -> 11.1 us  [the longest x1 5.34 us: on_device(): lax.ppermute(yz_msg, ('gy', 'gz'), pair_pairs(minus_one('gy'), minus_one(...]
    all_to_all x2, waiting for transfers between devices: 9.96 us -> 4.69 us  [total_over(): parts = lax.all_to_all(rows, axes, split_axis=0, concat_axis=0, tiled=True)]
    pallas_call x0 -> x5, Pallas kernels: none -> 4.76 us  [call(): pl.pallas_call(kernel, out_shape=[jax.ShapeDtypeStruct(shape, jnp.float32...]
    concatenate x7 -> x6, other arithmetic: 4.27 us -> 0.31 us  [the longest x5 0.29 us: heights_by_side(): out.append(jnp.roll(stacked, (first, first), (1, 2)) if first else stacked)]
    mul x5 -> x0, other arithmetic: 2.43 us -> none  [the longest x1 1.19 us: on_device(): return (jnp.stack(adjoint_zero), -3.0 * omega * omega * grad, sums[0, :2])]
    unnamed x64 -> x16, local copies, waits for them, and re-layouts: 0.88 us -> 3.24 us
    reduce_sum x2 -> x0, other arithmetic: 2.31 us -> none  [the longest x1 1.22 us: on_device(): jnp.sum(signed([(1, adjoint_one[i] * tangent_one[i]) for i in range(Q)])...]
    not x4 -> x0, other arithmetic: 2.04 us -> none  [push(): open_way = fluid if i == 0 else fluid & ~crossing(start, VEL[i])]
  transfers between devices with their start and end apart: 10 -> 10, of which waited for: 6 -> 6; matrix products, arithmetic and copies ran while one was open for 7% -> 4% of each run, Pallas kernels for 0% -> 0%
where the time goes in v2:
time: 84.7 us; the launch traced here: 83.8 us
  starting transfers between devices  53.8 us (64%)
  waiting for transfers between devices  16.3 us (19%)
  local copies, waits for them, and re-layouts  5.43 us (6%)
  Pallas kernels  4.76 us (6%)
  other arithmetic  2 us (2%)
  between operations  1.52 us (2%)
    all_to_all x2, starting transfers between devices, total_over(): parts = lax.all_to_all(rows, axes, split_axis=0, concat_axis=0, tiled=True)  20.2 us
    ppermute x1, starting transfers between devices, on_device(): y_msg = lax.ppermute(y_msg, 'gy', minus_one('gy'))  9.37 us
    ppermute x1, starting transfers between devices, on_device(): columns = lax.ppermute(columns, 'gx', minus_one('gx'))  6.89 us
    ppermute x1, starting transfers between devices, on_device(): back_columns = lax.ppermute(back_columns, 'gx', plus_one('gx'))  5.96 us
    ppermute x1, waiting for transfers between devices, on_device(): lax.ppermute(yz_msg, ('gy', 'gz'), pair_pairs(minus_one('gy'), minus_one(...  5.34 us
    pallas_call x5, Pallas kernels, call(): pl.pallas_call(kernel, out_shape=[jax.ShapeDtypeStruct(shape, jnp.float32...  4.76 us
    all_to_all x2, waiting for transfers between devices, total_over(): parts = lax.all_to_all(rows, axes, split_axis=0, concat_axis=0, tiled=True)  4.69 us
    ppermute x1, waiting for transfers between devices, on_device(): y_msg = lax.ppermute(y_msg, 'gy', plus_one('gy'))  3.3 us
  transfers between devices with their start and end apart: 10, of which 6 were waited for; matrix products, arithmetic and copies ran while one was open for 4% of the time, Pallas kernels for 0%

profile of v2, /device:TPU:1, one launch (start us, length us, event | category | flops | bytes accessed | tf_op | source)
XLA Modules:
  0.0 83.8 jit_solution(563674742978845016)
XLA Ops:
  0.6 0.0 copy-start
  0.6 1.0 %copy-done = f32[19,4,8,128]{3,2,1,0:T(8,128)S(1)} copy-done((f32[19,4,8,128]{3,2,1,0:T(8,128)S(1)}, f32[19,4,8,128]{3,2,1,0:T(8,128)}, u32[]{:S(2)}) %copy-start) | copy-done | bytes 311320
  1.6 1.0 %copy-done.2 = f32[19,4,8,128]{3,2,1,0:T(8,128)S(1)} copy-done((f32[19,4,8,128]{3,2,1,0:T(8,128)S(1)}, f32[19,4,8,128]{3,2,1,0:T(8,128)}, u32[]{:S(2)}) %copy-start.2) | copy-done | bytes 311320
  2.6 0.7 copy-done.4
  3.3 0.2 shard_map.76
  3.5 6.9 %collective-permute-start = (f32[8,384]{1,0:T(8,128)S(1)}, f32[8,384]{1,0:T(8,128)S(1)}, u32[]{:S(2)}, u32[]{:S(2)}) collective-permute-start(f32[8,384]{1,0:T(8,128)S(1)} %shard_map.76), channel_id=1, source_target_pairs={{64,0},{128,64},{192,128},{256,192},{320,256},{384,320},{448,384},... | collective-permute-start | bytes 36872 | tf_op jit(solution)/shard_map/ppermute | solution.py:615
  10.4 0.0 copy-done.6
  10.4 0.0 slice-start
  10.4 0.7 slice-done
  11.2 0.1 slice.188
  11.2 0.1 fusion.19
  11.3 0.1 fusion.18
  11.4 0.1 concatenate.23
  11.6 0.0 copy-start.1
  11.6 0.1 constant_dynamic-update-slice_fusion.35
  11.7 0.1 constant_dynamic-update-slice_fusion.34
  11.7 0.1 constant_dynamic-update-slice_fusion.33
  11.8 0.1 constant_dynamic-update-slice_fusion.29
  11.9 0.1 constant_dynamic-update-slice_fusion.28
  12.0 0.1 constant_dynamic-update-slice_fusion.27
  12.1 0.1 constant_dynamic-update-slice_fusion.21
  12.1 0.1 constant_dynamic-update-slice_fusion.20
  12.2 0.1 constant_dynamic-update-slice_fusion.19
  12.3 0.1 constant_dynamic-update-slice_fusion.18
  12.4 0.1 constant_dynamic-update-slice_fusion.17
  12.5 0.1 constant_dynamic-update-slice_fusion.16
  12.5 0.1 constant_dynamic-update-slice_fusion.15
  12.6 0.1 constant_dynamic-update-slice_fusion.11
  12.7 0.1 constant_dynamic-update-slice_fusion.10
  12.8 0.1 constant_dynamic-update-slice_fusion.9
  12.9 0.1 constant_dynamic-update-slice_fusion.3
  12.9 0.1 constant_dynamic-update-slice_fusion.2
  13.0 0.1 constant_dynamic-update-slice_fusion.1
  13.1 0.1 constant_dynamic-update-slice_fusion
  13.2 0.0 copy-start.5
  13.2 0.1 slice_add_fusion
  13.3 0.0 collective-permute-done.x_ref
  13.3 0.6 copy-done.5
  13.9 0.1 shard_map.77
  14.0 1.9 %collective-permute-start.2 = (f32[67,8,128]{2,1,0:T(8,128)S(1)}, f32[67,8,128]{2,1,0:T(8,128)S(1)}, u32[]{:S(2)}, u32[]{:S(2)}) collective-permute-start(f32[67,8,128]{2,1,0:T(8,128)S(1)} %get-tuple-element.15), channel_id=1, source_target_pairs={{1,0},{2,1},{3,2},{4,3},{5,4},{6,5},{7,6},{8,7},{9,8},{10,9},{11,1... | collective-permute-start | bytes 823304 | tf_op jit(solution)/shard_map/ppermute | solution.py:626
  15.9 9.4 %collective-permute-start.1 = (f32[40,8,128]{2,1,0:T(8,128)S(1)}, f32[40,8,128]{2,1,0:T(8,128)S(1)}, u32[]{:S(2)}, u32[]{:S(2)}) collective-permute-start(f32[40,8,128]{2,1,0:T(8,128)S(1)} %get-tuple-element.14), channel_id=1, source_target_pairs={{16,0},{32,16},{48,32},{0,48},{17,1},{33,17},{49,33},{1,49},{18,2}... | collective-permute-start | bytes 491528 | tf_op jit(solution)/shard_map/ppermute | solution.py:627
  25.3 0.1 slice_add_fusion.1
  26.1 1.9 %collective-permute-start.3 = (f32[21,8,128]{2,1,0:T(8,128)S(1)}, f32[21,8,128]{2,1,0:T(8,128)S(1)}, u32[]{:S(2)}, u32[]{:S(2)}) collective-permute-start(f32[21,8,128]{2,1,0:T(8,128)S(1)} %get-tuple-element.16), channel_id=1, source_target_pairs={{17,0},{18,1},{19,2},{20,3},{21,4},{22,5},{23,6},{24,7},{25,8},{26... | collective-permute-start | bytes 258056 | tf_op jit(solution)/shard_map/ppermute | solution.py:628
  28.0 0.1 pad_add_fusion.3
  28.1 5.3 %collective-permute-done.3.yz_ref = f32[21,8,128]{2,1,0:T(8,128)S(1)} collective-permute-done((f32[21,8,128]{2,1,0:T(8,128)S(1)}, f32[21,8,128]{2,1,0:T(8,128)S(1)}, u32[]{:S(2)}, u32[]{:S(2)}) %collective-permute-start.3) | collective-permute-done | bytes 86048 | tf_op jit(solution)/shard_map/ppermute | solution.py:628
  33.4 0.7 collective-permute-done.1.y_ref
  34.2 0.0 collective-permute-done.2.z_ref
  34.2 3.1 %shard_map.78 = (f32[20,4,8,128]{3,2,1,0:T(8,128)S(1)}, f32[8,256]{1,0:T(8,128)S(1)}, f32[64,128]{1,0:T(8,128)}) custom-call(s32[1]{0:T(128)} %bitcast.place_ref, f32[1]{0:T(128)} %bitcast.117.smag_ref, f32[19,4,8,128]{3,2,1,0:T(8,128)S(1)} %copy-done.1, f32[19,4,8,128]{3,2,1,0:T(8,128)S(1)} %copy-done.3, f32[4,8,128]{2,1,0:T(8,128)S(1)} %copy-done.5, ...), custom_call_target="tpu_custom_call" | custom-call | flops 20000000 | bytes 1048576 | tf_op jit(solution)/shard_map/pallas_call | solution.py:582
  37.2 9.9 %all-to-all-start = ((f32[64,1,128]{2,1,0:T(1,128)}), f32[64,1,128]{2,1,0:T(1,128)S(1)}, u32[]{:S(2)}, u32[]{:S(2)}) async-start(f32[64,1,128]{2,1,0:T(1,128)} %bitcast.35), calls=%async_computation | async-start | bytes 65536 | tf_op jit(solution)/shard_map/all_to_all | solution.py:594
  47.2 6.0 %collective-permute-start.4 = (f32[8,256]{1,0:T(8,128)S(1)}, f32[8,256]{1,0:T(8,128)S(1)}, u32[]{:S(2)}, u32[]{:S(2)}) collective-permute-start(f32[8,256]{1,0:T(8,128)S(1)} %get-tuple-element.18), channel_id=1, source_target_pairs={{0,64},{64,128},{128,192},{192,256},{256,320},{320,384},{384,448},... | collective-permute-start | bytes 24584 | tf_op jit(solution)/shard_map/ppermute | solution.py:651
  53.1 4.7 %all-to-all-done = f32[64,1,128]{2,1,0:T(1,128)S(1)} async-done(((f32[64,1,128]{2,1,0:T(1,128)}), f32[64,1,128]{2,1,0:T(1,128)S(1)}, u32[]{:S(2)}, u32[]{:S(2)}) %all-to-all-start) | async-done | bytes 32800 | tf_op jit(solution)/shard_map/all_to_all | solution.py:594
  57.8 0.1 reduce_sum.18
  57.9 0.6 broadcast_in_dim.49
  58.5 10.3 %all-to-all-start.1 = ((f32[8,1,128]{2,1,0:T(1,128)}), f32[8,1,128]{2,1,0:T(1,128)S(1)}, u32[]{:S(2)}, u32[]{:S(2)}) async-start(f32[8,1,128]{2,1,0:T(1,128)} %broadcast_in_dim.49), calls=%async_computation.1 | async-start | bytes 8192 | tf_op jit(solution)/shard_map/all_to_all | solution.py:594
  68.8 0.0 collective-permute-done.4.x_ref
  68.8 2.4 %collective-permute-start.7 = (f32[11,8,128]{2,1,0:T(8,128)S(1)}, f32[11,8,128]{2,1,0:T(8,128)S(1)}, u32[]{:S(2)}, u32[]{:S(2)}) collective-permute-start(f32[11,8,128]{2,1,0:T(8,128)S(1)} %get-tuple-element.21), channel_id=1, source_target_pairs={{0,17},{1,18},{2,19},{3,20},{4,21},{5,22},{6,23},{7,24},{8,25},{9,... | collective-permute-start | bytes 135176 | tf_op jit(solution)/shard_map/ppermute | solution.py:665
  71.2 3.2 %collective-permute-start.5 = (f32[21,8,128]{2,1,0:T(8,128)S(1)}, f32[21,8,128]{2,1,0:T(8,128)S(1)}, u32[]{:S(2)}, u32[]{:S(2)}) collective-permute-start(f32[21,8,128]{2,1,0:T(8,128)S(1)} %get-tuple-element.19), channel_id=1, source_target_pairs={{0,16},{16,32},{32,48},{48,0},{1,17},{17,33},{33,49},{49,1},{2,18}... | collective-permute-start | bytes 258056 | tf_op jit(solution)/shard_map/ppermute | solution.py:664
  74.4 1.9 %collective-permute-start.6 = (f32[27,8,128]{2,1,0:T(8,128)S(1)}, f32[27,8,128]{2,1,0:T(8,128)S(1)}, u32[]{:S(2)}, u32[]{:S(2)}) collective-permute-start(f32[27,8,128]{2,1,0:T(8,128)S(1)} %get-tuple-element.20), channel_id=1, source_target_pairs={{0,1},{1,2},{2,3},{3,4},{4,5},{5,6},{6,7},{7,8},{8,9},{9,10},{10,1... | collective-permute-start | bytes 331784 | tf_op jit(solution)/shard_map/ppermute | solution.py:663
  76.3 0.0 all-to-all-done.1
  76.4 0.5 slice_bitcast_fusion
  76.9 0.6 collective-permute-done.7.yz_ref
  77.5 3.3 %collective-permute-done.5.y_ref = f32[21,8,128]{2,1,0:T(8,128)S(1)} collective-permute-done((f32[21,8,128]{2,1,0:T(8,128)S(1)}, f32[21,8,128]{2,1,0:T(8,128)S(1)}, u32[]{:S(2)}, u32[]{:S(2)}) %collective-permute-start.5) | collective-permute-done | bytes 86048 | tf_op jit(solution)/shard_map/ppermute | solution.py:664
  80.8 1.7 %collective-permute-done.6.z_ref = f32[27,8,128]{2,1,0:T(8,128)S(1)} collective-permute-done((f32[27,8,128]{2,1,0:T(8,128)S(1)}, f32[27,8,128]{2,1,0:T(8,128)S(1)}, u32[]{:S(2)}, u32[]{:S(2)}) %collective-permute-start.6) | collective-permute-done | bytes 110624 | tf_op jit(solution)/shard_map/ppermute | solution.py:663
  82.5 1.4 %shard_map.80 = (f32[19,4,8,128]{3,2,1,0:T(8,128)}, f32[4,8,128]{2,1,0:T(8,128)}) custom-call(s32[1]{0:T(128)} %bitcast.place_ref, f32[1]{0:T(128)} %bitcast.118.smag_ref, f32[19,4,8,128]{3,2,1,0:T(8,128)S(1)} %copy-done.1, f32[4,8,128]{2,1,0:T(8,128)S(1)} %copy-done.5, f32[20,4,8,128]{3,2,1,0:T(8,128)S(1)} %get-tuple-element.17.back_ref, ...), custom_call_target="tpu_custom_call" | custom-call | flops 20000000 | bytes 1048576 | tf_op jit(solution)/shard_map/pallas_call | solution.py:582
  (23 shorter events, 0.2 us)
Async XLA Ops:
  0.6 1.0 %copy-start = (f32[19,4,8,128]{3,2,1,0:T(8,128)S(1)}, f32[19,4,8,128]{3,2,1,0:T(8,128)}, u32[]{:S(2)}) copy-start(f32[19,4,8,128]{3,2,1,0:T(8,128)} %state_ref.7) | copy-start | bytes 933892
  1.6 1.0 %copy-start.2 = (f32[19,4,8,128]{3,2,1,0:T(8,128)S(1)}, f32[19,4,8,128]{3,2,1,0:T(8,128)}, u32[]{:S(2)}) copy-start(f32[19,4,8,128]{3,2,1,0:T(8,128)} %seed_ref.5) | copy-start | bytes 933892
  2.6 0.7 copy-start.4
  3.3 7.1 %copy-start.6 = (s32[32,1024]{1,0:T(8,128)S(1)}, s32[32,1024]{1,0:T(8,128)}, u32[]{:S(2)}) copy-start(s32[32,1024]{1,0:T(8,128)} %param.9) | copy-start | bytes 393220
  3.5 9.8 %collective-permute-start = (f32[8,384]{1,0:T(8,128)S(1)}, f32[8,384]{1,0:T(8,128)S(1)}, u32[]{:S(2)}, u32[]{:S(2)}) collective-permute-start(f32[8,384]{1,0:T(8,128)S(1)} %shard_map.76), channel_id=1, source_target_pairs={{64,0},{128,64},{192,128},{256,192},{320,256},{384,320},{448,384},... | collective-permute-start | bytes 36872 | tf_op jit(solution)/shard_map/ppermute | solution.py:615
  10.4 0.7 slice-start
  11.4 1.9 %copy-start.3 = (f32[19,4,8,128]{3,2,1,0:T(8,128)S(1)}, f32[19,4,8,128]{3,2,1,0:T(8,128)}, u32[]{:S(2)}) copy-start(f32[19,4,8,128]{3,2,1,0:T(8,128)} %seed_ref.5) | copy-start | bytes 933892
  11.6 1.8 %copy-start.1 = (f32[19,4,8,128]{3,2,1,0:T(8,128)S(1)}, f32[19,4,8,128]{3,2,1,0:T(8,128)}, u32[]{:S(2)}) copy-start(f32[19,4,8,128]{3,2,1,0:T(8,128)} %state_ref.7) | copy-start | bytes 933892
  13.2 0.7 copy-start.5
  14.0 20.2 %collective-permute-start.2 = (f32[67,8,128]{2,1,0:T(8,128)S(1)}, f32[67,8,128]{2,1,0:T(8,128)S(1)}, u32[]{:S(2)}, u32[]{:S(2)}) collective-permute-start(f32[67,8,128]{2,1,0:T(8,128)S(1)} %get-tuple-element.15), channel_id=1, source_target_pairs={{1,0},{2,1},{3,2},{4,3},{5,4},{6,5},{7,6},{8,7},{9,8},{10,9},{11,1... | collective-permute-start | bytes 823304 | tf_op jit(solution)/shard_map/ppermute | solution.py:626
  15.9 18.2 %collective-permute-start.1 = (f32[40,8,128]{2,1,0:T(8,128)S(1)}, f32[40,8,128]{2,1,0:T(8,128)S(1)}, u32[]{:S(2)}, u32[]{:S(2)}) collective-permute-start(f32[40,8,128]{2,1,0:T(8,128)S(1)} %get-tuple-element.14), channel_id=1, source_target_pairs={{16,0},{32,16},{48,32},{0,48},{17,1},{33,17},{49,33},{1,49},{18,2}... | collective-permute-start | bytes 491528 | tf_op jit(solution)/shard_map/ppermute | solution.py:627
  26.1 7.4 %collective-permute-start.3 = (f32[21,8,128]{2,1,0:T(8,128)S(1)}, f32[21,8,128]{2,1,0:T(8,128)S(1)}, u32[]{:S(2)}, u32[]{:S(2)}) collective-permute-start(f32[21,8,128]{2,1,0:T(8,128)S(1)} %get-tuple-element.16), channel_id=1, source_target_pairs={{17,0},{18,1},{19,2},{20,3},{21,4},{22,5},{23,6},{24,7},{25,8},{26... | collective-permute-start | bytes 258056 | tf_op jit(solution)/shard_map/ppermute | solution.py:628
  37.2 20.6 %all-to-all-start = ((f32[64,1,128]{2,1,0:T(1,128)}), f32[64,1,128]{2,1,0:T(1,128)S(1)}, u32[]{:S(2)}, u32[]{:S(2)}) async-start(f32[64,1,128]{2,1,0:T(1,128)} %bitcast.35), calls=%async_computation | async-start | bytes 65536 | tf_op jit(solution)/shard_map/all_to_all | solution.py:594
  47.2 21.6 %collective-permute-start.4 = (f32[8,256]{1,0:T(8,128)S(1)}, f32[8,256]{1,0:T(8,128)S(1)}, u32[]{:S(2)}, u32[]{:S(2)}) collective-permute-start(f32[8,256]{1,0:T(8,128)S(1)} %get-tuple-element.18), channel_id=1, source_target_pairs={{0,64},{64,128},{128,192},{192,256},{256,320},{320,384},{384,448},... | collective-permute-start | bytes 24584 | tf_op jit(solution)/shard_map/ppermute | solution.py:651
  58.5 17.8 %all-to-all-start.1 = ((f32[8,1,128]{2,1,0:T(1,128)}), f32[8,1,128]{2,1,0:T(1,128)S(1)}, u32[]{:S(2)}, u32[]{:S(2)}) async-start(f32[8,1,128]{2,1,0:T(1,128)} %broadcast_in_dim.49), calls=%async_computation.1 | async-start | bytes 8192 | tf_op jit(solution)/shard_map/all_to_all | solution.py:594
  68.8 8.6 %collective-permute-start.7 = (f32[11,8,128]{2,1,0:T(8,128)S(1)}, f32[11,8,128]{2,1,0:T(8,128)S(1)}, u32[]{:S(2)}, u32[]{:S(2)}) collective-permute-start(f32[11,8,128]{2,1,0:T(8,128)S(1)} %get-tuple-element.21), channel_id=1, source_target_pairs={{0,17},{1,18},{2,19},{3,20},{4,21},{5,22},{6,23},{7,24},{8,25},{9,... | collective-permute-start | bytes 135176 | tf_op jit(solution)/shard_map/ppermute | solution.py:665
  71.2 9.6 %collective-permute-start.5 = (f32[21,8,128]{2,1,0:T(8,128)S(1)}, f32[21,8,128]{2,1,0:T(8,128)S(1)}, u32[]{:S(2)}, u32[]{:S(2)}) collective-permute-start(f32[21,8,128]{2,1,0:T(8,128)S(1)} %get-tuple-element.19), channel_id=1, source_target_pairs={{0,16},{16,32},{32,48},{48,0},{1,17},{17,33},{33,49},{49,1},{2,18}... | collective-permute-start | bytes 258056 | tf_op jit(solution)/shard_map/ppermute | solution.py:664
  74.4 8.0 %collective-permute-start.6 = (f32[27,8,128]{2,1,0:T(8,128)S(1)}, f32[27,8,128]{2,1,0:T(8,128)S(1)}, u32[]{:S(2)}, u32[]{:S(2)}) collective-permute-start(f32[27,8,128]{2,1,0:T(8,128)S(1)} %get-tuple-element.20), channel_id=1, source_target_pairs={{0,1},{1,2},{2,3},{3,4},{4,5},{5,6},{6,7},{7,8},{8,9},{9,10},{10,1... | collective-permute-start | bytes 331784 | tf_op jit(solution)/shard_map/ppermute | solution.py:663

commit v3 on v2

v3 whole, which is shorter than its diff:
```python
import functools
import math

import jax
import jax.numpy as jnp
from jax import lax
from jax.experimental import pallas as pl
from jax.experimental.pallas import tpu as pltpu
from jax.sharding import PartitionSpec as P

VEL = [
    (0, 0, 0),
    (1, 0, 0),
    (-1, 0, 0),
    (0, 1, 0),
    (0, -1, 0),
    (0, 0, 1),
    (0, 0, -1),
    (1, 1, 0),
    (-1, -1, 0),
    (1, -1, 0),
    (-1, 1, 0),
    (1, 0, 1),
    (-1, 0, -1),
    (1, 0, -1),
    (-1, 0, 1),
    (0, 1, 1),
    (0, -1, -1),
    (0, 1, -1),
    (0, -1, 1),
]
OPPOSITE = [0, 2, 1, 4, 3, 6, 5, 8, 7, 10, 9, 12, 11, 14, 13, 16, 15, 18, 17]
LATTICE_WEIGHTS = [1.0 / 3.0] + [1.0 / 18.0] * 6 + [1.0 / 36.0] * 12
UREF = 0.08
NU_BASE = 0.004
Q = 19
DEPTH = 4
ROWS = 8
COLS = 128
FAR = 1 << 20
SIDES = [(dy, dx) for dy in (-1, 0, 1) for dx in (-1, 0, 1)]

LAYER = [("f", i) for i in range(Q)] + [("e", 0)] + [("g", i) for i in range(Q)]
BACK = [("a", i) for i in range(Q)] + [("d", 0)]
FIELDS = [(name, i) for name in "ptg" for i in range(Q)] + [("e", 0)]


def crossing_items(axes, back):
    down = [i for i in range(Q) if all(VEL[i][a] == -1 for a in axes)]
    if back:
        return [("a", i) for i in down]
    up = [i for i in range(Q) if all(VEL[i][a] == 1 for a in axes)]
    return [(name, i) for i in down for name in "pt"] + [("g", i) for i in up]


def face_plan(back):
    near = BACK if back else LAYER
    vertical = [(item, 0) for item in near] + [(item, 1) for item in crossing_items([2], back)]
    spanwise = [(item, z, 0) for item in near for z in range(DEPTH)]
    spanwise += [(item, z, 1) for item in crossing_items([1], back) for z in range(DEPTH)]
    corner = [(item, 0, 0) for item in near]
    corner += [(item, 0, 1) for item in crossing_items([1], back)]
    corner += [(item, 1, 0) for item in crossing_items([2], back)]
    corner += [(item, 1, 1) for item in crossing_items([1, 2], back)]
    return vertical, spanwise, corner


def places(keys):
    return {key: at for at, key in enumerate(keys)}


def tiles_of(keys):
    return -(-len(keys) // ROWS)


PLANS = {back: face_plan(back) for back in (False, True)}
PLACES = {back: [places(keys) for keys in PLANS[back]] for back in (False, True)}


def strips(back):
    return -(-len(BACK if back else LAYER) * DEPTH * 2 // COLS)


def face_shapes(back):
    vertical, spanwise, corner = PLANS[back]
    return [
        (len(vertical) + strips(back), ROWS, COLS),
        (tiles_of(spanwise) + 1, ROWS, COLS),
        (tiles_of(corner) + 1, ROWS, COLS),
    ]


def signed(terms):
    total = None
    for factor, value in terms:
        if factor == 0:
            continue
        piece = value if factor == 1 else (-value if factor == -1 else factor * value)
        total = piece if total is None else total + piece
    return total


def along(idx, vec):
    return signed([(VEL[idx][axis], vec[axis]) for axis in range(3)])


def flow(pops):
    rho = signed([(1, p) for p in pops])
    inverse = 1.0 / rho
    vel = [signed([(VEL[i][axis], pops[i]) for i in range(Q)]) * inverse for axis in range(3)]
    return rho, vel


def shapes(vel):
    base = 1.0 - 1.5 * (vel[0] * vel[0] + vel[1] * vel[1] + vel[2] * vel[2])
    out = [base] + [None] * (Q - 1)
    for i in range(1, Q, 2):
        cu = along(i, vel)
        even = base + 4.5 * cu * cu
        out[i] = even + 3.0 * cu
        out[i + 1] = even - 3.0 * cu
    return out


def departures(pops):
    rho, vel = flow(pops)
    shape = shapes(vel)
    return [LATTICE_WEIGHTS[i] * rho * shape[i] - pops[i] for i in range(Q)]


def collide_adjoint(pops, omega, cot):
    rho, vel = flow(pops)
    shape = shapes(vel)
    weighted = [LATTICE_WEIGHTS[i] * cot[i] for i in range(Q)]
    level = signed([(1, weighted[i] * shape[i]) for i in range(Q)])
    mass = signed([(1, w) for w in weighted])
    first = [signed([(VEL[i][axis], weighted[i]) for i in range(Q)]) for axis in range(3)]

    def second(a, b):
        return signed([(VEL[i][a] * VEL[i][b], weighted[i]) for i in range(Q)])

    pair = {(a, b): second(a, b) for a in range(3) for b in range(a, 3)}
    slope = []
    for a in range(3):
        mixed = signed([(1, pair[min(a, b), max(a, b)] * vel[b]) for b in range(3)])
        slope.append(3.0 * first[a] + 9.0 * mixed - 3.0 * mass * vel[a])
    base = omega * (level - (slope[0] * vel[0] + slope[1] * vel[1] + slope[2] * vel[2]))
    tilt = [omega * s for s in slope]
    keep = 1.0 - omega
    adjoint = []
    for i in range(Q):
        part = along(i, tilt)
        adjoint.append(keep * cot[i] + (base if part is None else base + part))
    away = [LATTICE_WEIGHTS[i] * rho * shape[i] - pops[i] for i in range(Q)]
    grad = signed([(1, cot[i] * away[i]) for i in range(Q)])
    return adjoint, grad, away


def relaxation(smag, eddy):
    return 1.0 / (0.5 + 3.0 * (NU_BASE + smag * eddy))


def row_ids():
    return lax.broadcasted_iota(jnp.int32, (ROWS, COLS), 0)


def lane_ids():
    return lax.broadcasted_iota(jnp.int32, (ROWS, COLS), 1)


def turn(tile, amount, axis):
    size = tile.shape[axis]
    if isinstance(amount, int):
        amount %= size
        return tile if amount == 0 else pltpu.roll(tile, amount, axis)
    return pltpu.roll(tile, lax.rem(amount + size, size), axis)


def pack_columns(out_ref, planes, start):
    lanes = lane_ids()
    per = COLS // 2
    for strip in range(-(-len(planes) // per)):
        total = None
        for j, plane in enumerate(planes[strip * per : (strip + 1) * per]):
            moved = turn(plane(), 2 * j - start, 1)
            total = moved if total is None else jnp.where(lanes >= 2 * j, moved, total)
        out_ref[:, strip * COLS : (strip + 1) * COLS] = total


def pack_rows(pieces):
    rows = row_ids()
    total = None
    for j, (piece, row) in enumerate(pieces):
        moved = turn(piece, j - row, 0)
        total = moved if total is None else jnp.where(rows >= j, moved, total)
    return total


def pack_planes(back, plane, x_ref, z_ref):
    vertical = PLANS[back][0]
    for at, (item, layer) in enumerate(vertical):
        z_ref[at] = plane(item, DEPTH - 1 - layer if back else layer)
    for v in range(strips(back)):
        z_ref[len(vertical) + v] = x_ref[:, v * COLS : (v + 1) * COLS]


def pack_border(keys, plane, row_at, x_ref, out_ref):
    columns = [x_ref[:, v * COLS : (v + 1) * COLS] for v in range(x_ref.shape[1] // COLS)]
    for at in range(0, len(keys), ROWS):
        out_ref[at // ROWS] = pack_rows(
            [(plane(item, z), row_at[r]) for item, z, r in keys[at : at + ROWS]]
        )
    out_ref[tiles_of(keys)] = pack_rows([(tile, row_at[r]) for tile in columns for r in (0, 1)])


def fetch_kernel(
    state_ref, seed_ref, eddy_ref, state_out, seed_out, eddy_out, columns_ref, sems
):
    copies = [
        pltpu.make_async_copy(src, dst, sems.at[k])
        for k, (src, dst) in enumerate(
            ((state_ref, state_out), (eddy_ref, eddy_out), (seed_ref, seed_out))
        )
    ]
    for copy in copies:
        copy.start()
    for copy in copies:
        copy.wait()
    planes = (
        [functools.partial(lambda i, z: state_out[i, z], i, z) for i in range(Q) for z in range(DEPTH)]
        + [functools.partial(lambda z: eddy_out[z], z) for z in range(DEPTH)]
        + [functools.partial(lambda i, z: seed_out[i, z], i, z) for i in range(Q) for z in range(DEPTH)]
    )
    pack_columns(columns_ref, planes, 0)


def collide_fields(smag, pops, eddy):
    omega = relaxation(smag, eddy)
    away = departures(pops)
    heat = omega * omega * eddy
    post = [pops[i] + omega * away[i] for i in range(Q)]
    return post, [heat * away[i] for i in range(Q)]


def first_kernel(
    total_y, total_x, place_ref, smag_ref, state_ref, eddy_ref, near_ref, post_ref, tang_ref, high_ref, own_ref
):
    smag = smag_ref[0]
    for z in range(DEPTH):
        post, tang = collide_fields(smag, [state_ref[i, z] for i in range(Q)], eddy_ref[z])
        for i in range(Q):
            post_ref[i, z] = post[i]
            tang_ref[i, z] = tang[i]
    rows, lanes = row_ids(), lane_ids()
    start_y, start_x = place_ref[1], place_ref[2]

    @functools.cache
    def cut(row, col):
        left, right = near_ref[row : row + ROWS, :COLS], near_ref[row : row + ROWS, COLS:]
        if col == 0:
            return left
        return jnp.where(lanes < COLS - col, turn(left, -col, 1), turn(right, -col, 1))

    for k, first in enumerate((1, 0)):
        for side, (dy, dx) in enumerate(SIDES):
            high = cut(first + 1 + dy, first + 1 + dx)
            own = cut(first + 1, first + 1)
            if dy:
                y = start_y + first + min(dy, 0) + rows
                wall = (y == -1) | (y == total_y - 1)
                high, own = jnp.where(wall, FAR, high), jnp.where(wall, FAR, own)
            if dx:
                x = start_x + first + min(dx, 0) + lanes
                wall = (x == -1) | (x == total_x - 1)
                high, own = jnp.where(wall, FAR, high), jnp.where(wall, FAR, own)
            high_ref[k, side] = turn(turn(high, first, 0), first, 1)
            own_ref[k, side] = turn(turn(own, first, 0), first, 1)


def up_plane(state_ref, seed_ref, eddy_ref, post_ref, tang_ref):
    fields = {"f": state_ref, "g": seed_ref, "p": post_ref, "t": tang_ref}

    def plane(item, z):
        name, i = item
        return eddy_ref[z] if name == "e" else fields[name][i, z]

    return plane


def up_faces_kernel(
    state_ref, seed_ref, eddy_ref, post_ref, tang_ref, x_ref, z_ref, y_ref, yz_ref
):
    plane = up_plane(state_ref, seed_ref, eddy_ref, post_ref, tang_ref)
    pack_planes(False, plane, x_ref, z_ref)
    pack_border(PLANS[False][1], plane, (0, 1), x_ref, y_ref)
    pack_border(PLANS[False][2], plane, (0, 1), x_ref, yz_ref)


def back_rows_kernel(back_ref, x_ref, y_ref):
    def plane(item, z):
        return back_ref[BACK.index(item), z]

    pack_border(PLANS[True][1], plane, (0, ROWS - 1), x_ref, y_ref)


def back_planes_kernel(back_ref, x_ref, y_ref, z_ref):
    pack_planes(True, lambda item, z: back_ref[BACK.index(item), z], x_ref, z_ref)
    vertical, _, corner = PLANS[True]
    y_at = PLACES[True][1]
    first = len(vertical) + strips(True)
    for at in range(0, len(corner), ROWS):
        spots = [y_at[item, DEPTH - 1 - layer, r] for item, layer, r in corner[at : at + ROWS]]
        z_ref[first + at // ROWS] = pack_rows([(y_ref[k // ROWS], k % ROWS) for k in spots])
    z_ref[first + tiles_of(corner)] = y_ref[tiles_of(y_at)]


def level_of(start_z, total_z, plane):
    level = start_z + plane
    return lax.rem(level + total_z, total_z)


def wall_between(start_z, total_z, plane, step):
    upper = start_z + plane + (1 if step > 0 else 0)
    return (upper == total_z) | (upper == 0)


def masks_at(high_ref, own_ref, frame, start_z, total_z, plane):
    solid, way = {}, {}
    here = level_of(start_z, total_z, plane)
    for i in range(Q):
        dx, dy, dz = VEL[i]
        side = SIDES.index((dy, dx))
        there, mine = here, here
        if dz:
            wall = wall_between(start_z, total_z, plane, dz)
            there = jnp.where(wall, -1, level_of(start_z, total_z, plane + dz))
            mine = jnp.where(wall, -1, here)
        solid[VEL[i]] = there < high_ref[frame, side]
        way[VEL[i]] = mine >= own_ref[frame, side]
    return solid, way


def drag_links(solid, way, scale):
    fluid = way[VEL[0]]
    return {
        i: jnp.where(fluid & solid[VEL[i]], 2.0 * scale * VEL[i][0], 0.0)
        for i in range(Q)
        if VEL[i][0] != 0
    }


def pushed(i, own, target, solid, way, links):
    value = jnp.where(way[VEL[i]], target, 0.0) + jnp.where(solid[VEL[i]], own, 0.0)
    return value + links[i] if i in links else value


def middle_kernel(
    total_z,
    scale,
    sens_scale,
    place_ref,
    smag_ref,
    post_ref,
    tang_ref,
    seed_ref,
    eddy_ref,
    x_ref,
    y_ref,
    z_ref,
    yz_ref,
    high_ref,
    own_ref,
    back_ref,
    columns_ref,
    sums_ref,
    main,
    y_tiles,
    x_tiles,
):
    smag = smag_ref[0]
    start_z = place_ref[0]
    rows, lanes = row_ids(), lane_ids()
    z_at, y_at, yz_at = PLACES[False]
    per = COLS // (2 * DEPTH)
    pops_items = [("f", i) for i in range(Q)]

    def collided(tile):
        post, tang = collide_fields(smag, [tile(item) for item in pops_items], tile(("e", 0)))
        out = {("p", i): post[i] for i in range(Q)}
        out.update({("t", i): tang[i] for i in range(Q)})
        out.update({item: tile(item) for item in LAYER if item[0] in "eg"})
        return out

    above = collided(lambda item: z_ref[z_at[item, 0]])

    def copy_planes(z, carry):
        for ref, first in ((post_ref, 0), (tang_ref, Q), (seed_ref, 2 * Q)):
            for i in range(Q):
                main[first + i, z] = ref[i, z]
        main[3 * Q, z] = eddy_ref[z]
        return carry

    lax.fori_loop(0, DEPTH, copy_planes, 0)
    for at, item in enumerate(FIELDS):
        main[at, DEPTH] = above[item]
        if (item, 1) in z_at:
            main[at, DEPTH + 1] = z_ref[z_at[item, 1]]

    def y_piece(key, row):
        at = y_at[key]
        return turn(y_ref[at // ROWS], row - at % ROWS, 0)

    def yz_piece(key, row):
        at = yz_at[key]
        return turn(yz_ref[at // ROWS], row - at % ROWS, 0)

    y_near = collided(lambda item: y_piece((item, 0, 0), 0))
    y_above = collided(lambda item: yz_piece((item, 0, 0), 0))

    for at, item in enumerate(FIELDS):
        tile = y_near[item]
        if (item, 0, 1) in y_at:
            tile = jnp.where(rows < DEPTH, tile, y_piece((item, 0, 1), DEPTH))
        y_tiles[at, 0] = tile
        tile = y_above[item]
        for z, r in ((1, 0), (0, 1), (1, 1)):
            if (item, z, r) in yz_at:
                row = DEPTH * r + z
                tile = jnp.where(rows == row, yz_piece((item, z, r), row), tile)
        y_tiles[at, 1] = tile

    n_strips = strips(False)
    yx_tiles = [turn(y_ref[tiles_of(y_at)], -2 * v, 0) for v in range(n_strips)]
    yzx_tiles = [turn(yz_ref[tiles_of(yz_at)], -2 * v, 0) for v in range(n_strips)]

    def column_tile(item):
        v, at = divmod(LAYER.index(item), per)
        at *= 2 * DEPTH
        near = turn(x_ref[:, v * COLS : (v + 1) * COLS], -at, 1)
        high = turn(z_ref[len(z_at) + v], 8 - at, 1)
        near_rows = turn(yx_tiles[v], 16 - at, 1)
        high_rows = turn(yzx_tiles[v], 24 - at, 1)
        return jnp.where(
            lanes < 16,
            jnp.where(lanes < 8, near, high),
            jnp.where(lanes < 24, near_rows, high_rows),
        )

    sides = collided(column_tile)
    for at, item in enumerate(FIELDS):
        x_tiles[at] = sides[item]

    def viewer(plane_of):
        @functools.cache
        def view(item, dz, dy, dx):
            at, plane = FIELDS.index(item), plane_of[dz]
            tile = main[at, plane]
            if dx >= 0:
                tile = jnp.where(lanes <= dx, turn(x_tiles[at], -2 * plane, 1), tile)
            if dy >= 0:
                k = plane // DEPTH
                z = plane - k * DEPTH
                low = turn(y_tiles[at, k], -z, 0)
                if dy == 1:
                    low = jnp.where(rows == 0, low, turn(y_tiles[at, k], 1 - DEPTH - z, 0))
                if dx >= 0:
                    low = jnp.where(lanes <= dx, turn(x_tiles[at], -2 * plane - 16, 1), low)
                tile = jnp.where(rows <= dy, low, tile)
            return turn(turn(tile, -dx, 1), -dy, 0)

        return view

    def step(z, carry):
        drag, sens = carry
        plane = z + 1
        view = viewer({dz: plane + dz for dz in (-1, 0, 1)})
        solid, way = masks_at(high_ref, own_ref, 0, start_z, total_z, plane)
        links = drag_links(solid, way, scale)

        def pulled(name, i):
            dx, dy, dz = VEL[i]
            away = view((name, i), -dz, -dy, -dx)
            if i == 0:
                return away
            return jnp.where(solid[-dx, -dy, -dz], view((name, OPPOSITE[i]), 0, 0, 0), away)

        f_one = [pulled("p", i) for i in range(Q)]
        cot = []
        for i in range(Q):
            dx, dy, dz = VEL[i]
            own = view(("g", OPPOSITE[i]), 0, 0, 0)
            cot.append(pushed(i, own, view(("g", i), dz, dy, dx), solid, way, links))
        eddy = view(("e", 0), 0, 0, 0)
        omega = relaxation(smag, eddy)
        adjoint, grad, away = collide_adjoint(f_one, omega, cot)
        for i in range(Q):
            back_ref[i, z] = adjoint[i]
        back_ref[Q, z] = grad
        for i in links:
            drag = drag + links[i] * (view(("p", i), 0, 0, 0) + f_one[i] + omega * away[i])
            sens = sens + links[i] * view(("t", i), 0, 0, 0)
        sens = sens + omega * omega * eddy * grad
        for i in range(Q):
            sens = sens + adjoint[i] * pulled("t", i)
        return drag, sens

    zero = jnp.zeros((ROWS, COLS), jnp.float32)
    drag, sens = lax.fori_loop(0, DEPTH, step, (zero, zero))
    sums_ref[...] = jnp.where(
        lax.broadcasted_iota(jnp.int32, sums_ref.shape, 1) == 0,
        jnp.sum(drag),
        jnp.sum(sens) * sens_scale,
    )
    planes = [
        functools.partial(lambda c, z: back_ref[c, z], c, z)
        for c in range(len(BACK))
        for z in range(DEPTH)
    ]
    pack_columns(columns_ref, planes, COLS - 1)


def last_kernel(
    total_z,
    scale,
    place_ref,
    smag_ref,
    state_ref,
    eddy_ref,
    back_ref,
    x_ref,
    y_ref,
    z_ref,
    high_ref,
    own_ref,
    out_ref,
    grad_ref,
    main,
    low_rows,
    strip_tiles,
):
    smag = smag_ref[0]
    start_z = place_ref[0]
    rows, lanes = row_ids(), lane_ids()
    z_at, y_at, yz_at = PLACES[True]
    yz_ref = z_ref.at[pl.ds(len(z_at) + strips(True), tiles_of(yz_at) + 1)]
    per = COLS // 2 // DEPTH

    def copy_planes(z, carry):
        for at in range(len(BACK)):
            main[at, z + 2] = back_ref[at, z]
        return carry

    lax.fori_loop(0, DEPTH, copy_planes, 0)
    for at, item in enumerate(BACK):
        for plane in range(-1, DEPTH + 1):
            if plane >= 1:
                places_of, ref, layer = y_at, y_ref, plane - 1
            else:
                places_of, ref, layer = yz_at, yz_ref, -plane
                if (item, layer) in z_at:
                    main[at, plane + 1] = z_ref[z_at[item, layer]]
            low = None
            for r, row in ((0, 0), (1, ROWS - 1)):
                if (item, layer, r) in places_of:
                    k = places_of[item, layer, r]
                    piece = turn(ref[k // ROWS], row - k % ROWS, 0)
                    low = piece if low is None else jnp.where(rows == 0, low, piece)
            if low is not None:
                low_rows[at, plane + 1] = low
    for v in range(strips(True)):
        strip_tiles[0, v] = x_ref[:, v * COLS : (v + 1) * COLS]
        strip_tiles[1, v] = z_ref[len(z_at) + v]
        for k, tile in ((2, y_ref[tiles_of(y_at)]), (3, yz_ref[tiles_of(yz_at)])):
            first = turn(tile, -2 * v, 0)
            strip_tiles[k, v] = jnp.where(rows == 0, first, turn(first, -2, 0))

    def step(z, carry):
        @functools.cache
        def view(item, dz, dy, dx):
            at, plane = BACK.index(item), z + dz
            lower = jnp.where(plane >= 1, 0, 1)
            layer = lax.rem(plane + DEPTH - 1, DEPTH)
            shift = -2 * (DEPTH * (at % per) + layer) - 1
            keep = (lanes == 0) if dx == 0 else (lanes == 0) | (lanes == COLS - 1)

            def with_columns(tile, kind):
                if dx > 0:
                    return tile
                return jnp.where(keep, turn(strip_tiles[kind + lower, at // per], shift, 1), tile)

            tile = with_columns(main[at, plane + 1], 0)
            if dy <= 0:
                low = with_columns(low_rows[at, plane + 1], 2)
                edge = (rows == 0) if dy == 0 else (rows == 0) | (rows == ROWS - 1)
                tile = jnp.where(edge, low, tile)
            return turn(turn(tile, -dx, 1), -dy, 0)

        solid, way = masks_at(high_ref, own_ref, 1, start_z, total_z, z)
        links = drag_links(solid, way, scale)
        cot = []
        for i in range(Q):
            dx, dy, dz = VEL[i]
            own = view(("a", OPPOSITE[i]), 0, 0, 0)
            cot.append(pushed(i, own, view(("a", i), dz, dy, dx), solid, way, links))
        omega = relaxation(smag, eddy_ref[z])
        adjoint, grad, _ = collide_adjoint([state_ref[i, z] for i in range(Q)], omega, cot)
        for i in range(Q):
            out_ref[i, z] = adjoint[i]
        grad_ref[z] = -3.0 * omega * omega * (grad + view(("d", 0), 0, 0, 0))
        return carry

    lax.fori_loop(0, DEPTH, step, 0)


def plus_one(axis):
    count = lax.axis_size(axis)
    return [(i, (i + 1) % count) for i in range(count)]


def minus_one(axis):
    return [(target, source) for source, target in plus_one(axis)]


def pair_pairs(first, second):
    count = lax.axis_size("gz")
    return [(a * count + b, c * count + d) for a, c in first for b, d in second]


def heights_near(heights):
    padded = jnp.pad(heights, ((1, 2), (1, 2)), mode="wrap")
    start = (lax.axis_index("gy") * ROWS, lax.axis_index("gx") * COLS)
    near = lax.dynamic_slice(padded, start, (ROWS + 3, COLS + 3))
    return jnp.pad(near, ((0, ROWS - 3), (0, COLS - 3)))


def call(kernel, outs, operands, scalars=0, far=False, scratch=(), flops=0):
    def kind(k):
        if k < scalars:
            return pltpu.SMEM
        return pltpu.HBM if far else pltpu.VMEM

    outs = [out if isinstance(out[-1], type) else (out, jnp.float32) for out in outs]
    return pl.pallas_call(
        kernel,
        out_shape=[jax.ShapeDtypeStruct(*out) for out in outs],
        in_specs=[pl.BlockSpec(memory_space=kind(k)) for k in range(len(operands))],
        out_specs=[pl.BlockSpec(memory_space=pltpu.VMEM)] * len(outs),
        scratch_shapes=list(scratch),
        compiler_params=pltpu.CompilerParams(vmem_limit_bytes=32 << 20),
        cost_estimate=pl.CostEstimate(flops=flops, bytes_accessed=1 << 20, transcendentals=0),
    )(*operands)


def exchange_faces(messages, step):
    vertical, spanwise, corner = messages
    vertical = lax.ppermute(vertical, "gz", step("gz"))
    spanwise = lax.ppermute(spanwise, "gy", step("gy"))
    corner = lax.ppermute(corner, ("gy", "gz"), pair_pairs(step("gy"), step("gz")))
    return vertical, spanwise, corner


def on_device(state, adjoint_seed, eddy_rate, smag_coeff, heights):
    total_x = COLS * lax.axis_size("gx")
    total_y = ROWS * lax.axis_size("gy")
    total_z = DEPTH * lax.axis_size("gz")
    scale = 1.0 / (2.0 * UREF * total_x * total_y)
    sens_scale = -3.0 / math.sqrt(total_x * total_y * total_z)
    tile = (ROWS, COLS)
    place = jnp.stack(
        [
            lax.axis_index("gz") * DEPTH,
            lax.axis_index("gy") * ROWS,
            lax.axis_index("gx") * COLS,
        ]
    ).astype(jnp.int32)
    smag = smag_coeff.reshape(1)
    block = state.shape
    layer = eddy_rate.shape

    state, seed, eddy, columns = call(
        fetch_kernel,
        [block, block, layer, (ROWS, strips(False) * COLS)],
        (state, adjoint_seed, eddy_rate),
        far=True,
        scratch=[pltpu.SemaphoreType.DMA((3,))],
    )
    columns = lax.ppermute(columns, "gx", minus_one("gx"))
    beside = ((2, len(SIDES), ROWS, COLS), jnp.int32)
    post, tang, high, own = call(
        functools.partial(first_kernel, total_y, total_x),
        [block, block, beside, beside],
        (place, smag, state, eddy, heights_near(heights)),
        scalars=2,
        flops=8_000_000,
    )
    messages = call(
        up_faces_kernel, face_shapes(False), (state, seed, eddy, post, tang, columns)
    )
    vertical, spanwise, corner = exchange_faces(messages, minus_one)
    n_first = lax.axis_size("gy") * lax.axis_size("gz")
    back, back_columns, sums = call(
        functools.partial(middle_kernel, total_z, scale, sens_scale),
        [(len(BACK), *layer), (ROWS, strips(True) * COLS), (n_first, COLS)],
        (place, smag, post, tang, seed, eddy, columns, spanwise, vertical, corner, high, own),
        scalars=2,
        scratch=[
            pltpu.VMEM(shape, jnp.float32)
            for shape in (
                (len(FIELDS), DEPTH + 2, ROWS, COLS),
                (len(FIELDS), 2, ROWS, COLS),
                (len(FIELDS), ROWS, COLS),
            )
        ],
        flops=20_000_000,
    )
    back_columns = lax.ppermute(back_columns, "gx", plus_one("gx"))
    sums = lax.all_to_all(sums, ("gy", "gz"), split_axis=0, concat_axis=0, tiled=True)
    shape_z, shape_y, shape_yz = face_shapes(True)
    (spanwise,) = call(back_rows_kernel, [shape_y], (back, back_columns))
    spanwise = lax.ppermute(spanwise, "gy", plus_one("gy"))
    (vertical,) = call(
        back_planes_kernel,
        [(shape_z[0] + shape_yz[0], *tile)],
        (back, back_columns, spanwise),
    )
    vertical, sums = lax.optimization_barrier((vertical, sums))
    vertical = lax.ppermute(vertical, "gz", plus_one("gz"))
    sums = jnp.broadcast_to(jnp.sum(sums, 0, keepdims=True), (lax.axis_size("gx"), COLS))
    sums = lax.all_to_all(sums, "gx", split_axis=0, concat_axis=0, tiled=True)
    adjoint_state, gradient = call(
        functools.partial(last_kernel, total_z, scale),
        [block, layer],
        (place, smag, state, eddy, back, back_columns, spanwise, vertical, high, own),
        scalars=2,
        scratch=[
            pltpu.VMEM(shape, jnp.float32)
            for shape in (
                (len(BACK), DEPTH + 2, ROWS, COLS),
                (len(BACK), DEPTH + 2, ROWS, COLS),
                (4, strips(True), ROWS, COLS),
            )
        ],
        flops=20_000_000,
    )
    gradient, sums = lax.optimization_barrier((gradient, sums))
    return adjoint_state, gradient, jnp.sum(sums[:, :2], 0)


def solution(mesh):
    return jax.shard_map(
        on_device,
        mesh=mesh,
        in_specs=(
            P(None, "gz", "gy", "gx"),
            P(None, "gz", "gy", "gx"),
            P("gz", "gy", "gx"),
            P(),
            P(),
        ),
        out_specs=(P(None, "gz", "gy", "gx"), P("gz", "gy", "gx"), P()),
        check_vma=False,
    )
```

time: 84.7 us -> 72.3 us (0.85)
  starting transfers between devices: 53.8 us -> 44.3 us
  Pallas kernels: 4.76 us -> 6.95 us
  waiting for transfers between devices: 16.3 us -> 14.2 us
  other arithmetic: 2 us -> 0.65 us
  local copies, waits for them, and re-layouts: 5.43 us -> 4.25 us
    all_to_all x2, starting transfers between devices: 20.2 us -> 15.3 us  [the longest x1 9.49 us: on_device(): lax.all_to_all(sums, ('gy', 'gz'), split_axis=0, concat_axis=0, tiled=True)]
    ppermute x1, starting transfers between devices: 5.96 us -> 2.95 us  [on_device(): back_columns = lax.ppermute(back_columns, 'gx', plus_one('gx'))]
    ppermute x6 -> x5, waiting for transfers between devices: 11.6 us -> 8.81 us  [the longest x1 5.02 us: exchange_faces(): lax.ppermute(corner, ('gy', 'gz'), pair_pairs(step('gy'), step('gz')))]
    pallas_call x5 -> x7, Pallas kernels: 4.76 us -> 6.95 us  [call(): pl.pallas_call(kernel, out_shape=[jax.ShapeDtypeStruct(*out) for out in o...]
    ppermute x6 -> x5, starting transfers between devices: 20.7 us -> 19.2 us  [the longest x1 9.37 us: exchange_faces(): spanwise = lax.ppermute(spanwise, 'gy', step('gy'))]
    unnamed x20 -> x0, other arithmetic: 1.27 us -> none
    unnamed x16 -> x8, local copies, waits for them, and re-layouts: 3.24 us -> 2.65 us
  transfers between devices with their start and end apart: 10 -> 9, of which waited for: 6 -> 4; matrix products, arithmetic and copies ran while one was open for 4% -> 1% of each run, Pallas kernels for 0% -> 4%
where the time goes in v3:
time: 72.3 us; the launch traced here: 71.8 us
  starting transfers between devices  44.3 us (61%)
  waiting for transfers between devices  14.2 us (20%)
  Pallas kernels  6.95 us (10%)
  local copies, waits for them, and re-layouts  4.25 us (6%)
  between operations  1.44 us (2%)
    all_to_all x1, starting transfers between devices, on_device(): lax.all_to_all(sums, ('gy', 'gz'), split_axis=0, concat_axis=0, tiled=True)  9.49 us
    ppermute x1, starting transfers between devices, exchange_faces(): spanwise = lax.ppermute(spanwise, 'gy', step('gy'))  9.37 us
    pallas_call x7, Pallas kernels, call(): pl.pallas_call(kernel, out_shape=[jax.ShapeDtypeStruct(*out) for out in o...  6.95 us
    ppermute x1, starting transfers between devices, on_device(): columns = lax.ppermute(columns, 'gx', minus_one('gx'))  6.89 us
    all_to_all x1, starting transfers between devices, on_device(): sums = lax.all_to_all(sums, 'gx', split_axis=0, concat_axis=0, tiled=True)  5.78 us
    ppermute x1, waiting for transfers between devices, exchange_faces(): lax.ppermute(corner, ('gy', 'gz'), pair_pairs(step('gy'), step('gz')))  5.02 us
    ppermute x1, starting transfers between devices, on_device(): spanwise = lax.ppermute(spanwise, 'gy', plus_one('gy'))  3.83 us
    ppermute x1, waiting for transfers between devices, on_device(): spanwise = lax.ppermute(spanwise, 'gy', plus_one('gy'))  3.77 us
  transfers between devices with their start and end apart: 9, of which 4 were waited for; matrix products, arithmetic and copies ran while one was open for 1% of the time, Pallas kernels for 4%

profile of v3, /device:TPU:1, one launch (start us, length us, event | category | flops | bytes accessed | tf_op | source)
XLA Modules:
  0.0 71.8 jit_solution(2258268202916748084)
XLA Ops:
  0.6 0.0 copy-start
  0.6 1.0 %copy-done = f32[19,4,8,128]{3,2,1,0:T(8,128)S(1)} copy-done((f32[19,4,8,128]{3,2,1,0:T(8,128)S(1)}, f32[19,4,8,128]{3,2,1,0:T(8,128)}, u32[]{:S(2)}) %copy-start) | copy-done | bytes 311320
  1.6 0.0 copy-start.1
  1.6 1.0 %copy-done.1 = f32[19,4,8,128]{3,2,1,0:T(8,128)S(1)} copy-done((f32[19,4,8,128]{3,2,1,0:T(8,128)S(1)}, f32[19,4,8,128]{3,2,1,0:T(8,128)}, u32[]{:S(2)}) %copy-start.1) | copy-done | bytes 311320
  2.6 0.0 copy-start.2
  2.6 0.7 copy-done.2
  3.3 0.0 copy-start.3
  3.3 0.4 shard_map.76
  3.7 6.9 %collective-permute-start = (f32[8,384]{1,0:T(8,128)S(1)}, f32[8,384]{1,0:T(8,128)S(1)}, u32[]{:S(2)}, u32[]{:S(2)}) collective-permute-start(f32[8,384]{1,0:T(8,128)S(1)} %get-tuple-element.28), channel_id=1, source_target_pairs={{64,0},{128,64},{192,128},{256,192},{320,256},{384,320},{448,384},... | collective-permute-start | bytes 36872 | tf_op jit(solution)/shard_map/ppermute | solution.py:687
  10.6 0.0 copy-done.3
  10.6 0.0 slice-start
  10.7 0.7 slice-done
  11.4 0.1 pad_add_fusion.1.place_ref
  11.4 0.1 slice.24
  12.2 0.1 concatenate.9
  12.3 0.1 dynamic_slice.3
  12.4 0.8 %shard_map.77 = (f32[19,4,8,128]{3,2,1,0:T(8,128)S(1)}, f32[19,4,8,128]{3,2,1,0:T(8,128)S(1)}, s32[2,9,8,128]{3,2,1,0:T(8,128)S(1)}, s32[2,9,8,128]{3,2,1,0:T(8,128)S(1)}) custom-call(s32[3]{0:T(128)S(1)} %pad_add_fusion.1.place_ref, f32[1]{0:T(128)} %bitcast.9.smag_ref, f32[19,4,8,128]{3,2,1,0:T(8,128)S(1)} %get-tuple-element.23.state_ref, ...), custom_call_target="tpu_custom_call" | custom-call | flops 8000000 | bytes 1048576 | tf_op jit(solution)/shard_map/pallas_call | solution.py:643
  13.2 0.0 collective-permute-done.x_ref
  13.2 0.1 shard_map.78
  13.3 1.9 %collective-permute-start.2 = (f32[57,8,128]{2,1,0:T(8,128)S(1)}, f32[57,8,128]{2,1,0:T(8,128)S(1)}, u32[]{:S(2)}, u32[]{:S(2)}) collective-permute-start(f32[57,8,128]{2,1,0:T(8,128)S(1)} %get-tuple-element.30), channel_id=1, source_target_pairs={{1,0},{2,1},{3,2},{4,3},{5,4},{6,5},{7,6},{8,7},{9,8},{10,9},{11,1... | collective-permute-start | bytes 700424 | tf_op jit(solution)/shard_map/ppermute | solution.py:656
  15.2 9.4 %collective-permute-start.1 = (f32[28,8,128]{2,1,0:T(8,128)S(1)}, f32[28,8,128]{2,1,0:T(8,128)S(1)}, u32[]{:S(2)}, u32[]{:S(2)}) collective-permute-start(f32[28,8,128]{2,1,0:T(8,128)S(1)} %get-tuple-element.29), channel_id=1, source_target_pairs={{16,0},{32,16},{48,32},{0,48},{17,1},{33,17},{49,33},{1,49},{18,2}... | collective-permute-start | bytes 344072 | tf_op jit(solution)/shard_map/ppermute | solution.py:657
  24.6 1.9 %collective-permute-start.3 = (f32[10,8,128]{2,1,0:T(8,128)S(1)}, f32[10,8,128]{2,1,0:T(8,128)S(1)}, u32[]{:S(2)}, u32[]{:S(2)}) collective-permute-start(f32[10,8,128]{2,1,0:T(8,128)S(1)} %get-tuple-element.31), channel_id=1, source_target_pairs={{17,0},{18,1},{19,2},{20,3},{21,4},{22,5},{23,6},{24,7},{25,8},{26... | collective-permute-start | bytes 122888 | tf_op jit(solution)/shard_map/ppermute | solution.py:658
  26.5 5.0 %collective-permute-done.3.yz_ref = f32[10,8,128]{2,1,0:T(8,128)S(1)} collective-permute-done((f32[10,8,128]{2,1,0:T(8,128)S(1)}, f32[10,8,128]{2,1,0:T(8,128)S(1)}, u32[]{:S(2)}, u32[]{:S(2)}) %collective-permute-start.3) | collective-permute-done | bytes 40992 | tf_op jit(solution)/shard_map/ppermute | solution.py:658
  31.6 0.0 collective-permute-done.1.y_ref
  31.6 0.0 collective-permute-done.2.z_ref
  31.6 3.4 %shard_map.79 = (f32[20,4,8,128]{3,2,1,0:T(8,128)S(1)}, f32[8,256]{1,0:T(8,128)S(1)}, f32[64,128]{1,0:T(8,128)}) custom-call(s32[3]{0:T(128)S(1)} %pad_add_fusion.1.place_ref, f32[1]{0:T(128)} %bitcast.10.smag_ref, f32[19,4,8,128]{3,2,1,0:T(8,128)S(1)} %get-tuple-element.25.post_ref, f32[19,4,8,128]{3,2,1,0:T(8,128)S(1)} %get-tuple-element.26.tang_ref, ...), custom_call_target="tpu_custom_call" | custom-call | flops 20000000 | bytes 1048576 | tf_op jit(solution)/shard_map/pallas_call | solution.py:643
  35.0 2.9 %collective-permute-start.4 = (f32[8,256]{1,0:T(8,128)S(1)}, f32[8,256]{1,0:T(8,128)S(1)}, u32[]{:S(2)}, u32[]{:S(2)}) collective-permute-start(f32[8,256]{1,0:T(8,128)S(1)} %get-tuple-element.35), channel_id=1, source_target_pairs={{0,64},{64,128},{128,192},{192,256},{256,320},{320,384},{384,448},... | collective-permute-start | bytes 24584 | tf_op jit(solution)/shard_map/ppermute | solution.py:716
  37.9 9.5 %all-to-all-start = ((f32[64,1,128]{2,1,0:T(1,128)}), f32[64,1,128]{2,1,0:T(1,128)S(1)}, u32[]{:S(2)}, u32[]{:S(2)}) async-start(f32[64,1,128]{2,1,0:T(1,128)} %bitcast.5), calls=%async_computation | async-start | bytes 65536 | tf_op jit(solution)/shard_map/all_to_all | solution.py:717
  47.4 0.0 collective-permute-done.4.x_ref
  47.5 3.8 %collective-permute-start.5 = (f32[14,8,128]{2,1,0:T(8,128)S(1)}, f32[14,8,128]{2,1,0:T(8,128)S(1)}, u32[]{:S(2)}, u32[]{:S(2)}) collective-permute-start(f32[14,8,128]{2,1,0:T(8,128)S(1)} %shard_map.80), channel_id=1, source_target_pairs={{0,16},{16,32},{32,48},{48,0},{1,17},{17,33},{33,49},{49,1},{2,18}... | collective-permute-start | bytes 172040 | tf_op jit(solution)/shard_map/ppermute | solution.py:720
  51.3 3.8 %collective-permute-done.5.y_ref = f32[14,8,128]{2,1,0:T(8,128)S(1)} collective-permute-done((f32[14,8,128]{2,1,0:T(8,128)S(1)}, f32[14,8,128]{2,1,0:T(8,128)S(1)}, u32[]{:S(2)}, u32[]{:S(2)}) %collective-permute-start.5) | collective-permute-done | bytes 57376 | tf_op jit(solution)/shard_map/ppermute | solution.py:720
  55.1 3.0 %all-to-all-done = f32[64,1,128]{2,1,0:T(1,128)S(1)} async-done(((f32[64,1,128]{2,1,0:T(1,128)}), f32[64,1,128]{2,1,0:T(1,128)S(1)}, u32[]{:S(2)}, u32[]{:S(2)}) %all-to-all-start) | async-done | bytes 32800 | tf_op jit(solution)/shard_map/all_to_all | solution.py:717
  58.1 2.2 %collective-permute-start.6 = (f32[32,8,128]{2,1,0:T(8,128)S(1)}, f32[32,8,128]{2,1,0:T(8,128)S(1)}, u32[]{:S(2)}, u32[]{:S(2)}) collective-permute-start(f32[32,8,128]{2,1,0:T(8,128)S(1)} %shard_map.81), channel_id=1, source_target_pairs={{0,1},{1,2},{2,3},{3,4},{4,5},{5,6},{6,7},{7,8},{8,9},{9,10},{10,1... | collective-permute-start | bytes 393224 | tf_op jit(solution)/shard_map/ppermute | solution.py:727
  60.3 0.6 broadcast_in_dim.2
  60.9 5.8 %all-to-all-start.1 = ((f32[8,1,128]{2,1,0:T(1,128)}), f32[8,1,128]{2,1,0:T(1,128)S(1)}, u32[]{:S(2)}, u32[]{:S(2)}) async-start(f32[8,1,128]{2,1,0:T(1,128)} %broadcast_in_dim.2), calls=%async_computation.1 | async-start | bytes 8192 | tf_op jit(solution)/shard_map/all_to_all | solution.py:729
  66.7 0.0 collective-permute-done.6.z_ref
  66.7 2.2 %shard_map.82 = (f32[19,4,8,128]{3,2,1,0:T(8,128)}, f32[4,8,128]{2,1,0:T(8,128)}) custom-call(s32[3]{0:T(128)S(1)} %pad_add_fusion.1.place_ref, f32[1]{0:T(128)} %bitcast.11.smag_ref, f32[19,4,8,128]{3,2,1,0:T(8,128)S(1)} %get-tuple-element.23.state_ref, f32[4,8,128]{2,1,0:T(8,128)S(1)} %get-tuple-element.24.eddy_ref, ...), custom_call_target="tpu_custom_call" | custom-call | flops 20000000 | bytes 1048576 | tf_op jit(solution)/shard_map/pallas_call | solution.py:643
  68.9 2.4 %all-to-all-done.1 = f32[8,1,128]{2,1,0:T(1,128)S(1)} async-done(((f32[8,1,128]{2,1,0:T(1,128)}), f32[8,1,128]{2,1,0:T(1,128)S(1)}, u32[]{:S(2)}, u32[]{:S(2)}) %all-to-all-start.1) | async-done | bytes 4128 | tf_op jit(solution)/shard_map/all_to_all | solution.py:729
  71.3 0.5 slice_reduce_fusion
  (7 shorter events, 0.1 us)
Async XLA Ops:
  0.6 1.0 %copy-start = (f32[19,4,8,128]{3,2,1,0:T(8,128)S(1)}, f32[19,4,8,128]{3,2,1,0:T(8,128)}, u32[]{:S(2)}) copy-start(f32[19,4,8,128]{3,2,1,0:T(8,128)} %state_ref.1) | copy-start | bytes 933892
  1.6 1.0 %copy-start.1 = (f32[19,4,8,128]{3,2,1,0:T(8,128)S(1)}, f32[19,4,8,128]{3,2,1,0:T(8,128)}, u32[]{:S(2)}) copy-start(f32[19,4,8,128]{3,2,1,0:T(8,128)} %seed_ref.1) | copy-start | bytes 933892
  2.6 0.7 copy-start.2
  3.3 7.3 %copy-start.3 = (s32[32,1024]{1,0:T(8,128)S(1)}, s32[32,1024]{1,0:T(8,128)}, u32[]{:S(2)}) copy-start(s32[32,1024]{1,0:T(8,128)} %param.9) | copy-start | bytes 393220
  3.7 9.5 %collective-permute-start = (f32[8,384]{1,0:T(8,128)S(1)}, f32[8,384]{1,0:T(8,128)S(1)}, u32[]{:S(2)}, u32[]{:S(2)}) collective-permute-start(f32[8,384]{1,0:T(8,128)S(1)} %get-tuple-element.28), channel_id=1, source_target_pairs={{64,0},{128,64},{192,128},{256,192},{320,256},{384,320},{448,384},... | collective-permute-start | bytes 36872 | tf_op jit(solution)/shard_map/ppermute | solution.py:687
  10.6 0.7 slice-start
  13.3 18.3 %collective-permute-start.2 = (f32[57,8,128]{2,1,0:T(8,128)S(1)}, f32[57,8,128]{2,1,0:T(8,128)S(1)}, u32[]{:S(2)}, u32[]{:S(2)}) collective-permute-start(f32[57,8,128]{2,1,0:T(8,128)S(1)} %get-tuple-element.30), channel_id=1, source_target_pairs={{1,0},{2,1},{3,2},{4,3},{5,4},{6,5},{7,6},{8,7},{9,8},{10,9},{11,1... | collective-permute-start | bytes 700424 | tf_op jit(solution)/shard_map/ppermute | solution.py:656
  15.2 16.3 %collective-permute-start.1 = (f32[28,8,128]{2,1,0:T(8,128)S(1)}, f32[28,8,128]{2,1,0:T(8,128)S(1)}, u32[]{:S(2)}, u32[]{:S(2)}) collective-permute-start(f32[28,8,128]{2,1,0:T(8,128)S(1)} %get-tuple-element.29), channel_id=1, source_target_pairs={{16,0},{32,16},{48,32},{0,48},{17,1},{33,17},{49,33},{1,49},{18,2}... | collective-permute-start | bytes 344072 | tf_op jit(solution)/shard_map/ppermute | solution.py:657
  24.6 6.9 %collective-permute-start.3 = (f32[10,8,128]{2,1,0:T(8,128)S(1)}, f32[10,8,128]{2,1,0:T(8,128)S(1)}, u32[]{:S(2)}, u32[]{:S(2)}) collective-permute-start(f32[10,8,128]{2,1,0:T(8,128)S(1)} %get-tuple-element.31), channel_id=1, source_target_pairs={{17,0},{18,1},{19,2},{20,3},{21,4},{22,5},{23,6},{24,7},{25,8},{26... | collective-permute-start | bytes 122888 | tf_op jit(solution)/shard_map/ppermute | solution.py:658
  35.0 12.5 %collective-permute-start.4 = (f32[8,256]{1,0:T(8,128)S(1)}, f32[8,256]{1,0:T(8,128)S(1)}, u32[]{:S(2)}, u32[]{:S(2)}) collective-permute-start(f32[8,256]{1,0:T(8,128)S(1)} %get-tuple-element.35), channel_id=1, source_target_pairs={{0,64},{64,128},{128,192},{192,256},{256,320},{320,384},{384,448},... | collective-permute-start | bytes 24584 | tf_op jit(solution)/shard_map/ppermute | solution.py:716
  37.9 20.2 %all-to-all-start = ((f32[64,1,128]{2,1,0:T(1,128)}), f32[64,1,128]{2,1,0:T(1,128)S(1)}, u32[]{:S(2)}, u32[]{:S(2)}) async-start(f32[64,1,128]{2,1,0:T(1,128)} %bitcast.5), calls=%async_computation | async-start | bytes 65536 | tf_op jit(solution)/shard_map/all_to_all | solution.py:717
  47.5 7.6 %collective-permute-start.5 = (f32[14,8,128]{2,1,0:T(8,128)S(1)}, f32[14,8,128]{2,1,0:T(8,128)S(1)}, u32[]{:S(2)}, u32[]{:S(2)}) collective-permute-start(f32[14,8,128]{2,1,0:T(8,128)S(1)} %shard_map.80), channel_id=1, source_target_pairs={{0,16},{16,32},{32,48},{48,0},{1,17},{17,33},{33,49},{49,1},{2,18}... | collective-permute-start | bytes 172040 | tf_op jit(solution)/shard_map/ppermute | solution.py:720
  58.1 8.6 %collective-permute-start.6 = (f32[32,8,128]{2,1,0:T(8,128)S(1)}, f32[32,8,128]{2,1,0:T(8,128)S(1)}, u32[]{:S(2)}, u32[]{:S(2)}) collective-permute-start(f32[32,8,128]{2,1,0:T(8,128)S(1)} %shard_map.81), channel_id=1, source_target_pairs={{0,1},{1,2},{2,3},{3,4},{4,5},{5,6},{6,7},{7,8},{8,9},{9,10},{10,1... | collective-permute-start | bytes 393224 | tf_op jit(solution)/shard_map/ppermute | solution.py:727
  60.9 10.3 %all-to-all-start.1 = ((f32[8,1,128]{2,1,0:T(1,128)}), f32[8,1,128]{2,1,0:T(1,128)S(1)}, u32[]{:S(2)}, u32[]{:S(2)}) async-start(f32[8,1,128]{2,1,0:T(1,128)} %broadcast_in_dim.2), calls=%async_computation.1 | async-start | bytes 8192 | tf_op jit(solution)/shard_map/all_to_all | solution.py:729

commit v4 on v3

--- a/solution.py
+++ b/solution.py
@@ -40,7 +40,7 @@
 FAR = 1 << 20
 SIDES = [(dy, dx) for dy in (-1, 0, 1) for dx in (-1, 0, 1)]
 
-LAYER = [("f", i) for i in range(Q)] + [("e", 0)] + [("g", i) for i in range(Q)]
+LAYER = [("f", i) for i in range(Q)] + [("g", i) for i in range(Q)] + [("e", 0)]
 BACK = [("a", i) for i in range(Q)] + [("d", 0)]
 FIELDS = [(name, i) for name in "ptg" for i in range(Q)] + [("e", 0)]
 
@@ -69,10 +69,19 @@
     return {key: at for at, key in enumerate(keys)}
 
 
+def early_and_rest():
+    vertical = PLANS[False][0]
+    return [k for k in vertical if is_early(k)], [k for k in vertical if not is_early(k)]
+
+
 def tiles_of(keys):
     return -(-len(keys) // ROWS)
 
 
+def is_early(key):
+    return key[0][0] in "fg"
+
+
 PLANS = {back: face_plan(back) for back in (False, True)}
 PLACES = {back: [places(keys) for keys in PLANS[back]] for back in (False, True)}
 
@@ -83,8 +92,9 @@
 
 def face_shapes(back):
     vertical, spanwise, corner = PLANS[back]
+    planes = vertical if back else early_and_rest()[1]
     return [
-        (len(vertical) + strips(back), ROWS, COLS),
+        (len(planes) + strips(back), ROWS, COLS),
         (tiles_of(spanwise) + 1, ROWS, COLS),
         (tiles_of(corner) + 1, ROWS, COLS),
     ]
@@ -196,12 +206,11 @@
     return total
 
 
-def pack_planes(back, plane, x_ref, z_ref):
-    vertical = PLANS[back][0]
-    for at, (item, layer) in enumerate(vertical):
-        z_ref[at] = plane(item, DEPTH - 1 - layer if back else layer)
-    for v in range(strips(back)):
-        z_ref[len(vertical) + v] = x_ref[:, v * COLS : (v + 1) * COLS]
+def pack_planes(keys, plane, x_ref, z_ref):
+    for at, (item, layer) in enumerate(keys):
+        z_ref[at] = plane(item, layer)
+    for v in range(x_ref.shape[1] // COLS):
+        z_ref[len(keys) + v] = x_ref[:, v * COLS : (v + 1) * COLS]
 
 
 def pack_border(keys, plane, row_at, x_ref, out_ref):
@@ -214,24 +223,38 @@
 
 
 def fetch_kernel(
-    state_ref, seed_ref, eddy_ref, state_out, seed_out, eddy_out, columns_ref, sems
+    state_ref, seed_ref, state_out, seed_out, columns_ref, early_ref, sems
 ):
     copies = [
         pltpu.make_async_copy(src, dst, sems.at[k])
-        for k, (src, dst) in enumerate(
-            ((state_ref, state_out), (eddy_ref, eddy_out), (seed_ref, seed_out))
-        )
+        for k, (src, dst) in enumerate(((state_ref, state_out), (seed_ref, seed_out)))
     ]
     for copy in copies:
         copy.start()
     for copy in copies:
         copy.wait()
-    planes = (
-        [functools.partial(lambda i, z: state_out[i, z], i, z) for i in range(Q) for z in range(DEPTH)]
-        + [functools.partial(lambda z: eddy_out[z], z) for z in range(DEPTH)]
-        + [functools.partial(lambda i, z: seed_out[i, z], i, z) for i in range(Q) for z in range(DEPTH)]
-    )
+
+    def plane(item, z):
+        name, i = item
+        return {"f": state_out, "g": seed_out}[name][i, z]
+
+    planes = [
+        functools.partial(plane, item, z) for item in LAYER if item[0] != "e" for z in range(DEPTH)
+    ]
     pack_columns(columns_ref, planes, 0)
+    for at, (item, layer) in enumerate(early_and_rest()[0]):
+        early_ref[at] = plane(item, layer)
+
+
+def eddy_columns_kernel(columns_ref, eddy_ref, out_ref):
+    lanes = lane_ids()
+    first = 2 * DEPTH * (len(LAYER) - 1)
+    out_ref[:, :] = columns_ref[:, :]
+    for z in range(DEPTH):
+        strip, lane = divmod(first + 2 * z, COLS)
+        spot = slice(strip * COLS, (strip + 1) * COLS)
+        moved = turn(eddy_ref[z], lane, 1)
+        out_ref[:, spot] = jnp.where(lanes // 2 == lane // 2, moved, out_ref[:, spot])
 
 
 def collide_fields(smag, pops, eddy):
@@ -243,7 +266,7 @@
 
 
 def first_kernel(
-    total_y, total_x, place_ref, smag_ref, state_ref, eddy_ref, near_ref, post_ref, tang_ref, high_ref, own_ref
+    total_y, total_x, place_ref, smag_ref, state_ref, eddy_ref, heights_ref, post_ref, tang_ref, high_ref, own_ref
 ):
     smag = smag_ref[0]
     for z in range(DEPTH):
@@ -254,27 +277,53 @@
     rows, lanes = row_ids(), lane_ids()
     start_y, start_x = place_ref[1], place_ref[2]
 
-    @functools.cache
-    def cut(row, col):
-        left, right = near_ref[row : row + ROWS, :COLS], near_ref[row : row + ROWS, COLS:]
-        if col == 0:
-            return left
-        return jnp.where(lanes < COLS - col, turn(left, -col, 1), turn(right, -col, 1))
+    def block(dy, dx):
+        y = lax.rem(start_y + dy * ROWS + total_y, total_y)
+        x = lax.rem(start_x + dx * COLS + total_x, total_x)
+        return heights_ref[
+            pl.ds(pl.multiple_of(y, ROWS), ROWS), pl.ds(pl.multiple_of(x, COLS), COLS)
+        ]
+
+    blocks = {side: block(*side) for side in SIDES}
+
+    def beside(lower, own, upper, ids, axis, size, first, step):
+        if first:
+            if step < 0:
+                return turn(own, 1, axis)
+            return turn(jnp.where(ids <= step, upper, own), -step, axis)
+        if step == 0:
+            return own
+        edge = jnp.where(ids == size - 1, lower, own) if step < 0 else jnp.where(ids == 0, upper, own)
+        return turn(edge, -step, axis)
 
     for k, first in enumerate((1, 0)):
+        across = {
+            (dy, dx): beside(
+                *(blocks[dy, n] for n in (-1, 0, 1)), lanes, 1, COLS, first, dx
+            )
+            for dy in (-1, 0, 1)
+            for dx in (-1, 0, 1)
+        }
+        near = {
+            (dy, dx): beside(
+                *(across[n, dx] for n in (-1, 0, 1)), rows, 0, ROWS, first, dy
+            )
+            for dy, dx in SIDES
+        }
+        y = start_y + jnp.where((rows == 0) & (first == 1), ROWS, rows)
+        x = start_x + jnp.where((lanes == 0) & (first == 1), COLS, lanes)
         for side, (dy, dx) in enumerate(SIDES):
-            high = cut(first + 1 + dy, first + 1 + dx)
-            own = cut(first + 1, first + 1)
+            high, own = near[dy, dx], near[0, 0]
             if dy:
-                y = start_y + first + min(dy, 0) + rows
-                wall = (y == -1) | (y == total_y - 1)
+                low_y = y + min(dy, 0)
+                wall = (low_y == -1) | (low_y == total_y - 1)
                 high, own = jnp.where(wall, FAR, high), jnp.where(wall, FAR, own)
             if dx:
-                x = start_x + first + min(dx, 0) + lanes
-                wall = (x == -1) | (x == total_x - 1)
+                low_x = x + min(dx, 0)
+                wall = (low_x == -1) | (low_x == total_x - 1)
                 high, own = jnp.where(wall, FAR, high), jnp.where(wall, FAR, own)
-            high_ref[k, side] = turn(turn(high, first, 0), first, 1)
-            own_ref[k, side] = turn(turn(own, first, 0), first, 1)
+            high_ref[k, side] = high
+            own_ref[k, side] = own
 
 
 def up_plane(state_ref, seed_ref, eddy_ref, post_ref, tang_ref):
@@ -291,7 +340,7 @@
     state_ref, seed_ref, eddy_ref, post_ref, tang_ref, x_ref, z_ref, y_ref, yz_ref
 ):
     plane = up_plane(state_ref, seed_ref, eddy_ref, post_ref, tang_ref)
-    pack_planes(False, plane, x_ref, z_ref)
+    pack_planes(early_and_rest()[1], plane, x_ref, z_ref)
     pack_border(PLANS[False][1], plane, (0, 1), x_ref, y_ref)
     pack_border(PLANS[False][2], plane, (0, 1), x_ref, yz_ref)
 
@@ -304,8 +353,12 @@
 
 
 def back_planes_kernel(back_ref, x_ref, y_ref, z_ref):
-    pack_planes(True, lambda item, z: back_ref[BACK.index(item), z], x_ref, z_ref)
     vertical, _, corner = PLANS[True]
+
+    def plane(item, layer):
+        return back_ref[BACK.index(item), DEPTH - 1 - layer]
+
+    pack_planes(vertical, plane, x_ref, z_ref)
     y_at = PLACES[True][1]
     first = len(vertical) + strips(True)
     for at in range(0, len(corner), ROWS):
@@ -366,6 +419,7 @@
     eddy_ref,
     x_ref,
     y_ref,
+    early_ref,
     z_ref,
     yz_ref,
     high_ref,
@@ -380,7 +434,8 @@
     smag = smag_ref[0]
     start_z = place_ref[0]
     rows, lanes = row_ids(), lane_ids()
-    z_at, y_at, yz_at = PLACES[False]
+    _, y_at, yz_at = PLACES[False]
+    early_at, rest_at = (places(keys) for keys in early_and_rest())
     per = COLS // (2 * DEPTH)
     pops_items = [("f", i) for i in range(Q)]
 
@@ -391,7 +446,9 @@
         out.update({item: tile(item) for item in LAYER if item[0] in "eg"})
         return out
 
-    above = collided(lambda item: z_ref[z_at[item, 0]])
+    above = collided(
+        lambda item: (z_ref[rest_at[item, 0]] if item[0] == "e" else early_ref[early_at[item, 0]])
+    )
 
     def copy_planes(z, carry):
         for ref, first in ((post_ref, 0), (tang_ref, Q), (seed_ref, 2 * Q)):
@@ -403,8 +460,10 @@
     lax.fori_loop(0, DEPTH, copy_planes, 0)
     for at, item in enumerate(FIELDS):
         main[at, DEPTH] = above[item]
-        if (item, 1) in z_at:
-            main[at, DEPTH + 1] = z_ref[z_at[item, 1]]
+        if (item, 1) in early_at:
+            main[at, DEPTH + 1] = early_ref[early_at[item, 1]]
+        if (item, 1) in rest_at:
+            main[at, DEPTH + 1] = z_ref[rest_at[item, 1]]
 
     def y_piece(key, row):
         at = y_at[key]
@@ -437,7 +496,7 @@
         v, at = divmod(LAYER.index(item), per)
         at *= 2 * DEPTH
         near = turn(x_ref[:, v * COLS : (v + 1) * COLS], -at, 1)
-        high = turn(z_ref[len(z_at) + v], 8 - at, 1)
+        high = turn(z_ref[len(rest_at) + v], 8 - at, 1)
         near_rows = turn(yx_tiles[v], 16 - at, 1)
         high_rows = turn(yzx_tiles[v], 24 - at, 1)
         return jnp.where(
@@ -626,14 +685,7 @@
     return [(a * count + b, c * count + d) for a, c in first for b, d in second]
 
 
-def heights_near(heights):
-    padded = jnp.pad(heights, ((1, 2), (1, 2)), mode="wrap")
-    start = (lax.axis_index("gy") * ROWS, lax.axis_index("gx") * COLS)
-    near = lax.dynamic_slice(padded, start, (ROWS + 3, COLS + 3))
-    return jnp.pad(near, ((0, ROWS - 3), (0, COLS - 3)))
-
-
-def call(kernel, outs, operands, scalars=0, far=False, scratch=(), flops=0):
+def call(kernel, outs, operands, scalars=0, far=False, scratch=(), flops=0, limit=32 << 20):
     def kind(k):
         if k < scalars:
             return pltpu.SMEM
@@ -646,7 +698,7 @@
         in_specs=[pl.BlockSpec(memory_space=kind(k)) for k in range(len(operands))],
         out_specs=[pl.BlockSpec(memory_space=pltpu.VMEM)] * len(outs),
         scratch_shapes=list(scratch),
-        compiler_params=pltpu.CompilerParams(vmem_limit_bytes=32 << 20),
+        compiler_params=pltpu.CompilerParams(vmem_limit_bytes=limit),
         cost_estimate=pl.CostEstimate(flops=flops, bytes_accessed=1 << 20, transcendentals=0),
     )(*operands)
 
@@ -677,19 +729,28 @@
     block = state.shape
     layer = eddy_rate.shape
 
-    state, seed, eddy, columns = call(
+    eddy = eddy_rate
+    state, seed, columns, early = call(
         fetch_kernel,
-        [block, block, layer, (ROWS, strips(False) * COLS)],
-        (state, adjoint_seed, eddy_rate),
+        [
+            block,
+            block,
+            (ROWS, strips(False) * COLS),
+            (len(early_and_rest()[0]), *tile),
+        ],
+        (state, adjoint_seed),
         far=True,
-        scratch=[pltpu.SemaphoreType.DMA((3,))],
+        scratch=[pltpu.SemaphoreType.DMA((2,))],
+        limit=(52 << 20) + (960 << 10),
     )
+    (columns,) = call(eddy_columns_kernel, [columns.shape], (columns, eddy))
     columns = lax.ppermute(columns, "gx", minus_one("gx"))
+    early = lax.ppermute(early, "gz", minus_one("gz"))
     beside = ((2, len(SIDES), ROWS, COLS), jnp.int32)
     post, tang, high, own = call(
         functools.partial(first_kernel, total_y, total_x),
         [block, block, beside, beside],
-        (place, smag, state, eddy, heights_near(heights)),
+        (place, smag, state, eddy, heights),
         scalars=2,
         flops=8_000_000,
     )
@@ -701,7 +762,7 @@
     back, back_columns, sums = call(
         functools.partial(middle_kernel, total_z, scale, sens_scale),
         [(len(BACK), *layer), (ROWS, strips(True) * COLS), (n_first, COLS)],
-        (place, smag, post, tang, seed, eddy, columns, spanwise, vertical, corner, high, own),
+        (place, smag, post, tang, seed, eddy, columns, spanwise, early, vertical, corner, high, own),
         scalars=2,
         scratch=[
             pltpu.VMEM(shape, jnp.float32)

time: 72.3 us -> 68.4 us (0.946)
  local copies, waits for them, and re-layouts: 4.25 us -> 0.6 us
  waiting for transfers between devices: 14.2 us -> 13 us
  Pallas kernels: 6.95 us -> 7.87 us
    all_to_all x1, starting transfers between devices: 9.49 us -> 6.11 us  [on_device(): lax.all_to_all(sums, ('gy', 'gz'), split_axis=0, concat_axis=0, tiled=True)]
    unnamed x8 -> x4, local copies, waits for them, and re-layouts: 2.65 us -> 0.01 us
    ppermute x0 -> x1, starting transfers between devices: none -> 1.91 us  [on_device(): early = lax.ppermute(early, 'gz', minus_one('gz'))]
    ppermute x1, starting transfers between devices: 1.92 us -> 2.97 us  [exchange_faces(): lax.ppermute(corner, ('gy', 'gz'), pair_pairs(step('gy'), step('gz')))]
    ppermute x1, waiting for transfers between devices: 5.02 us -> 4 us  [exchange_faces(): lax.ppermute(corner, ('gy', 'gz'), pair_pairs(step('gy'), step('gz')))]
    pallas_call x7 -> x8, Pallas kernels: 6.95 us -> 7.87 us  [call(): pl.pallas_call(kernel, out_shape=[jax.ShapeDtypeStruct(*out) for out in o...]
    slice x5 -> x0, local copies, waits for them, and re-layouts: 0.77 us -> none  [heights_near(): padded = jnp.pad(heights, ((1, 2), (1, 2)), mode='wrap')]
  transfers between devices with their start and end apart: 9 -> 10, of which waited for: 4 -> 4; matrix products, arithmetic and copies ran while one was open for 1% -> 1% of each run, Pallas kernels for 4% -> 4%
where the time goes in v4:
time: 68.4 us; the launch traced here: 68.1 us
  starting transfers between devices  44.5 us (65%)
  waiting for transfers between devices  13 us (19%)
  Pallas kernels  7.87 us (12%)
  between operations  1.44 us (2%)
    ppermute x1, starting transfers between devices, exchange_faces(): spanwise = lax.ppermute(spanwise, 'gy', step('gy'))  9.37 us
    pallas_call x8, Pallas kernels, call(): pl.pallas_call(kernel, out_shape=[jax.ShapeDtypeStruct(*out) for out in o...  7.87 us
    ppermute x1, starting transfers between devices, on_device(): columns = lax.ppermute(columns, 'gx', minus_one('gx'))  6.88 us
    all_to_all x1, starting transfers between devices, on_device(): lax.all_to_all(sums, ('gy', 'gz'), split_axis=0, concat_axis=0, tiled=True)  6.11 us
    all_to_all x1, starting transfers between devices, on_device(): sums = lax.all_to_all(sums, 'gx', split_axis=0, concat_axis=0, tiled=True)  5.97 us
    ppermute x1, waiting for transfers between devices, exchange_faces(): lax.ppermute(corner, ('gy', 'gz'), pair_pairs(step('gy'), step('gz')))  4 us
    ppermute x1, starting transfers between devices, on_device(): spanwise = lax.ppermute(spanwise, 'gy', plus_one('gy'))  3.83 us
    ppermute x1, waiting for transfers between devices, on_device(): spanwise = lax.ppermute(spanwise, 'gy', plus_one('gy'))  3.58 us
  transfers between devices with their start and end apart: 10, of which 4 were waited for; matrix products, arithmetic and copies ran while one was open for 1% of the time, Pallas kernels for 4%

profile of v4, /device:TPU:1, one launch (start us, length us, event | category | flops | bytes accessed | tf_op | source)
XLA Modules:
  0.0 68.1 jit_solution(1686348691958463954)
XLA Ops:
  0.6 0.0 copy-start
  0.6 0.0 copy-start.1
  0.7 1.3 %shard_map.76 = (f32[19,4,8,128]{3,2,1,0:T(8,128)S(1)}, f32[19,4,8,128]{3,2,1,0:T(8,128)S(1)}, f32[8,384]{1,0:T(8,128)S(1)}, f32[43,8,128]{2,1,0:T(8,128)S(1)}) custom-call(f32[19,4,8,128]{3,2,1,0:T(8,128)} %state_ref.1, f32[19,4,8,128]{3,2,1,0:T(8,128)} %seed_ref.1), custom_call_target="tpu_custom_call" | custom-call | bytes 1048576 | tf_op jit(solution)/shard_map/pallas_call | solution.py:695
  2.0 0.0 copy-done
  2.0 0.1 shard_map.78
  2.1 6.9 %collective-permute-start = (f32[8,384]{1,0:T(8,128)S(1)}, f32[8,384]{1,0:T(8,128)S(1)}, u32[]{:S(2)}, u32[]{:S(2)}) collective-permute-start(f32[8,384]{1,0:T(8,128)S(1)} %shard_map.78), channel_id=1, source_target_pairs={{64,0},{128,64},{192,128},{256,192},{320,256},{384,320},{448,384},... | collective-permute-start | bytes 36872 | tf_op jit(solution)/shard_map/ppermute | solution.py:747
  9.0 1.9 %collective-permute-start.2 = (f32[43,8,128]{2,1,0:T(8,128)S(1)}, f32[43,8,128]{2,1,0:T(8,128)S(1)}, u32[]{:S(2)}, u32[]{:S(2)}) collective-permute-start(f32[43,8,128]{2,1,0:T(8,128)S(1)} %get-tuple-element.29), channel_id=1, source_target_pairs={{1,0},{2,1},{3,2},{4,3},{5,4},{6,5},{7,6},{8,7},{9,8},{10,9},{11,1... | collective-permute-start | bytes 528392 | tf_op jit(solution)/shard_map/ppermute | solution.py:748
  10.9 0.1 pad_add_fusion.place_ref
  11.6 0.0 copy-done.1
  11.6 0.7 %shard_map.77 = (f32[19,4,8,128]{3,2,1,0:T(8,128)S(1)}, f32[19,4,8,128]{3,2,1,0:T(8,128)S(1)}, s32[2,9,8,128]{3,2,1,0:T(8,128)S(1)}, s32[2,9,8,128]{3,2,1,0:T(8,128)S(1)}) custom-call(s32[3]{0:T(128)S(1)} %pad_add_fusion.place_ref, f32[1]{0:T(128)} %bitcast.9.smag_ref, f32[19,4,8,128]{3,2,1,0:T(8,128)S(1)} %get-tuple-element.23.state_ref, ...), custom_call_target="tpu_custom_call" | custom-call | flops 8000000 | bytes 1048576 | tf_op jit(solution)/shard_map/pallas_call | solution.py:695
  12.4 0.0 collective-permute-done.x_ref
  12.4 0.1 shard_map.79
  12.5 9.4 %collective-permute-start.1 = (f32[28,8,128]{2,1,0:T(8,128)S(1)}, f32[28,8,128]{2,1,0:T(8,128)S(1)}, u32[]{:S(2)}, u32[]{:S(2)}) collective-permute-start(f32[28,8,128]{2,1,0:T(8,128)S(1)} %get-tuple-element.28), channel_id=1, source_target_pairs={{16,0},{32,16},{48,32},{0,48},{17,1},{33,17},{49,33},{1,49},{18,2}... | collective-permute-start | bytes 344072 | tf_op jit(solution)/shard_map/ppermute | solution.py:709
  21.8 2.2 %collective-permute-start.3 = (f32[14,8,128]{2,1,0:T(8,128)S(1)}, f32[14,8,128]{2,1,0:T(8,128)S(1)}, u32[]{:S(2)}, u32[]{:S(2)}) collective-permute-start(f32[14,8,128]{2,1,0:T(8,128)S(1)} %get-tuple-element.30), channel_id=1, source_target_pairs={{1,0},{2,1},{3,2},{4,3},{5,4},{6,5},{7,6},{8,7},{9,8},{10,9},{11,1... | collective-permute-start | bytes 172040 | tf_op jit(solution)/shard_map/ppermute | solution.py:708
  24.0 3.0 %collective-permute-start.4 = (f32[10,8,128]{2,1,0:T(8,128)S(1)}, f32[10,8,128]{2,1,0:T(8,128)S(1)}, u32[]{:S(2)}, u32[]{:S(2)}) collective-permute-start(f32[10,8,128]{2,1,0:T(8,128)S(1)} %get-tuple-element.31), channel_id=1, source_target_pairs={{17,0},{18,1},{19,2},{20,3},{21,4},{22,5},{23,6},{24,7},{25,8},{26... | collective-permute-start | bytes 122888 | tf_op jit(solution)/shard_map/ppermute | solution.py:710
  27.0 4.0 %collective-permute-done.4.yz_ref = f32[10,8,128]{2,1,0:T(8,128)S(1)} collective-permute-done((f32[10,8,128]{2,1,0:T(8,128)S(1)}, f32[10,8,128]{2,1,0:T(8,128)S(1)}, u32[]{:S(2)}, u32[]{:S(2)}) %collective-permute-start.4) | collective-permute-done | bytes 40992 | tf_op jit(solution)/shard_map/ppermute | solution.py:710
  31.0 0.0 collective-permute-done.3.z_ref
  31.0 0.0 collective-permute-done.1.y_ref
  31.0 0.0 collective-permute-done.2.early_ref
  31.0 3.4 %shard_map.80 = (f32[20,4,8,128]{3,2,1,0:T(8,128)S(1)}, f32[8,256]{1,0:T(8,128)S(1)}, f32[64,128]{1,0:T(8,128)}) custom-call(s32[3]{0:T(128)S(1)} %pad_add_fusion.place_ref, f32[1]{0:T(128)} %bitcast.10.smag_ref, f32[19,4,8,128]{3,2,1,0:T(8,128)S(1)} %get-tuple-element.24.post_ref, f32[19,4,8,128]{3,2,1,0:T(8,128)S(1)} %get-tuple-element.25.tang_ref, ...), custom_call_target="tpu_custom_call" | custom-call | flops 20000000 | bytes 1048576 | tf_op jit(solution)/shard_map/pallas_call | solution.py:695
  34.4 3.1 %collective-permute-start.5 = (f32[8,256]{1,0:T(8,128)S(1)}, f32[8,256]{1,0:T(8,128)S(1)}, u32[]{:S(2)}, u32[]{:S(2)}) collective-permute-start(f32[8,256]{1,0:T(8,128)S(1)} %get-tuple-element.35), channel_id=1, source_target_pairs={{0,64},{64,128},{128,192},{192,256},{256,320},{320,384},{384,448},... | collective-permute-start | bytes 24584 | tf_op jit(solution)/shard_map/ppermute | solution.py:777
  37.5 6.1 %all-to-all-start = ((f32[64,1,128]{2,1,0:T(1,128)}), f32[64,1,128]{2,1,0:T(1,128)S(1)}, u32[]{:S(2)}, u32[]{:S(2)}) async-start(f32[64,1,128]{2,1,0:T(1,128)} %bitcast.5), calls=%async_computation | async-start | bytes 65536 | tf_op jit(solution)/shard_map/all_to_all | solution.py:778
  43.7 0.0 collective-permute-done.5.x_ref
  43.7 3.8 %collective-permute-start.6 = (f32[14,8,128]{2,1,0:T(8,128)S(1)}, f32[14,8,128]{2,1,0:T(8,128)S(1)}, u32[]{:S(2)}, u32[]{:S(2)}) collective-permute-start(f32[14,8,128]{2,1,0:T(8,128)S(1)} %shard_map.81), channel_id=1, source_target_pairs={{0,16},{16,32},{32,48},{48,0},{1,17},{17,33},{33,49},{49,1},{2,18}... | collective-permute-start | bytes 172040 | tf_op jit(solution)/shard_map/ppermute | solution.py:781
  47.5 3.6 %collective-permute-done.6.y_ref = f32[14,8,128]{2,1,0:T(8,128)S(1)} collective-permute-done((f32[14,8,128]{2,1,0:T(8,128)S(1)}, f32[14,8,128]{2,1,0:T(8,128)S(1)}, u32[]{:S(2)}, u32[]{:S(2)}) %collective-permute-start.6) | collective-permute-done | bytes 57376 | tf_op jit(solution)/shard_map/ppermute | solution.py:781
  51.1 3.2 %all-to-all-done = f32[64,1,128]{2,1,0:T(1,128)S(1)} async-done(((f32[64,1,128]{2,1,0:T(1,128)}), f32[64,1,128]{2,1,0:T(1,128)S(1)}, u32[]{:S(2)}, u32[]{:S(2)}) %all-to-all-start) | async-done | bytes 32800 | tf_op jit(solution)/shard_map/all_to_all | solution.py:778
  54.3 2.2 %collective-permute-start.7 = (f32[32,8,128]{2,1,0:T(8,128)S(1)}, f32[32,8,128]{2,1,0:T(8,128)S(1)}, u32[]{:S(2)}, u32[]{:S(2)}) collective-permute-start(f32[32,8,128]{2,1,0:T(8,128)S(1)} %shard_map.82), channel_id=1, source_target_pairs={{0,1},{1,2},{2,3},{3,4},{4,5},{5,6},{6,7},{7,8},{8,9},{9,10},{10,1... | collective-permute-start | bytes 393224 | tf_op jit(solution)/shard_map/ppermute | solution.py:788
  56.5 0.6 broadcast_in_dim.2
  57.1 6.0 %all-to-all-start.1 = ((f32[8,1,128]{2,1,0:T(1,128)}), f32[8,1,128]{2,1,0:T(1,128)S(1)}, u32[]{:S(2)}, u32[]{:S(2)}) async-start(f32[8,1,128]{2,1,0:T(1,128)} %broadcast_in_dim.2), calls=%async_computation.1 | async-start | bytes 8192 | tf_op jit(solution)/shard_map/all_to_all | solution.py:790
  63.1 0.0 collective-permute-done.7.z_ref
  63.1 2.2 %shard_map.83 = (f32[19,4,8,128]{3,2,1,0:T(8,128)}, f32[4,8,128]{2,1,0:T(8,128)}) custom-call(s32[3]{0:T(128)S(1)} %pad_add_fusion.place_ref, f32[1]{0:T(128)} %bitcast.11.smag_ref, f32[19,4,8,128]{3,2,1,0:T(8,128)S(1)} %get-tuple-element.23.state_ref, f32[4,8,128]{2,1,0:T(8,128)S(1)} %copy-done, f32[20,4,8,128]{3,2,1,0:T(8,128)S(1)} %get-tuple-element.34.back_ref, ...), custom_call_target="tpu_custom_call" | custom-call | flops 20000000 | bytes 1048576 | tf_op jit(solution)/shard_map/pallas_call | solution.py:695
  65.3 2.3 %all-to-all-done.1 = f32[8,1,128]{2,1,0:T(1,128)S(1)} async-done(((f32[8,1,128]{2,1,0:T(1,128)}), f32[8,1,128]{2,1,0:T(1,128)S(1)}, u32[]{:S(2)}, u32[]{:S(2)}) %all-to-all-start.1) | async-done | bytes 4128 | tf_op jit(solution)/shard_map/all_to_all | solution.py:790
  67.5 0.5 slice_reduce_fusion
  (3 shorter events, 0.1 us)
Async XLA Ops:
  0.6 1.4 %copy-start = (f32[4,8,128]{2,1,0:T(8,128)S(1)}, f32[4,8,128]{2,1,0:T(8,128)}, u32[]{:S(2)}) copy-start(f32[4,8,128]{2,1,0:T(8,128)} %eddy_ref.9) | copy-start | bytes 49156
  0.6 11.0 %copy-start.1 = (s32[32,1024]{1,0:T(8,128)S(1)}, s32[32,1024]{1,0:T(8,128)}, u32[]{:S(2)}) copy-start(s32[32,1024]{1,0:T(8,128)} %heights_ref.1) | copy-start | bytes 393220
  2.1 10.3 %collective-permute-start = (f32[8,384]{1,0:T(8,128)S(1)}, f32[8,384]{1,0:T(8,128)S(1)}, u32[]{:S(2)}, u32[]{:S(2)}) collective-permute-start(f32[8,384]{1,0:T(8,128)S(1)} %shard_map.78), channel_id=1, source_target_pairs={{64,0},{128,64},{192,128},{256,192},{320,256},{384,320},{448,384},... | collective-permute-start | bytes 36872 | tf_op jit(solution)/shard_map/ppermute | solution.py:747
  9.0 22.0 %collective-permute-start.2 = (f32[43,8,128]{2,1,0:T(8,128)S(1)}, f32[43,8,128]{2,1,0:T(8,128)S(1)}, u32[]{:S(2)}, u32[]{:S(2)}) collective-permute-start(f32[43,8,128]{2,1,0:T(8,128)S(1)} %get-tuple-element.29), channel_id=1, source_target_pairs={{1,0},{2,1},{3,2},{4,3},{5,4},{6,5},{7,6},{8,7},{9,8},{10,9},{11,1... | collective-permute-start | bytes 528392 | tf_op jit(solution)/shard_map/ppermute | solution.py:748
  12.5 18.5 %collective-permute-start.1 = (f32[28,8,128]{2,1,0:T(8,128)S(1)}, f32[28,8,128]{2,1,0:T(8,128)S(1)}, u32[]{:S(2)}, u32[]{:S(2)}) collective-permute-start(f32[28,8,128]{2,1,0:T(8,128)S(1)} %get-tuple-element.28), channel_id=1, source_target_pairs={{16,0},{32,16},{48,32},{0,48},{17,1},{33,17},{49,33},{1,49},{18,2}... | collective-permute-start | bytes 344072 | tf_op jit(solution)/shard_map/ppermute | solution.py:709
  21.8 9.2 %collective-permute-start.3 = (f32[14,8,128]{2,1,0:T(8,128)S(1)}, f32[14,8,128]{2,1,0:T(8,128)S(1)}, u32[]{:S(2)}, u32[]{:S(2)}) collective-permute-start(f32[14,8,128]{2,1,0:T(8,128)S(1)} %get-tuple-element.30), channel_id=1, source_target_pairs={{1,0},{2,1},{3,2},{4,3},{5,4},{6,5},{7,6},{8,7},{9,8},{10,9},{11,1... | collective-permute-start | bytes 172040 | tf_op jit(solution)/shard_map/ppermute | solution.py:708
  24.0 7.0 %collective-permute-start.4 = (f32[10,8,128]{2,1,0:T(8,128)S(1)}, f32[10,8,128]{2,1,0:T(8,128)S(1)}, u32[]{:S(2)}, u32[]{:S(2)}) collective-permute-start(f32[10,8,128]{2,1,0:T(8,128)S(1)} %get-tuple-element.31), channel_id=1, source_target_pairs={{17,0},{18,1},{19,2},{20,3},{21,4},{22,5},{23,6},{24,7},{25,8},{26... | collective-permute-start | bytes 122888 | tf_op jit(solution)/shard_map/ppermute | solution.py:710
  34.4 9.2 %collective-permute-start.5 = (f32[8,256]{1,0:T(8,128)S(1)}, f32[8,256]{1,0:T(8,128)S(1)}, u32[]{:S(2)}, u32[]{:S(2)}) collective-permute-start(f32[8,256]{1,0:T(8,128)S(1)} %get-tuple-element.35), channel_id=1, source_target_pairs={{0,64},{64,128},{128,192},{192,256},{256,320},{320,384},{384,448},... | collective-permute-start | bytes 24584 | tf_op jit(solution)/shard_map/ppermute | solution.py:777
  37.5 16.8 %all-to-all-start = ((f32[64,1,128]{2,1,0:T(1,128)}), f32[64,1,128]{2,1,0:T(1,128)S(1)}, u32[]{:S(2)}, u32[]{:S(2)}) async-start(f32[64,1,128]{2,1,0:T(1,128)} %bitcast.5), calls=%async_computation | async-start | bytes 65536 | tf_op jit(solution)/shard_map/all_to_all | solution.py:778
  43.7 7.4 %collective-permute-start.6 = (f32[14,8,128]{2,1,0:T(8,128)S(1)}, f32[14,8,128]{2,1,0:T(8,128)S(1)}, u32[]{:S(2)}, u32[]{:S(2)}) collective-permute-start(f32[14,8,128]{2,1,0:T(8,128)S(1)} %shard_map.81), channel_id=1, source_target_pairs={{0,16},{16,32},{32,48},{48,0},{1,17},{17,33},{33,49},{49,1},{2,18}... | collective-permute-start | bytes 172040 | tf_op jit(solution)/shard_map/ppermute | solution.py:781
  54.3 8.8 %collective-permute-start.7 = (f32[32,8,128]{2,1,0:T(8,128)S(1)}, f32[32,8,128]{2,1,0:T(8,128)S(1)}, u32[]{:S(2)}, u32[]{:S(2)}) collective-permute-start(f32[32,8,128]{2,1,0:T(8,128)S(1)} %shard_map.82), channel_id=1, source_target_pairs={{0,1},{1,2},{2,3},{3,4},{4,5},{5,6},{6,7},{7,8},{8,9},{9,10},{10,1... | collective-permute-start | bytes 393224 | tf_op jit(solution)/shard_map/ppermute | solution.py:788
  57.1 10.4 %all-to-all-start.1 = ((f32[8,1,128]{2,1,0:T(1,128)}), f32[8,1,128]{2,1,0:T(1,128)S(1)}, u32[]{:S(2)}, u32[]{:S(2)}) async-start(f32[8,1,128]{2,1,0:T(1,128)} %broadcast_in_dim.2), calls=%async_computation.1 | async-start | bytes 8192 | tf_op jit(solution)/shard_map/all_to_all | solution.py:790

commit v5 on v4

--- a/solution.py
+++ b/solution.py
@@ -266,7 +266,7 @@
 
 
 def first_kernel(
-    total_y, total_x, place_ref, smag_ref, state_ref, eddy_ref, heights_ref, post_ref, tang_ref, high_ref, own_ref
+    total_y, total_x, smag_ref, state_ref, eddy_ref, heights_ref, post_ref, tang_ref, high_ref, own_ref
 ):
     smag = smag_ref[0]
     for z in range(DEPTH):
@@ -275,7 +275,8 @@
             post_ref[i, z] = post[i]
             tang_ref[i, z] = tang[i]
     rows, lanes = row_ids(), lane_ids()
-    start_y, start_x = place_ref[1], place_ref[2]
+    start_y = lax.axis_index("gy") * ROWS
+    start_x = lax.axis_index("gx") * COLS
 
     def block(dy, dx):
         y = lax.rem(start_y + dy * ROWS + total_y, total_y)
@@ -411,7 +412,6 @@
     total_z,
     scale,
     sens_scale,
-    place_ref,
     smag_ref,
     post_ref,
     tang_ref,
@@ -432,7 +432,7 @@
     x_tiles,
 ):
     smag = smag_ref[0]
-    start_z = place_ref[0]
+    start_z = lax.axis_index("gz") * DEPTH
     rows, lanes = row_ids(), lane_ids()
     _, y_at, yz_at = PLACES[False]
     early_at, rest_at = (places(keys) for keys in early_and_rest())
@@ -581,7 +581,6 @@
 def last_kernel(
     total_z,
     scale,
-    place_ref,
     smag_ref,
     state_ref,
     eddy_ref,
@@ -598,7 +597,7 @@
     strip_tiles,
 ):
     smag = smag_ref[0]
-    start_z = place_ref[0]
+    start_z = lax.axis_index("gz") * DEPTH
     rows, lanes = row_ids(), lane_ids()
     z_at, y_at, yz_at = PLACES[True]
     yz_ref = z_ref.at[pl.ds(len(z_at) + strips(True), tiles_of(yz_at) + 1)]
@@ -718,13 +717,6 @@
     scale = 1.0 / (2.0 * UREF * total_x * total_y)
     sens_scale = -3.0 / math.sqrt(total_x * total_y * total_z)
     tile = (ROWS, COLS)
-    place = jnp.stack(
-        [
-            lax.axis_index("gz") * DEPTH,
-            lax.axis_index("gy") * ROWS,
-            lax.axis_index("gx") * COLS,
-        ]
-    ).astype(jnp.int32)
     smag = smag_coeff.reshape(1)
     block = state.shape
     layer = eddy_rate.shape
@@ -744,14 +736,15 @@
         limit=(52 << 20) + (960 << 10),
     )
     (columns,) = call(eddy_columns_kernel, [columns.shape], (columns, eddy))
+    columns, early = lax.optimization_barrier((columns, early))
     columns = lax.ppermute(columns, "gx", minus_one("gx"))
     early = lax.ppermute(early, "gz", minus_one("gz"))
     beside = ((2, len(SIDES), ROWS, COLS), jnp.int32)
     post, tang, high, own = call(
         functools.partial(first_kernel, total_y, total_x),
         [block, block, beside, beside],
-        (place, smag, state, eddy, heights),
-        scalars=2,
+        (smag, state, eddy, heights),
+        scalars=1,
         flops=8_000_000,
     )
     messages = call(
@@ -762,8 +755,8 @@
     back, back_columns, sums = call(
         functools.partial(middle_kernel, total_z, scale, sens_scale),
         [(len(BACK), *layer), (ROWS, strips(True) * COLS), (n_first, COLS)],
-        (place, smag, post, tang, seed, eddy, columns, spanwise, early, vertical, corner, high, own),
-        scalars=2,
+        (smag, post, tang, seed, eddy, columns, spanwise, early, vertical, corner, high, own),
+        scalars=1,
         scratch=[
             pltpu.VMEM(shape, jnp.float32)
             for shape in (
@@ -791,8 +784,8 @@
     adjoint_state, gradient = call(
         functools.partial(last_kernel, total_z, scale),
         [block, layer],
-        (place, smag, state, eddy, back, back_columns, spanwise, vertical, high, own),
-        scalars=2,
+        (smag, state, eddy, back, back_columns, spanwise, vertical, high, own),
+        scalars=1,
         scratch=[
             pltpu.VMEM(shape, jnp.float32)
             for shape in (

time: 68.4 us -> 67.6 us (0.988)
  waiting for transfers between devices: 13 us -> 14.8 us
  Pallas kernels: 7.87 us -> 6.25 us
  starting transfers between devices: 44.5 us -> 43.6 us
    ppermute x1, starting transfers between devices: 1.91 us -> 7.72 us  [on_device(): early = lax.ppermute(early, 'gz', minus_one('gz'))]
    ppermute x1, starting transfers between devices: 6.88 us -> 1.07 us  [on_device(): columns = lax.ppermute(columns, 'gx', minus_one('gx'))]
    pallas_call x8, Pallas kernels: 7.87 us -> 6.25 us  [call(): pl.pallas_call(kernel, out_shape=[jax.ShapeDtypeStruct(*out) for out in o...]
    ppermute x1, waiting for transfers between devices: 0.01 us -> 1.51 us  [on_device(): columns = lax.ppermute(columns, 'gx', minus_one('gx'))]
    all_to_all x1, starting transfers between devices: 5.97 us -> 5 us  [on_device(): sums = lax.all_to_all(sums, 'gx', split_axis=0, concat_axis=0, tiled=True)]
  transfers between devices with their start and end apart: 10 -> 10, of which waited for: 4 -> 5; matrix products, arithmetic and copies ran while one was open for 1% -> 1% of each run, Pallas kernels for 4% -> 3%
where the time goes in v5:
time: 67.6 us; the launch traced here: 67.2 us
  starting transfers between devices  43.6 us (64%)
  waiting for transfers between devices  14.8 us (22%)
  Pallas kernels  6.25 us (9%)
  between operations  1.42 us (2%)
    ppermute x1, starting transfers between devices, exchange_faces(): spanwise = lax.ppermute(spanwise, 'gy', step('gy'))  9.76 us
    ppermute x1, starting transfers between devices, on_device(): early = lax.ppermute(early, 'gz', minus_one('gz'))  7.72 us
    pallas_call x8, Pallas kernels, call(): pl.pallas_call(kernel, out_shape=[jax.ShapeDtypeStruct(*out) for out in o...  6.25 us
    all_to_all x1, starting transfers between devices, on_device(): lax.all_to_all(sums, ('gy', 'gz'), split_axis=0, concat_axis=0, tiled=True)  6 us
    all_to_all x1, starting transfers between devices, on_device(): sums = lax.all_to_all(sums, 'gx', split_axis=0, concat_axis=0, tiled=True)  5 us
    ppermute x1, starting transfers between devices, on_device(): spanwise = lax.ppermute(spanwise, 'gy', plus_one('gy'))  3.83 us
    ppermute x1, waiting for transfers between devices, exchange_faces(): lax.ppermute(corner, ('gy', 'gz'), pair_pairs(step('gy'), step('gz')))  3.71 us
    ppermute x1, waiting for transfers between devices, on_device(): spanwise = lax.ppermute(spanwise, 'gy', plus_one('gy'))  3.59 us
  transfers between devices with their start and end apart: 10, of which 5 were waited for; matrix products, arithmetic and copies ran while one was open for 1% of the time, Pallas kernels for 3%

profile of v5, /device:TPU:1, one launch (start us, length us, event | category | flops | bytes accessed | tf_op | source)
XLA Modules:
  0.0 67.2 jit_solution(15891598687073337995)
XLA Ops:
  0.6 0.0 copy-start
  0.6 0.0 copy-start.1
  0.7 1.3 %shard_map.76 = (f32[19,4,8,128]{3,2,1,0:T(8,128)S(1)}, f32[19,4,8,128]{3,2,1,0:T(8,128)S(1)}, f32[8,384]{1,0:T(8,128)S(1)}, f32[43,8,128]{2,1,0:T(8,128)S(1)}) custom-call(f32[19,4,8,128]{3,2,1,0:T(8,128)} %state_ref.1, f32[19,4,8,128]{3,2,1,0:T(8,128)} %seed_ref.1), custom_call_target="tpu_custom_call" | custom-call | bytes 1048576 | tf_op jit(solution)/shard_map/pallas_call | solution.py:694
  2.0 0.0 copy-done
  2.0 0.1 shard_map.78
  2.1 7.7 %collective-permute-start.2 = (f32[43,8,128]{2,1,0:T(8,128)S(1)}, f32[43,8,128]{2,1,0:T(8,128)S(1)}, u32[]{:S(2)}, u32[]{:S(2)}) collective-permute-start(f32[43,8,128]{2,1,0:T(8,128)S(1)} %get-tuple-element.33), channel_id=1, source_target_pairs={{1,0},{2,1},{3,2},{4,3},{5,4},{6,5},{7,6},{8,7},{9,8},{10,9},{11,1... | collective-permute-start | bytes 528392 | tf_op jit(solution)/shard_map/ppermute | solution.py:741
  9.8 1.1 %collective-permute-start = (f32[8,384]{1,0:T(8,128)S(1)}, f32[8,384]{1,0:T(8,128)S(1)}, u32[]{:S(2)}, u32[]{:S(2)}) collective-permute-start(f32[8,384]{1,0:T(8,128)S(1)} %shard_map.78), channel_id=1, source_target_pairs={{64,0},{128,64},{192,128},{256,192},{320,256},{384,320},{448,384},... | collective-permute-start | bytes 36872 | tf_op jit(solution)/shard_map/ppermute | solution.py:740
  11.5 0.0 copy-done.1
  11.6 0.2 shard_map.77
  11.8 1.5 %collective-permute-done.x_ref = f32[8,384]{1,0:T(8,128)S(1)} collective-permute-done((f32[8,384]{1,0:T(8,128)S(1)}, f32[8,384]{1,0:T(8,128)S(1)}, u32[]{:S(2)}, u32[]{:S(2)}) %collective-permute-start) | collective-permute-done | bytes 12320 | tf_op jit(solution)/shard_map/ppermute | solution.py:740
  13.3 0.1 shard_map.79
  13.3 9.8 %collective-permute-start.1 = (f32[28,8,128]{2,1,0:T(8,128)S(1)}, f32[28,8,128]{2,1,0:T(8,128)S(1)}, u32[]{:S(2)}, u32[]{:S(2)}) collective-permute-start(f32[28,8,128]{2,1,0:T(8,128)S(1)} %get-tuple-element.32), channel_id=1, source_target_pairs={{16,0},{32,16},{48,32},{0,48},{17,1},{33,17},{49,33},{1,49},{18,2}... | collective-permute-start | bytes 344072 | tf_op jit(solution)/shard_map/ppermute | solution.py:708
  23.1 2.2 %collective-permute-start.3 = (f32[14,8,128]{2,1,0:T(8,128)S(1)}, f32[14,8,128]{2,1,0:T(8,128)S(1)}, u32[]{:S(2)}, u32[]{:S(2)}) collective-permute-start(f32[14,8,128]{2,1,0:T(8,128)S(1)} %get-tuple-element.34), channel_id=1, source_target_pairs={{1,0},{2,1},{3,2},{4,3},{5,4},{6,5},{7,6},{8,7},{9,8},{10,9},{11,1... | collective-permute-start | bytes 172040 | tf_op jit(solution)/shard_map/ppermute | solution.py:707
  25.3 3.3 %collective-permute-start.4 = (f32[10,8,128]{2,1,0:T(8,128)S(1)}, f32[10,8,128]{2,1,0:T(8,128)S(1)}, u32[]{:S(2)}, u32[]{:S(2)}) collective-permute-start(f32[10,8,128]{2,1,0:T(8,128)S(1)} %get-tuple-element.35), channel_id=1, source_target_pairs={{17,0},{18,1},{19,2},{20,3},{21,4},{22,5},{23,6},{24,7},{25,8},{26... | collective-permute-start | bytes 122888 | tf_op jit(solution)/shard_map/ppermute | solution.py:709
  28.6 3.7 %collective-permute-done.4.yz_ref = f32[10,8,128]{2,1,0:T(8,128)S(1)} collective-permute-done((f32[10,8,128]{2,1,0:T(8,128)S(1)}, f32[10,8,128]{2,1,0:T(8,128)S(1)}, u32[]{:S(2)}, u32[]{:S(2)}) %collective-permute-start.4) | collective-permute-done | bytes 40992 | tf_op jit(solution)/shard_map/ppermute | solution.py:709
  32.3 0.0 collective-permute-done.3.z_ref
  32.3 0.0 collective-permute-done.1.y_ref
  32.3 0.0 collective-permute-done.2.early_ref
  32.3 2.9 %shard_map.80 = (f32[20,4,8,128]{3,2,1,0:T(8,128)S(1)}, f32[8,256]{1,0:T(8,128)S(1)}, f32[64,128]{1,0:T(8,128)}) custom-call(f32[1]{0:T(128)} %bitcast.7.smag_ref, f32[19,4,8,128]{3,2,1,0:T(8,128)S(1)} %get-tuple-element.26.post_ref, f32[19,4,8,128]{3,2,1,0:T(8,128)S(1)} %get-tuple-element.27.tang_ref, f32[19,4,8,128]{3,2,1,0:T(8,128)S(1)} %get-tuple-element.28.seed_ref, ...), custom_call_target="tpu_custom_call" | custom-call | flops 20000000 | bytes 1048576 | tf_op jit(solution)/shard_map/pallas_call | solution.py:694
  35.2 2.5 %collective-permute-start.5 = (f32[8,256]{1,0:T(8,128)S(1)}, f32[8,256]{1,0:T(8,128)S(1)}, u32[]{:S(2)}, u32[]{:S(2)}) collective-permute-start(f32[8,256]{1,0:T(8,128)S(1)} %get-tuple-element.39), channel_id=1, source_target_pairs={{0,64},{64,128},{128,192},{192,256},{256,320},{320,384},{384,448},... | collective-permute-start | bytes 24584 | tf_op jit(solution)/shard_map/ppermute | solution.py:770
  37.7 6.0 %all-to-all-start = ((f32[64,1,128]{2,1,0:T(1,128)}), f32[64,1,128]{2,1,0:T(1,128)S(1)}, u32[]{:S(2)}, u32[]{:S(2)}) async-start(f32[64,1,128]{2,1,0:T(1,128)} %bitcast.2), calls=%async_computation | async-start | bytes 65536 | tf_op jit(solution)/shard_map/all_to_all | solution.py:771
  43.7 0.0 collective-permute-done.5.x_ref
  43.8 3.8 %collective-permute-start.6 = (f32[14,8,128]{2,1,0:T(8,128)S(1)}, f32[14,8,128]{2,1,0:T(8,128)S(1)}, u32[]{:S(2)}, u32[]{:S(2)}) collective-permute-start(f32[14,8,128]{2,1,0:T(8,128)S(1)} %shard_map.81), channel_id=1, source_target_pairs={{0,16},{16,32},{32,48},{48,0},{1,17},{17,33},{33,49},{49,1},{2,18}... | collective-permute-start | bytes 172040 | tf_op jit(solution)/shard_map/ppermute | solution.py:774
  47.6 3.6 %collective-permute-done.6.y_ref = f32[14,8,128]{2,1,0:T(8,128)S(1)} collective-permute-done((f32[14,8,128]{2,1,0:T(8,128)S(1)}, f32[14,8,128]{2,1,0:T(8,128)S(1)}, u32[]{:S(2)}, u32[]{:S(2)}) %collective-permute-start.6) | collective-permute-done | bytes 57376 | tf_op jit(solution)/shard_map/ppermute | solution.py:774
  51.2 3.2 %all-to-all-done = f32[64,1,128]{2,1,0:T(1,128)S(1)} async-done(((f32[64,1,128]{2,1,0:T(1,128)}), f32[64,1,128]{2,1,0:T(1,128)S(1)}, u32[]{:S(2)}, u32[]{:S(2)}) %all-to-all-start) | async-done | bytes 32800 | tf_op jit(solution)/shard_map/all_to_all | solution.py:771
  54.4 2.2 %collective-permute-start.7 = (f32[32,8,128]{2,1,0:T(8,128)S(1)}, f32[32,8,128]{2,1,0:T(8,128)S(1)}, u32[]{:S(2)}, u32[]{:S(2)}) collective-permute-start(f32[32,8,128]{2,1,0:T(8,128)S(1)} %shard_map.82), channel_id=1, source_target_pairs={{0,1},{1,2},{2,3},{3,4},{4,5},{5,6},{6,7},{7,8},{8,9},{9,10},{10,1... | collective-permute-start | bytes 393224 | tf_op jit(solution)/shard_map/ppermute | solution.py:781
  56.6 0.6 broadcast_in_dim.2
  57.2 5.0 %all-to-all-start.1 = ((f32[8,1,128]{2,1,0:T(1,128)}), f32[8,1,128]{2,1,0:T(1,128)S(1)}, u32[]{:S(2)}, u32[]{:S(2)}) async-start(f32[8,1,128]{2,1,0:T(1,128)} %broadcast_in_dim.2), calls=%async_computation.1 | async-start | bytes 8192 | tf_op jit(solution)/shard_map/all_to_all | solution.py:783
  62.2 0.0 collective-permute-done.7.z_ref
  62.2 1.6 %shard_map.83 = (f32[19,4,8,128]{3,2,1,0:T(8,128)}, f32[4,8,128]{2,1,0:T(8,128)}) custom-call(f32[1]{0:T(128)} %bitcast.8.smag_ref, f32[19,4,8,128]{3,2,1,0:T(8,128)S(1)} %get-tuple-element.25.state_ref, f32[4,8,128]{2,1,0:T(8,128)S(1)} %copy-done, f32[20,4,8,128]{3,2,1,0:T(8,128)S(1)} %get-tuple-element.38.back_ref, ...), custom_call_target="tpu_custom_call" | custom-call | flops 20000000 | bytes 1048576 | tf_op jit(solution)/shard_map/pallas_call | solution.py:694
  63.8 2.8 %all-to-all-done.1 = f32[8,1,128]{2,1,0:T(1,128)S(1)} async-done(((f32[8,1,128]{2,1,0:T(1,128)}), f32[8,1,128]{2,1,0:T(1,128)S(1)}, u32[]{:S(2)}, u32[]{:S(2)}) %all-to-all-start.1) | async-done | bytes 4128 | tf_op jit(solution)/shard_map/all_to_all | solution.py:783
  66.6 0.5 slice_reduce_fusion
  (3 shorter events, 0.1 us)
Async XLA Ops:
  0.6 1.4 %copy-start = (f32[4,8,128]{2,1,0:T(8,128)S(1)}, f32[4,8,128]{2,1,0:T(8,128)}, u32[]{:S(2)}) copy-start(f32[4,8,128]{2,1,0:T(8,128)} %eddy_ref.9) | copy-start | bytes 49156
  0.6 10.9 %copy-start.1 = (s32[32,1024]{1,0:T(8,128)S(1)}, s32[32,1024]{1,0:T(8,128)}, u32[]{:S(2)}) copy-start(s32[32,1024]{1,0:T(8,128)} %heights_ref.1) | copy-start | bytes 393220
  2.1 30.2 %collective-permute-start.2 = (f32[43,8,128]{2,1,0:T(8,128)S(1)}, f32[43,8,128]{2,1,0:T(8,128)S(1)}, u32[]{:S(2)}, u32[]{:S(2)}) collective-permute-start(f32[43,8,128]{2,1,0:T(8,128)S(1)} %get-tuple-element.33), channel_id=1, source_target_pairs={{1,0},{2,1},{3,2},{4,3},{5,4},{6,5},{7,6},{8,7},{9,8},{10,9},{11,1... | collective-permute-start | bytes 528392 | tf_op jit(solution)/shard_map/ppermute | solution.py:741
  9.8 3.4 %collective-permute-start = (f32[8,384]{1,0:T(8,128)S(1)}, f32[8,384]{1,0:T(8,128)S(1)}, u32[]{:S(2)}, u32[]{:S(2)}) collective-permute-start(f32[8,384]{1,0:T(8,128)S(1)} %shard_map.78), channel_id=1, source_target_pairs={{64,0},{128,64},{192,128},{256,192},{320,256},{384,320},{448,384},... | collective-permute-start | bytes 36872 | tf_op jit(solution)/shard_map/ppermute | solution.py:740
  13.3 18.9 %collective-permute-start.1 = (f32[28,8,128]{2,1,0:T(8,128)S(1)}, f32[28,8,128]{2,1,0:T(8,128)S(1)}, u32[]{:S(2)}, u32[]{:S(2)}) collective-permute-start(f32[28,8,128]{2,1,0:T(8,128)S(1)} %get-tuple-element.32), channel_id=1, source_target_pairs={{16,0},{32,16},{48,32},{0,48},{17,1},{33,17},{49,33},{1,49},{18,2}... | collective-permute-start | bytes 344072 | tf_op jit(solution)/shard_map/ppermute | solution.py:708
  23.1 9.2 %collective-permute-start.3 = (f32[14,8,128]{2,1,0:T(8,128)S(1)}, f32[14,8,128]{2,1,0:T(8,128)S(1)}, u32[]{:S(2)}, u32[]{:S(2)}) collective-permute-start(f32[14,8,128]{2,1,0:T(8,128)S(1)} %get-tuple-element.34), channel_id=1, source_target_pairs={{1,0},{2,1},{3,2},{4,3},{5,4},{6,5},{7,6},{8,7},{9,8},{10,9},{11,1... | collective-permute-start | bytes 172040 | tf_op jit(solution)/shard_map/ppermute | solution.py:707
  25.3 7.0 %collective-permute-start.4 = (f32[10,8,128]{2,1,0:T(8,128)S(1)}, f32[10,8,128]{2,1,0:T(8,128)S(1)}, u32[]{:S(2)}, u32[]{:S(2)}) collective-permute-start(f32[10,8,128]{2,1,0:T(8,128)S(1)} %get-tuple-element.35), channel_id=1, source_target_pairs={{17,0},{18,1},{19,2},{20,3},{21,4},{22,5},{23,6},{24,7},{25,8},{26... | collective-permute-start | bytes 122888 | tf_op jit(solution)/shard_map/ppermute | solution.py:709
  35.2 8.5 %collective-permute-start.5 = (f32[8,256]{1,0:T(8,128)S(1)}, f32[8,256]{1,0:T(8,128)S(1)}, u32[]{:S(2)}, u32[]{:S(2)}) collective-permute-start(f32[8,256]{1,0:T(8,128)S(1)} %get-tuple-element.39), channel_id=1, source_target_pairs={{0,64},{64,128},{128,192},{192,256},{256,320},{320,384},{384,448},... | collective-permute-start | bytes 24584 | tf_op jit(solution)/shard_map/ppermute | solution.py:770
  37.7 16.7 %all-to-all-start = ((f32[64,1,128]{2,1,0:T(1,128)}), f32[64,1,128]{2,1,0:T(1,128)S(1)}, u32[]{:S(2)}, u32[]{:S(2)}) async-start(f32[64,1,128]{2,1,0:T(1,128)} %bitcast.2), calls=%async_computation | async-start | bytes 65536 | tf_op jit(solution)/shard_map/all_to_all | solution.py:771
  43.8 7.4 %collective-permute-start.6 = (f32[14,8,128]{2,1,0:T(8,128)S(1)}, f32[14,8,128]{2,1,0:T(8,128)S(1)}, u32[]{:S(2)}, u32[]{:S(2)}) collective-permute-start(f32[14,8,128]{2,1,0:T(8,128)S(1)} %shard_map.81), channel_id=1, source_target_pairs={{0,16},{16,32},{32,48},{48,0},{1,17},{17,33},{33,49},{49,1},{2,18}... | collective-permute-start | bytes 172040 | tf_op jit(solution)/shard_map/ppermute | solution.py:774
  54.4 7.8 %collective-permute-start.7 = (f32[32,8,128]{2,1,0:T(8,128)S(1)}, f32[32,8,128]{2,1,0:T(8,128)S(1)}, u32[]{:S(2)}, u32[]{:S(2)}) collective-permute-start(f32[32,8,128]{2,1,0:T(8,128)S(1)} %shard_map.82), channel_id=1, source_target_pairs={{0,1},{1,2},{2,3},{3,4},{4,5},{5,6},{6,7},{7,8},{8,9},{9,10},{10,1... | collective-permute-start | bytes 393224 | tf_op jit(solution)/shard_map/ppermute | solution.py:781
  57.2 9.4 %all-to-all-start.1 = ((f32[8,1,128]{2,1,0:T(1,128)}), f32[8,1,128]{2,1,0:T(1,128)S(1)}, u32[]{:S(2)}, u32[]{:S(2)}) async-start(f32[8,1,128]{2,1,0:T(1,128)} %broadcast_in_dim.2), calls=%async_computation.1 | async-start | bytes 8192 | tf_op jit(solution)/shard_map/all_to_all | solution.py:783

commit v6 on v5

--- a/solution.py
+++ b/solution.py
@@ -667,7 +667,7 @@
         grad_ref[z] = -3.0 * omega * omega * (grad + view(("d", 0), 0, 0, 0))
         return carry
 
-    lax.fori_loop(0, DEPTH, step, 0)
+    lax.fori_loop(0, DEPTH, step, 0, unroll=2)
 
 
 def plus_one(axis):

time: 67.6 us -> 67.6 us (level)
  no operation moved by 1% of the time
where the time goes in v6:
time: 67.6 us; the launch traced here: 67.2 us
  starting transfers between devices  43.6 us (64%)
  waiting for transfers between devices  15 us (22%)
  Pallas kernels  6.09 us (9%)
  between operations  1.42 us (2%)
    ppermute x1, starting transfers between devices, exchange_faces(): spanwise = lax.ppermute(spanwise, 'gy', step('gy'))  9.76 us
    ppermute x1, starting transfers between devices, on_device(): early = lax.ppermute(early, 'gz', minus_one('gz'))  7.72 us
    pallas_call x8, Pallas kernels, call(): pl.pallas_call(kernel, out_shape=[jax.ShapeDtypeStruct(*out) for out in o...  6.09 us
    all_to_all x1, starting transfers between devices, on_device(): lax.all_to_all(sums, ('gy', 'gz'), split_axis=0, concat_axis=0, tiled=True)  6 us
    all_to_all x1, starting transfers between devices, on_device(): sums = lax.all_to_all(sums, 'gx', split_axis=0, concat_axis=0, tiled=True)  5 us
    ppermute x1, starting transfers between devices, on_device(): spanwise = lax.ppermute(spanwise, 'gy', plus_one('gy'))  3.83 us
    ppermute x1, waiting for transfers between devices, exchange_faces(): lax.ppermute(corner, ('gy', 'gz'), pair_pairs(step('gy'), step('gz')))  3.71 us
    ppermute x1, waiting for transfers between devices, on_device(): spanwise = lax.ppermute(spanwise, 'gy', plus_one('gy'))  3.59 us
  transfers between devices with their start and end apart: 10, of which 5 were waited for; matrix products, arithmetic and copies ran while one was open for 1% of the time, Pallas kernels for 3%

profile of v6, /device:TPU:1, one launch (start us, length us, event | category | flops | bytes accessed | tf_op | source)
XLA Modules:
  0.0 67.2 jit_solution(13054833890523988163)
XLA Ops:
  0.6 0.0 copy-start
  0.6 0.0 copy-start.1
  0.7 1.3 %shard_map.76 = (f32[19,4,8,128]{3,2,1,0:T(8,128)S(1)}, f32[19,4,8,128]{3,2,1,0:T(8,128)S(1)}, f32[8,384]{1,0:T(8,128)S(1)}, f32[43,8,128]{2,1,0:T(8,128)S(1)}) custom-call(f32[19,4,8,128]{3,2,1,0:T(8,128)} %state_ref.1, f32[19,4,8,128]{3,2,1,0:T(8,128)} %seed_ref.1), custom_call_target="tpu_custom_call" | custom-call | bytes 1048576 | tf_op jit(solution)/shard_map/pallas_call | solution.py:694
  2.0 0.0 copy-done
  2.0 0.1 shard_map.78
  2.1 7.7 %collective-permute-start.2 = (f32[43,8,128]{2,1,0:T(8,128)S(1)}, f32[43,8,128]{2,1,0:T(8,128)S(1)}, u32[]{:S(2)}, u32[]{:S(2)}) collective-permute-start(f32[43,8,128]{2,1,0:T(8,128)S(1)} %get-tuple-element.33), channel_id=1, source_target_pairs={{1,0},{2,1},{3,2},{4,3},{5,4},{6,5},{7,6},{8,7},{9,8},{10,9},{11,1... | collective-permute-start | bytes 528392 | tf_op jit(solution)/shard_map/ppermute | solution.py:741
  9.8 1.1 %collective-permute-start = (f32[8,384]{1,0:T(8,128)S(1)}, f32[8,384]{1,0:T(8,128)S(1)}, u32[]{:S(2)}, u32[]{:S(2)}) collective-permute-start(f32[8,384]{1,0:T(8,128)S(1)} %shard_map.78), channel_id=1, source_target_pairs={{64,0},{128,64},{192,128},{256,192},{320,256},{384,320},{448,384},... | collective-permute-start | bytes 36872 | tf_op jit(solution)/shard_map/ppermute | solution.py:740
  11.5 0.0 copy-done.1
  11.6 0.2 shard_map.77
  11.8 1.5 %collective-permute-done.x_ref = f32[8,384]{1,0:T(8,128)S(1)} collective-permute-done((f32[8,384]{1,0:T(8,128)S(1)}, f32[8,384]{1,0:T(8,128)S(1)}, u32[]{:S(2)}, u32[]{:S(2)}) %collective-permute-start) | collective-permute-done | bytes 12320 | tf_op jit(solution)/shard_map/ppermute | solution.py:740
  13.3 0.1 shard_map.79
  13.3 9.8 %collective-permute-start.1 = (f32[28,8,128]{2,1,0:T(8,128)S(1)}, f32[28,8,128]{2,1,0:T(8,128)S(1)}, u32[]{:S(2)}, u32[]{:S(2)}) collective-permute-start(f32[28,8,128]{2,1,0:T(8,128)S(1)} %get-tuple-element.32), channel_id=1, source_target_pairs={{16,0},{32,16},{48,32},{0,48},{17,1},{33,17},{49,33},{1,49},{18,2}... | collective-permute-start | bytes 344072 | tf_op jit(solution)/shard_map/ppermute | solution.py:708
  23.1 2.2 %collective-permute-start.3 = (f32[14,8,128]{2,1,0:T(8,128)S(1)}, f32[14,8,128]{2,1,0:T(8,128)S(1)}, u32[]{:S(2)}, u32[]{:S(2)}) collective-permute-start(f32[14,8,128]{2,1,0:T(8,128)S(1)} %get-tuple-element.34), channel_id=1, source_target_pairs={{1,0},{2,1},{3,2},{4,3},{5,4},{6,5},{7,6},{8,7},{9,8},{10,9},{11,1... | collective-permute-start | bytes 172040 | tf_op jit(solution)/shard_map/ppermute | solution.py:707
  25.3 3.3 %collective-permute-start.4 = (f32[10,8,128]{2,1,0:T(8,128)S(1)}, f32[10,8,128]{2,1,0:T(8,128)S(1)}, u32[]{:S(2)}, u32[]{:S(2)}) collective-permute-start(f32[10,8,128]{2,1,0:T(8,128)S(1)} %get-tuple-element.35), channel_id=1, source_target_pairs={{17,0},{18,1},{19,2},{20,3},{21,4},{22,5},{23,6},{24,7},{25,8},{26... | collective-permute-start | bytes 122888 | tf_op jit(solution)/shard_map/ppermute | solution.py:709
  28.6 3.7 %collective-permute-done.4.yz_ref = f32[10,8,128]{2,1,0:T(8,128)S(1)} collective-permute-done((f32[10,8,128]{2,1,0:T(8,128)S(1)}, f32[10,8,128]{2,1,0:T(8,128)S(1)}, u32[]{:S(2)}, u32[]{:S(2)}) %collective-permute-start.4) | collective-permute-done | bytes 40992 | tf_op jit(solution)/shard_map/ppermute | solution.py:709
  32.3 0.0 collective-permute-done.3.z_ref
  32.3 0.0 collective-permute-done.1.y_ref
  32.3 0.0 collective-permute-done.2.early_ref
  32.3 2.9 %shard_map.80 = (f32[20,4,8,128]{3,2,1,0:T(8,128)S(1)}, f32[8,256]{1,0:T(8,128)S(1)}, f32[64,128]{1,0:T(8,128)}) custom-call(f32[1]{0:T(128)} %bitcast.7.smag_ref, f32[19,4,8,128]{3,2,1,0:T(8,128)S(1)} %get-tuple-element.26.post_ref, f32[19,4,8,128]{3,2,1,0:T(8,128)S(1)} %get-tuple-element.27.tang_ref, f32[19,4,8,128]{3,2,1,0:T(8,128)S(1)} %get-tuple-element.28.seed_ref, ...), custom_call_target="tpu_custom_call" | custom-call | flops 20000000 | bytes 1048576 | tf_op jit(solution)/shard_map/pallas_call | solution.py:694
  35.2 2.5 %collective-permute-start.5 = (f32[8,256]{1,0:T(8,128)S(1)}, f32[8,256]{1,0:T(8,128)S(1)}, u32[]{:S(2)}, u32[]{:S(2)}) collective-permute-start(f32[8,256]{1,0:T(8,128)S(1)} %get-tuple-element.39), channel_id=1, source_target_pairs={{0,64},{64,128},{128,192},{192,256},{256,320},{320,384},{384,448},... | collective-permute-start | bytes 24584 | tf_op jit(solution)/shard_map/ppermute | solution.py:770
  37.7 6.0 %all-to-all-start = ((f32[64,1,128]{2,1,0:T(1,128)}), f32[64,1,128]{2,1,0:T(1,128)S(1)}, u32[]{:S(2)}, u32[]{:S(2)}) async-start(f32[64,1,128]{2,1,0:T(1,128)} %bitcast.2), calls=%async_computation | async-start | bytes 65536 | tf_op jit(solution)/shard_map/all_to_all | solution.py:771
  43.7 0.0 collective-permute-done.5.x_ref
  43.8 3.8 %collective-permute-start.6 = (f32[14,8,128]{2,1,0:T(8,128)S(1)}, f32[14,8,128]{2,1,0:T(8,128)S(1)}, u32[]{:S(2)}, u32[]{:S(2)}) collective-permute-start(f32[14,8,128]{2,1,0:T(8,128)S(1)} %shard_map.81), channel_id=1, source_target_pairs={{0,16},{16,32},{32,48},{48,0},{1,17},{17,33},{33,49},{49,1},{2,18}... | collective-permute-start | bytes 172040 | tf_op jit(solution)/shard_map/ppermute | solution.py:774
  47.6 3.6 %collective-permute-done.6.y_ref = f32[14,8,128]{2,1,0:T(8,128)S(1)} collective-permute-done((f32[14,8,128]{2,1,0:T(8,128)S(1)}, f32[14,8,128]{2,1,0:T(8,128)S(1)}, u32[]{:S(2)}, u32[]{:S(2)}) %collective-permute-start.6) | collective-permute-done | bytes 57376 | tf_op jit(solution)/shard_map/ppermute | solution.py:774
  51.2 3.2 %all-to-all-done = f32[64,1,128]{2,1,0:T(1,128)S(1)} async-done(((f32[64,1,128]{2,1,0:T(1,128)}), f32[64,1,128]{2,1,0:T(1,128)S(1)}, u32[]{:S(2)}, u32[]{:S(2)}) %all-to-all-start) | async-done | bytes 32800 | tf_op jit(solution)/shard_map/all_to_all | solution.py:771
  54.4 2.2 %collective-permute-start.7 = (f32[32,8,128]{2,1,0:T(8,128)S(1)}, f32[32,8,128]{2,1,0:T(8,128)S(1)}, u32[]{:S(2)}, u32[]{:S(2)}) collective-permute-start(f32[32,8,128]{2,1,0:T(8,128)S(1)} %shard_map.82), channel_id=1, source_target_pairs={{0,1},{1,2},{2,3},{3,4},{4,5},{5,6},{6,7},{7,8},{8,9},{9,10},{10,1... | collective-permute-start | bytes 393224 | tf_op jit(solution)/shard_map/ppermute | solution.py:781
  56.6 0.6 broadcast_in_dim.2
  57.2 5.0 %all-to-all-start.1 = ((f32[8,1,128]{2,1,0:T(1,128)}), f32[8,1,128]{2,1,0:T(1,128)S(1)}, u32[]{:S(2)}, u32[]{:S(2)}) async-start(f32[8,1,128]{2,1,0:T(1,128)} %broadcast_in_dim.2), calls=%async_computation.1 | async-start | bytes 8192 | tf_op jit(solution)/shard_map/all_to_all | solution.py:783
  62.2 0.0 collective-permute-done.7.z_ref
  62.2 1.5 %shard_map.83 = (f32[19,4,8,128]{3,2,1,0:T(8,128)}, f32[4,8,128]{2,1,0:T(8,128)}) custom-call(f32[1]{0:T(128)} %bitcast.8.smag_ref, f32[19,4,8,128]{3,2,1,0:T(8,128)S(1)} %get-tuple-element.25.state_ref, f32[4,8,128]{2,1,0:T(8,128)S(1)} %copy-done, f32[20,4,8,128]{3,2,1,0:T(8,128)S(1)} %get-tuple-element.38.back_ref, ...), custom_call_target="tpu_custom_call" | custom-call | flops 20000000 | bytes 1048576 | tf_op jit(solution)/shard_map/pallas_call | solution.py:694
  63.7 3.0 %all-to-all-done.1 = f32[8,1,128]{2,1,0:T(1,128)S(1)} async-done(((f32[8,1,128]{2,1,0:T(1,128)}), f32[8,1,128]{2,1,0:T(1,128)S(1)}, u32[]{:S(2)}, u32[]{:S(2)}) %all-to-all-start.1) | async-done | bytes 4128 | tf_op jit(solution)/shard_map/all_to_all | solution.py:783
  66.6 0.5 slice_reduce_fusion
  (3 shorter events, 0.1 us)
Async XLA Ops:
  0.6 1.4 %copy-start = (f32[4,8,128]{2,1,0:T(8,128)S(1)}, f32[4,8,128]{2,1,0:T(8,128)}, u32[]{:S(2)}) copy-start(f32[4,8,128]{2,1,0:T(8,128)} %eddy_ref.9) | copy-start | bytes 49156
  0.6 10.9 %copy-start.1 = (s32[32,1024]{1,0:T(8,128)S(1)}, s32[32,1024]{1,0:T(8,128)}, u32[]{:S(2)}) copy-start(s32[32,1024]{1,0:T(8,128)} %heights_ref.1) | copy-start | bytes 393220
  2.1 30.2 %collective-permute-start.2 = (f32[43,8,128]{2,1,0:T(8,128)S(1)}, f32[43,8,128]{2,1,0:T(8,128)S(1)}, u32[]{:S(2)}, u32[]{:S(2)}) collective-permute-start(f32[43,8,128]{2,1,0:T(8,128)S(1)} %get-tuple-element.33), channel_id=1, source_target_pairs={{1,0},{2,1},{3,2},{4,3},{5,4},{6,5},{7,6},{8,7},{9,8},{10,9},{11,1... | collective-permute-start | bytes 528392 | tf_op jit(solution)/shard_map/ppermute | solution.py:741
  9.8 3.4 %collective-permute-start = (f32[8,384]{1,0:T(8,128)S(1)}, f32[8,384]{1,0:T(8,128)S(1)}, u32[]{:S(2)}, u32[]{:S(2)}) collective-permute-start(f32[8,384]{1,0:T(8,128)S(1)} %shard_map.78), channel_id=1, source_target_pairs={{64,0},{128,64},{192,128},{256,192},{320,256},{384,320},{448,384},... | collective-permute-start | bytes 36872 | tf_op jit(solution)/shard_map/ppermute | solution.py:740
  13.3 18.9 %collective-permute-start.1 = (f32[28,8,128]{2,1,0:T(8,128)S(1)}, f32[28,8,128]{2,1,0:T(8,128)S(1)}, u32[]{:S(2)}, u32[]{:S(2)}) collective-permute-start(f32[28,8,128]{2,1,0:T(8,128)S(1)} %get-tuple-element.32), channel_id=1, source_target_pairs={{16,0},{32,16},{48,32},{0,48},{17,1},{33,17},{49,33},{1,49},{18,2}... | collective-permute-start | bytes 344072 | tf_op jit(solution)/shard_map/ppermute | solution.py:708
  23.1 9.2 %collective-permute-start.3 = (f32[14,8,128]{2,1,0:T(8,128)S(1)}, f32[14,8,128]{2,1,0:T(8,128)S(1)}, u32[]{:S(2)}, u32[]{:S(2)}) collective-permute-start(f32[14,8,128]{2,1,0:T(8,128)S(1)} %get-tuple-element.34), channel_id=1, source_target_pairs={{1,0},{2,1},{3,2},{4,3},{5,4},{6,5},{7,6},{8,7},{9,8},{10,9},{11,1... | collective-permute-start | bytes 172040 | tf_op jit(solution)/shard_map/ppermute | solution.py:707
  25.3 7.0 %collective-permute-start.4 = (f32[10,8,128]{2,1,0:T(8,128)S(1)}, f32[10,8,128]{2,1,0:T(8,128)S(1)}, u32[]{:S(2)}, u32[]{:S(2)}) collective-permute-start(f32[10,8,128]{2,1,0:T(8,128)S(1)} %get-tuple-element.35), channel_id=1, source_target_pairs={{17,0},{18,1},{19,2},{20,3},{21,4},{22,5},{23,6},{24,7},{25,8},{26... | collective-permute-start | bytes 122888 | tf_op jit(solution)/shard_map/ppermute | solution.py:709
  35.2 8.5 %collective-permute-start.5 = (f32[8,256]{1,0:T(8,128)S(1)}, f32[8,256]{1,0:T(8,128)S(1)}, u32[]{:S(2)}, u32[]{:S(2)}) collective-permute-start(f32[8,256]{1,0:T(8,128)S(1)} %get-tuple-element.39), channel_id=1, source_target_pairs={{0,64},{64,128},{128,192},{192,256},{256,320},{320,384},{384,448},... | collective-permute-start | bytes 24584 | tf_op jit(solution)/shard_map/ppermute | solution.py:770
  37.7 16.7 %all-to-all-start = ((f32[64,1,128]{2,1,0:T(1,128)}), f32[64,1,128]{2,1,0:T(1,128)S(1)}, u32[]{:S(2)}, u32[]{:S(2)}) async-start(f32[64,1,128]{2,1,0:T(1,128)} %bitcast.2), calls=%async_computation | async-start | bytes 65536 | tf_op jit(solution)/shard_map/all_to_all | solution.py:771
  43.8 7.4 %collective-permute-start.6 = (f32[14,8,128]{2,1,0:T(8,128)S(1)}, f32[14,8,128]{2,1,0:T(8,128)S(1)}, u32[]{:S(2)}, u32[]{:S(2)}) collective-permute-start(f32[14,8,128]{2,1,0:T(8,128)S(1)} %shard_map.81), channel_id=1, source_target_pairs={{0,16},{16,32},{32,48},{48,0},{1,17},{17,33},{33,49},{49,1},{2,18}... | collective-permute-start | bytes 172040 | tf_op jit(solution)/shard_map/ppermute | solution.py:774
  54.4 7.8 %collective-permute-start.7 = (f32[32,8,128]{2,1,0:T(8,128)S(1)}, f32[32,8,128]{2,1,0:T(8,128)S(1)}, u32[]{:S(2)}, u32[]{:S(2)}) collective-permute-start(f32[32,8,128]{2,1,0:T(8,128)S(1)} %shard_map.82), channel_id=1, source_target_pairs={{0,1},{1,2},{2,3},{3,4},{4,5},{5,6},{6,7},{7,8},{8,9},{9,10},{10,1... | collective-permute-start | bytes 393224 | tf_op jit(solution)/shard_map/ppermute | solution.py:781
  57.2 9.4 %all-to-all-start.1 = ((f32[8,1,128]{2,1,0:T(1,128)}), f32[8,1,128]{2,1,0:T(1,128)S(1)}, u32[]{:S(2)}, u32[]{:S(2)}) async-start(f32[8,1,128]{2,1,0:T(1,128)} %broadcast_in_dim.2), calls=%async_computation.1 | async-start | bytes 8192 | tf_op jit(solution)/shard_map/all_to_all | solution.py:783

commit v7 on v5

--- a/solution.py
+++ b/solution.py
@@ -736,7 +736,6 @@
         limit=(52 << 20) + (960 << 10),
     )
     (columns,) = call(eddy_columns_kernel, [columns.shape], (columns, eddy))
-    columns, early = lax.optimization_barrier((columns, early))
     columns = lax.ppermute(columns, "gx", minus_one("gx"))
     early = lax.ppermute(early, "gz", minus_one("gz"))
     beside = ((2, len(SIDES), ROWS, COLS), jnp.int32)

time: 67.6 us -> 67.6 us (level)
  no operation moved by 1% of the time
where the time goes in v7:
time: 67.6 us; the launch traced here: 67.2 us
  starting transfers between devices  43.6 us (64%)
  waiting for transfers between devices  14.8 us (22%)
  Pallas kernels  6.25 us (9%)
  between operations  1.42 us (2%)
    ppermute x1, starting transfers between devices, exchange_faces(): spanwise = lax.ppermute(spanwise, 'gy', step('gy'))  9.76 us
    ppermute x1, starting transfers between devices, on_device(): early = lax.ppermute(early, 'gz', minus_one('gz'))  7.74 us
    pallas_call x8, Pallas kernels, call(): pl.pallas_call(kernel, out_shape=[jax.ShapeDtypeStruct(*out) for out in o...  6.25 us
    all_to_all x1, starting transfers between devices, on_device(): lax.all_to_all(sums, ('gy', 'gz'), split_axis=0, concat_axis=0, tiled=True)  6 us
    all_to_all x1, starting transfers between devices, on_device(): sums = lax.all_to_all(sums, 'gx', split_axis=0, concat_axis=0, tiled=True)  5 us
    ppermute x1, starting transfers between devices, on_device(): spanwise = lax.ppermute(spanwise, 'gy', plus_one('gy'))  3.83 us
    ppermute x1, waiting for transfers between devices, exchange_faces(): lax.ppermute(corner, ('gy', 'gz'), pair_pairs(step('gy'), step('gz')))  3.7 us
    ppermute x1, waiting for transfers between devices, on_device(): spanwise = lax.ppermute(spanwise, 'gy', plus_one('gy'))  3.59 us
  transfers between devices with their start and end apart: 10, of which 5 were waited for; matrix products, arithmetic and copies ran while one was open for 1% of the time, Pallas kernels for 3%

profile of v7, /device:TPU:1, one launch (start us, length us, event | category | flops | bytes accessed | tf_op | source)
XLA Modules:
  0.0 67.2 jit_solution(5082309669852462474)
XLA Ops:
  0.6 0.0 copy-start
  0.6 0.0 copy-start.1
  0.7 1.3 %shard_map.76 = (f32[19,4,8,128]{3,2,1,0:T(8,128)S(1)}, f32[19,4,8,128]{3,2,1,0:T(8,128)S(1)}, f32[8,384]{1,0:T(8,128)S(1)}, f32[43,8,128]{2,1,0:T(8,128)S(1)}) custom-call(f32[19,4,8,128]{3,2,1,0:T(8,128)} %state_ref.1, f32[19,4,8,128]{3,2,1,0:T(8,128)} %seed_ref.1), custom_call_target="tpu_custom_call" | custom-call | bytes 1048576 | tf_op jit(solution)/shard_map/pallas_call | solution.py:694
  2.0 7.7 %collective-permute-start.2 = (f32[43,8,128]{2,1,0:T(8,128)S(1)}, f32[43,8,128]{2,1,0:T(8,128)S(1)}, u32[]{:S(2)}, u32[]{:S(2)}) collective-permute-start(f32[43,8,128]{2,1,0:T(8,128)S(1)} %get-tuple-element.29), channel_id=1, source_target_pairs={{1,0},{2,1},{3,2},{4,3},{5,4},{6,5},{7,6},{8,7},{9,8},{10,9},{11,1... | collective-permute-start | bytes 528392 | tf_op jit(solution)/shard_map/ppermute | solution.py:740
  9.7 0.0 copy-done
  9.8 0.1 shard_map.78
  9.8 1.1 %collective-permute-start = (f32[8,384]{1,0:T(8,128)S(1)}, f32[8,384]{1,0:T(8,128)S(1)}, u32[]{:S(2)}, u32[]{:S(2)}) collective-permute-start(f32[8,384]{1,0:T(8,128)S(1)} %shard_map.78), channel_id=1, source_target_pairs={{64,0},{128,64},{192,128},{256,192},{320,256},{384,320},{448,384},... | collective-permute-start | bytes 36872 | tf_op jit(solution)/shard_map/ppermute | solution.py:739
  11.5 0.0 copy-done.1
  11.6 0.2 shard_map.77
  11.8 1.5 %collective-permute-done.x_ref = f32[8,384]{1,0:T(8,128)S(1)} collective-permute-done((f32[8,384]{1,0:T(8,128)S(1)}, f32[8,384]{1,0:T(8,128)S(1)}, u32[]{:S(2)}, u32[]{:S(2)}) %collective-permute-start) | collective-permute-done | bytes 12320 | tf_op jit(solution)/shard_map/ppermute | solution.py:739
  13.3 0.1 shard_map.79
  13.3 9.8 %collective-permute-start.1 = (f32[28,8,128]{2,1,0:T(8,128)S(1)}, f32[28,8,128]{2,1,0:T(8,128)S(1)}, u32[]{:S(2)}, u32[]{:S(2)}) collective-permute-start(f32[28,8,128]{2,1,0:T(8,128)S(1)} %get-tuple-element.28), channel_id=1, source_target_pairs={{16,0},{32,16},{48,32},{0,48},{17,1},{33,17},{49,33},{1,49},{18,2}... | collective-permute-start | bytes 344072 | tf_op jit(solution)/shard_map/ppermute | solution.py:708
  23.1 2.2 %collective-permute-start.3 = (f32[14,8,128]{2,1,0:T(8,128)S(1)}, f32[14,8,128]{2,1,0:T(8,128)S(1)}, u32[]{:S(2)}, u32[]{:S(2)}) collective-permute-start(f32[14,8,128]{2,1,0:T(8,128)S(1)} %get-tuple-element.30), channel_id=1, source_target_pairs={{1,0},{2,1},{3,2},{4,3},{5,4},{6,5},{7,6},{8,7},{9,8},{10,9},{11,1... | collective-permute-start | bytes 172040 | tf_op jit(solution)/shard_map/ppermute | solution.py:707
  25.3 3.3 %collective-permute-start.4 = (f32[10,8,128]{2,1,0:T(8,128)S(1)}, f32[10,8,128]{2,1,0:T(8,128)S(1)}, u32[]{:S(2)}, u32[]{:S(2)}) collective-permute-start(f32[10,8,128]{2,1,0:T(8,128)S(1)} %get-tuple-element.31), channel_id=1, source_target_pairs={{17,0},{18,1},{19,2},{20,3},{21,4},{22,5},{23,6},{24,7},{25,8},{26... | collective-permute-start | bytes 122888 | tf_op jit(solution)/shard_map/ppermute | solution.py:709
  28.6 3.7 %collective-permute-done.4.yz_ref = f32[10,8,128]{2,1,0:T(8,128)S(1)} collective-permute-done((f32[10,8,128]{2,1,0:T(8,128)S(1)}, f32[10,8,128]{2,1,0:T(8,128)S(1)}, u32[]{:S(2)}, u32[]{:S(2)}) %collective-permute-start.4) | collective-permute-done | bytes 40992 | tf_op jit(solution)/shard_map/ppermute | solution.py:709
  32.3 0.0 collective-permute-done.3.z_ref
  32.3 0.0 collective-permute-done.1.y_ref
  32.3 0.0 collective-permute-done.2.early_ref
  32.3 2.9 %shard_map.80 = (f32[20,4,8,128]{3,2,1,0:T(8,128)S(1)}, f32[8,256]{1,0:T(8,128)S(1)}, f32[64,128]{1,0:T(8,128)}) custom-call(f32[1]{0:T(128)} %bitcast.7.smag_ref, f32[19,4,8,128]{3,2,1,0:T(8,128)S(1)} %get-tuple-element.24.post_ref, f32[19,4,8,128]{3,2,1,0:T(8,128)S(1)} %get-tuple-element.25.tang_ref, f32[19,4,8,128]{3,2,1,0:T(8,128)S(1)} %get-tuple-element.26.seed_ref, ...), custom_call_target="tpu_custom_call" | custom-call | flops 20000000 | bytes 1048576 | tf_op jit(solution)/shard_map/pallas_call | solution.py:694
  35.2 2.5 %collective-permute-start.5 = (f32[8,256]{1,0:T(8,128)S(1)}, f32[8,256]{1,0:T(8,128)S(1)}, u32[]{:S(2)}, u32[]{:S(2)}) collective-permute-start(f32[8,256]{1,0:T(8,128)S(1)} %get-tuple-element.35), channel_id=1, source_target_pairs={{0,64},{64,128},{128,192},{192,256},{256,320},{320,384},{384,448},... | collective-permute-start | bytes 24584 | tf_op jit(solution)/shard_map/ppermute | solution.py:769
  37.7 6.0 %all-to-all-start = ((f32[64,1,128]{2,1,0:T(1,128)}), f32[64,1,128]{2,1,0:T(1,128)S(1)}, u32[]{:S(2)}, u32[]{:S(2)}) async-start(f32[64,1,128]{2,1,0:T(1,128)} %bitcast.2), calls=%async_computation | async-start | bytes 65536 | tf_op jit(solution)/shard_map/all_to_all | solution.py:770
  43.7 0.0 collective-permute-done.5.x_ref
  43.8 3.8 %collective-permute-start.6 = (f32[14,8,128]{2,1,0:T(8,128)S(1)}, f32[14,8,128]{2,1,0:T(8,128)S(1)}, u32[]{:S(2)}, u32[]{:S(2)}) collective-permute-start(f32[14,8,128]{2,1,0:T(8,128)S(1)} %shard_map.81), channel_id=1, source_target_pairs={{0,16},{16,32},{32,48},{48,0},{1,17},{17,33},{33,49},{49,1},{2,18}... | collective-permute-start | bytes 172040 | tf_op jit(solution)/shard_map/ppermute | solution.py:773
  47.6 3.6 %collective-permute-done.6.y_ref = f32[14,8,128]{2,1,0:T(8,128)S(1)} collective-permute-done((f32[14,8,128]{2,1,0:T(8,128)S(1)}, f32[14,8,128]{2,1,0:T(8,128)S(1)}, u32[]{:S(2)}, u32[]{:S(2)}) %collective-permute-start.6) | collective-permute-done | bytes 57376 | tf_op jit(solution)/shard_map/ppermute | solution.py:773
  51.2 3.2 %all-to-all-done = f32[64,1,128]{2,1,0:T(1,128)S(1)} async-done(((f32[64,1,128]{2,1,0:T(1,128)}), f32[64,1,128]{2,1,0:T(1,128)S(1)}, u32[]{:S(2)}, u32[]{:S(2)}) %all-to-all-start) | async-done | bytes 32800 | tf_op jit(solution)/shard_map/all_to_all | solution.py:770
  54.4 2.2 %collective-permute-start.7 = (f32[32,8,128]{2,1,0:T(8,128)S(1)}, f32[32,8,128]{2,1,0:T(8,128)S(1)}, u32[]{:S(2)}, u32[]{:S(2)}) collective-permute-start(f32[32,8,128]{2,1,0:T(8,128)S(1)} %shard_map.82), channel_id=1, source_target_pairs={{0,1},{1,2},{2,3},{3,4},{4,5},{5,6},{6,7},{7,8},{8,9},{9,10},{10,1... | collective-permute-start | bytes 393224 | tf_op jit(solution)/shard_map/ppermute | solution.py:780
  56.6 0.6 broadcast_in_dim.2
  57.2 5.0 %all-to-all-start.1 = ((f32[8,1,128]{2,1,0:T(1,128)}), f32[8,1,128]{2,1,0:T(1,128)S(1)}, u32[]{:S(2)}, u32[]{:S(2)}) async-start(f32[8,1,128]{2,1,0:T(1,128)} %broadcast_in_dim.2), calls=%async_computation.1 | async-start | bytes 8192 | tf_op jit(solution)/shard_map/all_to_all | solution.py:782
  62.2 0.0 collective-permute-done.7.z_ref
  62.2 1.6 %shard_map.83 = (f32[19,4,8,128]{3,2,1,0:T(8,128)}, f32[4,8,128]{2,1,0:T(8,128)}) custom-call(f32[1]{0:T(128)} %bitcast.8.smag_ref, f32[19,4,8,128]{3,2,1,0:T(8,128)S(1)} %get-tuple-element.23.state_ref, f32[4,8,128]{2,1,0:T(8,128)S(1)} %copy-done, f32[20,4,8,128]{3,2,1,0:T(8,128)S(1)} %get-tuple-element.34.back_ref, ...), custom_call_target="tpu_custom_call" | custom-call | flops 20000000 | bytes 1048576 | tf_op jit(solution)/shard_map/pallas_call | solution.py:694
  63.8 2.8 %all-to-all-done.1 = f32[8,1,128]{2,1,0:T(1,128)S(1)} async-done(((f32[8,1,128]{2,1,0:T(1,128)}), f32[8,1,128]{2,1,0:T(1,128)S(1)}, u32[]{:S(2)}, u32[]{:S(2)}) %all-to-all-start.1) | async-done | bytes 4128 | tf_op jit(solution)/shard_map/all_to_all | solution.py:782
  66.6 0.5 slice_reduce_fusion
  (3 shorter events, 0.1 us)
Async XLA Ops:
  0.6 9.1 %copy-start = (f32[4,8,128]{2,1,0:T(8,128)S(1)}, f32[4,8,128]{2,1,0:T(8,128)}, u32[]{:S(2)}) copy-start(f32[4,8,128]{2,1,0:T(8,128)} %eddy_ref.9) | copy-start | bytes 49156
  0.6 10.9 %copy-start.1 = (s32[32,1024]{1,0:T(8,128)S(1)}, s32[32,1024]{1,0:T(8,128)}, u32[]{:S(2)}) copy-start(s32[32,1024]{1,0:T(8,128)} %heights_ref.1) | copy-start | bytes 393220
  2.0 30.3 %collective-permute-start.2 = (f32[43,8,128]{2,1,0:T(8,128)S(1)}, f32[43,8,128]{2,1,0:T(8,128)S(1)}, u32[]{:S(2)}, u32[]{:S(2)}) collective-permute-start(f32[43,8,128]{2,1,0:T(8,128)S(1)} %get-tuple-element.29), channel_id=1, source_target_pairs={{1,0},{2,1},{3,2},{4,3},{5,4},{6,5},{7,6},{8,7},{9,8},{10,9},{11,1... | collective-permute-start | bytes 528392 | tf_op jit(solution)/shard_map/ppermute | solution.py:740
  9.8 3.4 %collective-permute-start = (f32[8,384]{1,0:T(8,128)S(1)}, f32[8,384]{1,0:T(8,128)S(1)}, u32[]{:S(2)}, u32[]{:S(2)}) collective-permute-start(f32[8,384]{1,0:T(8,128)S(1)} %shard_map.78), channel_id=1, source_target_pairs={{64,0},{128,64},{192,128},{256,192},{320,256},{384,320},{448,384},... | collective-permute-start | bytes 36872 | tf_op jit(solution)/shard_map/ppermute | solution.py:739
  13.3 18.9 %collective-permute-start.1 = (f32[28,8,128]{2,1,0:T(8,128)S(1)}, f32[28,8,128]{2,1,0:T(8,128)S(1)}, u32[]{:S(2)}, u32[]{:S(2)}) collective-permute-start(f32[28,8,128]{2,1,0:T(8,128)S(1)} %get-tuple-element.28), channel_id=1, source_target_pairs={{16,0},{32,16},{48,32},{0,48},{17,1},{33,17},{49,33},{1,49},{18,2}... | collective-permute-start | bytes 344072 | tf_op jit(solution)/shard_map/ppermute | solution.py:708
  23.1 9.2 %collective-permute-start.3 = (f32[14,8,128]{2,1,0:T(8,128)S(1)}, f32[14,8,128]{2,1,0:T(8,128)S(1)}, u32[]{:S(2)}, u32[]{:S(2)}) collective-permute-start(f32[14,8,128]{2,1,0:T(8,128)S(1)} %get-tuple-element.30), channel_id=1, source_target_pairs={{1,0},{2,1},{3,2},{4,3},{5,4},{6,5},{7,6},{8,7},{9,8},{10,9},{11,1... | collective-permute-start | bytes 172040 | tf_op jit(solution)/shard_map/ppermute | solution.py:707
  25.3 7.0 %collective-permute-start.4 = (f32[10,8,128]{2,1,0:T(8,128)S(1)}, f32[10,8,128]{2,1,0:T(8,128)S(1)}, u32[]{:S(2)}, u32[]{:S(2)}) collective-permute-start(f32[10,8,128]{2,1,0:T(8,128)S(1)} %get-tuple-element.31), channel_id=1, source_target_pairs={{17,0},{18,1},{19,2},{20,3},{21,4},{22,5},{23,6},{24,7},{25,8},{26... | collective-permute-start | bytes 122888 | tf_op jit(solution)/shard_map/ppermute | solution.py:709
  35.2 8.5 %collective-permute-start.5 = (f32[8,256]{1,0:T(8,128)S(1)}, f32[8,256]{1,0:T(8,128)S(1)}, u32[]{:S(2)}, u32[]{:S(2)}) collective-permute-start(f32[8,256]{1,0:T(8,128)S(1)} %get-tuple-element.35), channel_id=1, source_target_pairs={{0,64},{64,128},{128,192},{192,256},{256,320},{320,384},{384,448},... | collective-permute-start | bytes 24584 | tf_op jit(solution)/shard_map/ppermute | solution.py:769
  37.7 16.7 %all-to-all-start = ((f32[64,1,128]{2,1,0:T(1,128)}), f32[64,1,128]{2,1,0:T(1,128)S(1)}, u32[]{:S(2)}, u32[]{:S(2)}) async-start(f32[64,1,128]{2,1,0:T(1,128)} %bitcast.2), calls=%async_computation | async-start | bytes 65536 | tf_op jit(solution)/shard_map/all_to_all | solution.py:770
  43.8 7.4 %collective-permute-start.6 = (f32[14,8,128]{2,1,0:T(8,128)S(1)}, f32[14,8,128]{2,1,0:T(8,128)S(1)}, u32[]{:S(2)}, u32[]{:S(2)}) collective-permute-start(f32[14,8,128]{2,1,0:T(8,128)S(1)} %shard_map.81), channel_id=1, source_target_pairs={{0,16},{16,32},{32,48},{48,0},{1,17},{17,33},{33,49},{49,1},{2,18}... | collective-permute-start | bytes 172040 | tf_op jit(solution)/shard_map/ppermute | solution.py:773
  54.4 7.8 %collective-permute-start.7 = (f32[32,8,128]{2,1,0:T(8,128)S(1)}, f32[32,8,128]{2,1,0:T(8,128)S(1)}, u32[]{:S(2)}, u32[]{:S(2)}) collective-permute-start(f32[32,8,128]{2,1,0:T(8,128)S(1)} %shard_map.82), channel_id=1, source_target_pairs={{0,1},{1,2},{2,3},{3,4},{4,5},{5,6},{6,7},{7,8},{8,9},{9,10},{10,1... | collective-permute-start | bytes 393224 | tf_op jit(solution)/shard_map/ppermute | solution.py:780
  57.2 9.4 %all-to-all-start.1 = ((f32[8,1,128]{2,1,0:T(1,128)}), f32[8,1,128]{2,1,0:T(1,128)S(1)}, u32[]{:S(2)}, u32[]{:S(2)}) async-start(f32[8,1,128]{2,1,0:T(1,128)} %broadcast_in_dim.2), calls=%async_computation.1 | async-start | bytes 8192 | tf_op jit(solution)/shard_map/all_to_all | solution.py:782
